TPU v7x, 128 devices: a whole 4x4x4 slice. The times are simulated.
128 devices in a mesh: row: 4 (over x_lo, core), col: 32 (over z, x_hi, y).
Axes of the slice: x: 4 (x_hi: 2, x_lo: 2; x = x_hi * 2 + x_lo), y: 4, z: 4, core: 2. Of those that a mesh axis runs over, the one named last changes fastest.
Arguments:
- images: bfloat16 [16384, 1280], P(('row', 'col')), may hold values from -0.5 to 0.5
- texts: bfloat16 [16384, 1280], P(('col', 'row')), may hold values from -0.5 to 0.5
- logit_scale: float32 [], replicated, may hold values from 30 to 100
Outputs:
- loss: float32 [], replicated
- grad_images: float32 [16384, 1280], P(('row', 'col'))
- grad_texts: float32 [16384, 1280], P(('col', 'row'))
- grad_scale: float32 [], replicated
All inputs are finite; a program needn't handle non-finite values.
Results may differ from a plain program's by a relative error of at most 0.0024.
Values may be sent and summed in bfloat16 or wider, within the bound.
No kernel may reach another device: no remote copies, remote signals or barrier semaphores. Data moves between devices by JAX's collectives and lax.ppermute only.
A program may use at most 128 MiB of HBM per device.

v0:
```python
import functools
import itertools

import jax
import jax.numpy as jnp
import numpy as np
from jax import lax
from jax.experimental import pallas as pl
from jax.experimental.pallas import tpu as pltpu
from jax.sharding import PartitionSpec as P

LOG2E = 1.4426950408889634
LN2 = 0.6931471805599453
AXES = ("row", "col")
ROWS = 256
VMEM = 60 * 1024 * 1024
EXTRA = 16
CALLS = ((0, 2), (2, 5), (5, 8))


def linear(x, y, z, core):
    return (((x % 2) * 2 + core) * 4 + z) * 8 + (x // 2) * 4 + y


def devices():
    return itertools.product(range(4), range(4), range(4), range(2))


def partner_perm():
    return [(linear(x, y, z, c), linear(x, y, z, 1 - c)) for x, y, z, c in devices()]


TARGETS = ((2, 1), (2, 0), (1, 1), (-1, 1), (1, 0), (-1, 0), (0, 1), (0, 0))


def moved(x, y, z, core, steps, pair):
    if core == 0:
        return (3 - x if pair else x, (y + steps) % 4, z, core)
    return (x ^ 1 if pair else x, y, (z + steps) % 4, core)


def ring_perm(steps, pair):
    return [(linear(*d), linear(*moved(*d, steps, pair))) for d in devices()]


def group_of(x, y, z, core):
    return sorted(linear(*moved(x, y, z, core, steps, pair)) for steps, pair in TARGETS)


def groups():
    return sorted(set(tuple(group_of(*d)) for d in devices()))


def block_ids(x, y, z, core):
    out = []
    for member in group_of(x, y, z, core):
        row, col = member // 32, member % 32
        for c in (0, 1):
            at = (row // 2) * 2 + c
            out.append(at * 32 + col if core == 0 else col * 4 + at)
    return out


def tables():
    match = np.full((128, 16), -1, np.int32)
    place = np.zeros((128, 8), np.int32)
    for d in devices():
        x, y, z, c = d
        own, other = block_ids(x, y, z, c), block_ids(x, y, z, 1 - c)
        for k, block in enumerate(own):
            if block in other:
                match[linear(*d), k] = other.index(block)
        for k, (steps, pair) in enumerate(TARGETS):
            place[linear(*d), k] = group_of(*d).index(linear(*moved(*d, steps, pair)))
    return match, place


def to_column(row):
    n = row.shape[1]
    eye = lax.broadcasted_iota(jnp.int32, (n, n), 0) == lax.broadcasted_iota(jnp.int32, (n, n), 1)
    return jnp.sum(jnp.where(eye, jnp.broadcast_to(row, (n, n)), 0.0), axis=1, keepdims=True)


def to_row(column):
    n = column.shape[0]
    eye = lax.broadcasted_iota(jnp.int32, (n, n), 0) == lax.broadcasted_iota(jnp.int32, (n, n), 1)
    return jnp.sum(jnp.where(eye, jnp.broadcast_to(column, (n, n)), 0.0), axis=0, keepdims=True)


def eye(n):
    return lax.broadcasted_iota(jnp.int32, (n, n), 0) == lax.broadcasted_iota(jnp.int32, (n, n), 1)


def score_kernel(match_ref, scale_ref, own_ref, other_ref, scores_ref, stats_ref):
    step = pl.program_id(0)
    chunk = 512
    peak = total = weighted = None
    for at in range(0, other_ref.shape[0], chunk):
        scores = scale_ref[0] * lax.dot_general(
            own_ref[...],
            other_ref[at : at + chunk, :],
            (((1,), (1,)), ((), ())),
            preferred_element_type=jnp.float32,
        )
        scores_ref[:, at : at + chunk] = scores
        parts = [scores[:, k : k + 128] for k in range(0, chunk, 128)]
        top = functools.reduce(jnp.maximum, parts)
        if peak is not None:
            top = jnp.maximum(top, peak)
        powers = [jnp.exp2(part - top) for part in parts]
        new_total = functools.reduce(jnp.add, powers)
        new_weighted = functools.reduce(jnp.add, [a * b for a, b in zip(powers, parts)])
        if peak is not None:
            shrink = jnp.exp2(peak - top)
            new_total = new_total + total * shrink
            new_weighted = new_weighted + weighted * shrink
        peak, total, weighted = top, new_total, new_weighted
    top = jnp.max(peak, axis=1, keepdims=True)
    shrink = jnp.exp2(peak - top)
    stats_ref[0:1, :] = to_row(top)
    stats_ref[1:2, :] = to_row(jnp.sum(total * shrink, axis=1, keepdims=True))
    stats_ref[2:3, :] = to_row(jnp.sum(weighted * shrink, axis=1, keepdims=True))
    stats_ref[3:4, :] = jnp.zeros_like(stats_ref[3:4, :])
    for half in range(ROWS // 128):
        place = match_ref[step * (ROWS // 128) + half]

        @pl.when(place >= 0)
        def _():
            rows = slice(half * 128, half * 128 + 128)
            corner = scores_ref[rows, pl.ds(pl.multiple_of(place * 128, 128), 128)]
            stats_ref[3:4, rows] = jnp.sum(jnp.where(eye(128), corner, 0.0), axis=0, keepdims=True)


def score_call(match, scale, own, other):
    n, width = own.shape
    m = other.shape[0]
    return pl.pallas_call(
        score_kernel,
        grid=(n // ROWS,),
        in_specs=[
            pl.BlockSpec(memory_space=pltpu.SMEM),
            pl.BlockSpec(memory_space=pltpu.SMEM),
            pl.BlockSpec((ROWS, width), lambda i: (i, 0)),
            pl.BlockSpec((m, width), lambda i: (0, 0)),
        ],
        out_specs=[
            pl.BlockSpec((ROWS, m), lambda i: (i, 0)),
            pl.BlockSpec((4, ROWS), lambda i: (0, i)),
        ],
        out_shape=[
            jax.ShapeDtypeStruct((n, m), jnp.float32),
            jax.ShapeDtypeStruct((4, n), jnp.float32),
        ],
        compiler_params=pltpu.CompilerParams(vmem_limit_bytes=VMEM),
        cost_estimate=pl.CostEstimate(
            flops=2 * n * m * width, bytes_accessed=4 * n * m, transcendentals=n * m
        ),
        name="scores",
    )(match, scale, own, other)


def grad_kernel(
    pairs, count, has_own, place_ref, match_ref, scale_ref, own_lse_ref, other_lse_ref, scores_ref, other_ref, *refs
):
    outs = refs[:count]
    weights, blocks, own, other, out_sems, other_sem = refs[count:]
    step = pl.program_id(0)
    m = other.shape[0]
    load_other = pltpu.make_async_copy(other_ref, other, other_sem)
    stores = [
        pltpu.make_async_copy(own if has_own and k == count - 1 else blocks.at[k], outs[k], out_sems.at[k])
        for k in range(count)
    ]

    @pl.when(step == 0)
    def _():
        load_other.start()

    begin = pl.multiple_of(place_ref[step] * ROWS, ROWS)
    own_lse = to_column(own_lse_ref[:, pl.ds(begin, ROWS)])
    for at in range(0, m, 512):
        part = scores_ref[:, at : at + 512]
        weights[:, at : at + 512] = (
            jnp.exp2(part - own_lse) + jnp.exp2(part - other_lse_ref[:, at : at + 512])
        ).astype(jnp.bfloat16)
    for half in range(ROWS // 128):
        place = match_ref[place_ref[step] * (ROWS // 128) + half]

        @pl.when(place >= 0)
        def _():
            rows = slice(half * 128, half * 128 + 128)
            columns = pl.ds(pl.multiple_of(place * 128, 128), 128)
            corner = scores_ref[rows, columns]
            weight = jnp.exp2(corner - own_lse[rows]) + jnp.exp2(corner - other_lse_ref[:, columns])
            weights[rows, columns] = (weight - jnp.where(eye(128), 1.0 / pairs, 0.0)).astype(jnp.bfloat16)

    @pl.when(step == 0)
    def _():
        load_other.wait()

    grad = scale_ref[0] * jnp.dot(weights[...], other[...], preferred_element_type=jnp.float32)
    blocks[step, 0:ROWS, :] = grad.astype(jnp.bfloat16)
    if has_own:
        own[...] = grad
    parts = other_lse_ref[:, m : m + 256]
    high = parts.astype(jnp.bfloat16).astype(jnp.float32)
    middle = (parts - high).astype(jnp.bfloat16).astype(jnp.float32)
    row = lax.broadcasted_iota(jnp.int32, (EXTRA, 256), 0)
    rows = [jnp.broadcast_to(v, (EXTRA, 256)) for v in (high, middle, parts - high - middle)]
    tile = jnp.where(row == 0, rows[0], jnp.where(row == 1, rows[1], jnp.where(row == 2, rows[2], 0.0)))
    blocks[step, ROWS:, :] = jnp.zeros((EXTRA, blocks.shape[2]), jnp.bfloat16)
    blocks[step, ROWS:, 0:256] = tile.astype(jnp.bfloat16)
    for k in range(count):

        @pl.when(step == k)
        def _():
            stores[k].start()

    @pl.when(step == count - 1)
    def _():
        for store in stores:
            store.wait()


def grad_call(pairs, targets, places, match, scale, scores, own_lse, other_lse, other):
    m, width = other.shape
    count = len(targets)
    has_own = targets[-1] == (0, 0)
    smem, vmem, anywhere = (pl.BlockSpec(memory_space=s) for s in (pltpu.SMEM, pltpu.VMEM, pl.ANY))
    sent = jax.ShapeDtypeStruct((ROWS + EXTRA, width), jnp.bfloat16)
    kept = jax.ShapeDtypeStruct((ROWS, width), jnp.float32)
    return pl.pallas_call(
        functools.partial(grad_kernel, pairs, count, has_own),
        grid_spec=pltpu.PrefetchScalarGridSpec(
            num_scalar_prefetch=1,
            grid=(count,),
            in_specs=[
                smem,
                smem,
                vmem,
                vmem,
                pl.BlockSpec((ROWS, m), lambda i, place: (place[i], 0)),
                anywhere,
            ],
            out_specs=[anywhere] * count,
            scratch_shapes=[
                pltpu.VMEM((ROWS, m), jnp.bfloat16),
                pltpu.VMEM((count, ROWS + EXTRA, width), jnp.bfloat16),
                pltpu.VMEM((ROWS, width), jnp.float32),
                pltpu.VMEM((m, width), jnp.bfloat16),
                pltpu.SemaphoreType.DMA((count,)),
                pltpu.SemaphoreType.DMA,
            ],
        ),
        out_shape=[kept if has_own and k == count - 1 else sent for k in range(count)],
        compiler_params=pltpu.CompilerParams(vmem_limit_bytes=VMEM),
        cost_estimate=pl.CostEstimate(
            flops=2 * count * ROWS * m * width,
            bytes_accessed=4 * count * ROWS * m,
            transcendentals=2 * count * ROWS * m,
        ),
        name="grads",
    )(places, match, scale, own_lse, other_lse, scores, other)


def on_device(images, texts, logit_scale):
    shard, width = images.shape
    pairs = shard * 128
    me = lax.axis_index(AXES)
    first = lax.rem(lax.axis_index("row"), 2) == 0
    swap = functools.partial(lax.ppermute, axis_name=AXES, perm=partner_perm())
    members = [list(g) for g in groups()]
    match, place = (lax.dynamic_slice(jnp.asarray(t), (me, 0), (1, t.shape[1])).reshape(-1) for t in tables())

    def spread(value):
        everywhere = jnp.broadcast_to(value[None], (8,) + value.shape)
        return lax.all_to_all(everywhere, AXES, 0, 0, axis_index_groups=members, tiled=True)

    got = swap(jnp.where(first, texts, images))
    mine = jnp.where(first, images, texts)
    chip = jnp.concatenate([jnp.where(first, mine, got), jnp.where(first, got, mine)], axis=0)
    own = spread(chip).reshape(16 * shard, width)
    other = swap(own)

    scale2 = (logit_scale * LOG2E).reshape(1)
    scores, stats = score_call(match, scale2, own, other)
    peaks, totals, weighted, matched = (spread(stats)[:, k] for k in range(4))
    peak = jnp.max(peaks, axis=0, keepdims=True)
    shrink = jnp.exp2(peaks - peak)
    total = jnp.sum(totals * shrink, axis=0, keepdims=True)
    shift = float(np.log2(2.0 * pairs))
    own_lse = peak + jnp.log2(total) + shift

    diagonal = jnp.sum(matched)
    mean_score = jnp.sum(jnp.sum(weighted * shrink, axis=0, keepdims=True) / total)
    parts = [jnp.sum(own_lse - shift) - diagonal, mean_score - diagonal]
    other_lse = swap(jnp.concatenate([own_lse] + [jnp.broadcast_to(v, (1, 128)) for v in parts], axis=1))

    received = []
    kept = None
    for begin, end in CALLS:
        targets = TARGETS[begin:end]
        out = grad_call(
            pairs, targets, place[begin:end], match, logit_scale.reshape(1), scores, own_lse, other_lse, other
        )
        for target, grad in zip(targets, out):
            if target == (0, 0):
                kept = grad
            else:
                received.append(lax.ppermute(grad, AXES, ring_perm(*target)))
    received = [v.astype(jnp.float32) for v in received]
    summed = functools.reduce(jnp.add, [v[:ROWS] for v in received]) + kept
    parts = functools.reduce(jnp.add, [jnp.sum(v[ROWS : ROWS + 3, 0:256], axis=0, keepdims=True) for v in received])
    parts = parts + other_lse[:, 16 * shard :]
    parts = jnp.pad(parts, ((0, 7), (0, width - 256)))
    keep = jnp.where(first, summed[:shard], summed[shard:])
    back = swap(jnp.concatenate([jnp.where(first, summed[shard:], summed[:shard]), parts], axis=0))
    parts = (parts[0] + back[shard]) * (LN2 / (2.0 * pairs))
    return (
        parts[0],
        jnp.where(first, keep, back[:shard]),
        jnp.where(first, back[:shard], keep),
        parts[128] / logit_scale,
    )


def solution(mesh):
    in_specs = (P(("row", "col"), None), P(("col", "row"), None), P())
    out_specs = (P(), P(("row", "col"), None), P(("col", "row"), None), P())
    return jax.shard_map(
        on_device, mesh=mesh, in_specs=in_specs, out_specs=out_specs, check_vma=False
    )
```

profile of v0, /device:TPU:1, one launch (start us, length us, event | category | flops | bytes accessed | tf_op | source)
XLA Modules:
  0.0 160.4 jit_solution(8549833768974607690)
XLA Ops:
  0.6 1.0 broadcast_select_fusion.2
  1.7 1.5 collective-permute-start
  3.2 1.3 collective-permute-done
  4.4 1.0 broadcast_select_fusion.1
  5.9 38.7 %all_to_all.13 = bf16[8,256,1280]{2,1,0:T(8,128)(2,1)} all-to-all(bf16[8,256,1280]{2,1,0:T(8,128)(2,1)S(1)} %broadcast_in_dim.8), channel_id=1, replica_groups={{0,1,2,3,68,69,70,71},{4,5,6,7,64,65,66,67},{8,9,10,11,76,77,78,79},{12..., dimensions={0} | all-to-all | bytes 10485760 | tf_op jit(solution)/shard_map/all_to_all | solution.py:277
  44.6 3.4 %collective-permute-start.1 = (bf16[2048,1280]{1,0:T(8,128)(2,1)}, bf16[2048,1280]{1,0:T(8,128)(2,1)}, u32[]{:S(2)}, u32[]{:S(2)}) collective-permute-start(bf16[2048,1280]{1,0:T(8,128)(2,1)} %bitcast.4.own_ref), channel_id=1, source_target_pairs={{0,32},{32,0},{8,40},{40,8},{16,48},{48,16},{24,56},{56,24},{1,33}... | collective-permute-start | bytes 15728648 | tf_op jit(solution)/shard_map/ppermute | solution.py:283
  48.7 1.2 dynamic-slice_bitcast_fusion.match_ref
  49.9 6.7 %collective-permute-done.1.other_ref = bf16[2048,1280]{1,0:T(8,128)(2,1)} collective-permute-done((bf16[2048,1280]{1,0:T(8,128)(2,1)}, bf16[2048,1280]{1,0:T(8,128)(2,1)}, u32[]{:S(2)}, u32[]{:S(2)}) %collective-permute-start.1) | collective-permute-done | bytes 5242912 | tf_op jit(solution)/shard_map/ppermute | solution.py:283
  56.6 19.1 %scores.1 = (f32[2048,2048]{1,0:T(8,128)}, f32[4,2048]{1,0:T(4,128)}) custom-call(s32[16]{0:T(128)} %dynamic-slice_bitcast_fusion.match_ref, f32[1]{0:T(128)} %bitcast.3.scale_ref, bf16[2048,1280]{1,0:T(8,128)(2,1)} %bitcast.4.own_ref, bf16[2048,1280]{1,0:T(8,128)(2,1)} %collective-permute-done.1.other_ref), custom_call_target="tpu_custom_call" | custom-call | flops 10737418240 | bytes 16777216 | tf_op jit(solution)/shard_map/scores/pallas_call | solution.py:137
  75.7 1.5 broadcast_in_dim.9
  77.2 4.9 %all-to-all-start.1 = ((f32[8,4,2048]{2,1,0:T(4,128)}), f32[8,4,2048]{2,1,0:T(4,128)S(1)}, u32[]{:S(2)}, u32[]{:S(2)}) async-start(f32[8,4,2048]{2,1,0:T(4,128)} %broadcast_in_dim.9), calls=%async_computation.1 | async-start | bytes 524288 | tf_op jit(solution)/shard_map/all_to_all | solution.py:277
  82.1 0.7 constant_dynamic-slice_fusion
  83.4 4.8 %all-to-all-done.1 = f32[8,4,2048]{2,1,0:T(4,128)S(1)} async-done(((f32[8,4,2048]{2,1,0:T(4,128)}), f32[8,4,2048]{2,1,0:T(4,128)S(1)}, u32[]{:S(2)}, u32[]{:S(2)}) %all-to-all-start.1) | async-done | bytes 262176 | tf_op jit(solution)/shard_map/all_to_all | solution.py:277
  88.2 0.8 fusion.10
  89.1 0.7 fusion.9
  92.4 1.3 collective-permute-start.2
  94.5 0.6 copy-done.2
  95.1 9.4 %grads.3 = (bf16[272,1280]{1,0:T(8,128)(2,1)}, bf16[272,1280]{1,0:T(8,128)(2,1)}) custom-call(s32[2]{0:T(128)} %slice_bitcast_fusion.2.place_ref, s32[16]{0:T(128)} %dynamic-slice_bitcast_fusion.match_ref, f32[1]{0:T(128)} %bitcast.37.scale_ref, f32[1,2048]{1,0:T(1,128)} %bitcast.41, f32[1,2304]{1,0:T(1,128)} %copy-done.2, ...), custom_call_target="tpu_custom_call" | custom-call | flops 2684354560 | bytes 4194304 | tf_op jit(solution)/shard_map/grads/pallas_call | solution.py:232
  104.7 3.5 %collective-permute-start.4 = (bf16[272,1280]{1,0:T(8,128)(2,1)}, bf16[272,1280]{1,0:T(8,128)(2,1)S(1)}, u32[]{:S(2)}, u32[]{:S(2)}) collective-permute-start(bf16[272,1280]{1,0:T(8,128)(2,1)} %get-tuple-element.17), channel_id=1, source_target_pairs={{0,2},{32,48},{8,10},{40,56},{16,18},{48,32},{24,26},{56,40},{1,3}... | collective-permute-start | bytes 2088968 | tf_op jit(solution)/shard_map/ppermute | solution.py:310
  108.2 11.6 %grads.4 = (bf16[272,1280]{1,0:T(8,128)(2,1)}, bf16[272,1280]{1,0:T(8,128)(2,1)}, bf16[272,1280]{1,0:T(8,128)(2,1)}) custom-call(s32[3]{0:T(128)} %get-tuple-element.42.place_ref, s32[16]{0:T(128)} %dynamic-slice_bitcast_fusion.match_ref, f32[1]{0:T(128)} %bitcast.38.scale_ref, f32[1,2048]{1,0:T(1,128)} %bitcast.42, f32[1,2304]{1,0:T(1,128)} %copy-done.2, ...), custom_call_target="tpu_custom_call" | custom-call | flops 4026531840 | bytes 6291456 | tf_op jit(solution)/shard_map/grads/pallas_call | solution.py:232
  119.9 1.8 %collective-permute-start.5 = (bf16[272,1280]{1,0:T(8,128)(2,1)}, bf16[272,1280]{1,0:T(8,128)(2,1)S(1)}, u32[]{:S(2)}, u32[]{:S(2)}) collective-permute-start(bf16[272,1280]{1,0:T(8,128)(2,1)} %get-tuple-element.18), channel_id=1, source_target_pairs={{0,69},{32,104},{8,77},{40,112},{16,85},{48,120},{24,93},{56,96},{... | collective-permute-start | bytes 2088968 | tf_op jit(solution)/shard_map/ppermute | solution.py:310
  121.7 2.2 %collective-permute-start.6 = (bf16[272,1280]{1,0:T(8,128)(2,1)}, bf16[272,1280]{1,0:T(8,128)(2,1)S(1)}, u32[]{:S(2)}, u32[]{:S(2)}) collective-permute-start(bf16[272,1280]{1,0:T(8,128)(2,1)} %get-tuple-element.19), channel_id=1, source_target_pairs={{0,71},{32,120},{8,79},{40,96},{16,87},{48,104},{24,95},{56,112},{... | collective-permute-start | bytes 2088968 | tf_op jit(solution)/shard_map/ppermute | solution.py:310
  123.9 11.9 %grads.5 = (bf16[272,1280]{1,0:T(8,128)(2,1)}, bf16[272,1280]{1,0:T(8,128)(2,1)}, f32[256,1280]{1,0:T(8,128)}) custom-call(s32[3]{0:T(128)} %get-tuple-element.43.place_ref, s32[16]{0:T(128)} %dynamic-slice_bitcast_fusion.match_ref, f32[1]{0:T(128)} %bitcast.39.scale_ref, f32[1,2048]{1,0:T(1,128)} %bitcast.43, f32[1,2304]{1,0:T(1,128)} %copy-done.2, ...), custom_call_target="tpu_custom_call" | custom-call | flops 4026531840 | bytes 6291456 | tf_op jit(solution)/shard_map/grads/pallas_call | solution.py:232
  135.9 2.6 %collective-permute-start.8 = (bf16[272,1280]{1,0:T(8,128)(2,1)}, bf16[272,1280]{1,0:T(8,128)(2,1)S(1)}, u32[]{:S(2)}, u32[]{:S(2)}) collective-permute-start(bf16[272,1280]{1,0:T(8,128)(2,1)} %get-tuple-element.21), channel_id=1, source_target_pairs={{0,3},{32,56},{8,11},{40,32},{16,19},{48,40},{24,27},{56,48},{1,0}... | collective-permute-start | bytes 2088968 | tf_op jit(solution)/shard_map/ppermute | solution.py:310
  138.5 0.7 collective-permute-start.9
  140.3 6.5 %collective-permute-done.8 = bf16[272,1280]{1,0:T(8,128)(2,1)S(1)} collective-permute-done((bf16[272,1280]{1,0:T(8,128)(2,1)}, bf16[272,1280]{1,0:T(8,128)(2,1)S(1)}, u32[]{:S(2)}, u32[]{:S(2)}) %collective-permute-start.8) | collective-permute-done | bytes 696352 | tf_op jit(solution)/shard_map/ppermute | solution.py:310
  147.0 1.9 %collective-permute-done.9 = bf16[272,1280]{1,0:T(8,128)(2,1)S(1)} collective-permute-done((bf16[272,1280]{1,0:T(8,128)(2,1)}, bf16[272,1280]{1,0:T(8,128)(2,1)S(1)}, u32[]{:S(2)}, u32[]{:S(2)}) %collective-permute-start.9) | collective-permute-done | bytes 696352 | tf_op jit(solution)/shard_map/ppermute | solution.py:310
  149.0 0.8 fusion
  149.9 0.7 slice_add_fusion.6
  150.6 4.5 %collective-permute-start.10 = (f32[136,1280]{1,0:T(8,128)S(1)}, f32[136,1280]{1,0:T(8,128)S(1)}, u32[]{:S(2)}, u32[]{:S(2)}) collective-permute-start(f32[136,1280]{1,0:T(8,128)S(1)} %pad_maximum_fusion), channel_id=1, source_target_pairs={{0,32},{32,0},{8,40},{40,8},{16,48},{48,16},{24,56},{56,24},{1,33}... | collective-permute-start | bytes 2088968 | tf_op jit(solution)/shard_map/ppermute | solution.py:317
  155.1 1.8 %collective-permute-done.10 = f32[136,1280]{1,0:T(8,128)S(1)} collective-permute-done((f32[136,1280]{1,0:T(8,128)S(1)}, f32[136,1280]{1,0:T(8,128)S(1)}, u32[]{:S(2)}, u32[]{:S(2)}) %collective-permute-start.10) | collective-permute-done | bytes 696352 | tf_op jit(solution)/shard_map/ppermute | solution.py:317
  158.1 1.2 slice_select_fusion
  (43 shorter events, 4.1 us)
Async XLA Ops:
  1.7 2.8 %collective-permute-start = (bf16[128,1280]{1,0:T(8,128)(2,1)S(1)}, bf16[128,1280]{1,0:T(8,128)(2,1)S(1)}, u32[]{:S(2)}, u32[]{:S(2)}) collective-permute-start(bf16[128,1280]{1,0:T(8,128)(2,1)S(1)} %broadcast_select_fusion.2), channel_id=1, source_target_pairs={{0,32},{32,0},{8,40},{40,8},{16,48},{48,16},{24,56},{56,24},{1,33}... | collective-permute-start | bytes 983048 | tf_op jit(solution)/shard_map/ppermute | solution.py:279
  44.6 12.1 %collective-permute-start.1 = (bf16[2048,1280]{1,0:T(8,128)(2,1)}, bf16[2048,1280]{1,0:T(8,128)(2,1)}, u32[]{:S(2)}, u32[]{:S(2)}) collective-permute-start(bf16[2048,1280]{1,0:T(8,128)(2,1)} %bitcast.4.own_ref), channel_id=1, source_target_pairs={{0,32},{32,0},{8,40},{40,8},{16,48},{48,16},{24,56},{56,24},{1,33}... | collective-permute-start | bytes 15728648 | tf_op jit(solution)/shard_map/ppermute | solution.py:283
  77.2 11.0 %all-to-all-start.1 = ((f32[8,4,2048]{2,1,0:T(4,128)}), f32[8,4,2048]{2,1,0:T(4,128)S(1)}, u32[]{:S(2)}, u32[]{:S(2)}) async-start(f32[8,4,2048]{2,1,0:T(4,128)} %broadcast_in_dim.9), calls=%async_computation.1 | async-start | bytes 524288 | tf_op jit(solution)/shard_map/all_to_all | solution.py:277
  89.8 4.8 %copy-start.1 = (f32[2048]{0:T(1024)}, f32[2048]{0:T(1024)S(1)}, u32[]{:S(2)}) copy-start(f32[2048]{0:T(1024)S(1)} %get-tuple-element.39) | copy-start | bytes 24580
  92.4 2.1 %collective-permute-start.2 = (f32[1,2304]{1,0:T(1,128)S(1)}, f32[1,2304]{1,0:T(1,128)S(1)}, u32[]{:S(2)}, u32[]{:S(2)}) collective-permute-start(f32[1,2304]{1,0:T(1,128)S(1)} %reshape_maximum_fusion), channel_id=1, source_target_pairs={{0,32},{32,0},{8,40},{40,8},{16,48},{48,16},{24,56},{56,24},{1,33}... | collective-permute-start | bytes 27656 | tf_op jit(solution)/shard_map/ppermute | solution.py:297
  94.5 0.6 copy-start.2
  104.6 31.3 %collective-permute-start.3 = (bf16[272,1280]{1,0:T(8,128)(2,1)}, bf16[272,1280]{1,0:T(8,128)(2,1)S(1)}, u32[]{:S(2)}, u32[]{:S(2)}) collective-permute-start(bf16[272,1280]{1,0:T(8,128)(2,1)} %get-tuple-element.16), channel_id=1, source_target_pairs={{0,70},{32,112},{8,78},{40,120},{16,86},{48,96},{24,94},{56,104},{... | collective-permute-start | bytes 2088968 | tf_op jit(solution)/shard_map/ppermute | solution.py:310
  104.7 33.8 %collective-permute-start.4 = (bf16[272,1280]{1,0:T(8,128)(2,1)}, bf16[272,1280]{1,0:T(8,128)(2,1)S(1)}, u32[]{:S(2)}, u32[]{:S(2)}) collective-permute-start(bf16[272,1280]{1,0:T(8,128)(2,1)} %get-tuple-element.17), channel_id=1, source_target_pairs={{0,2},{32,48},{8,10},{40,56},{16,18},{48,32},{24,26},{56,40},{1,3}... | collective-permute-start | bytes 2088968 | tf_op jit(solution)/shard_map/ppermute | solution.py:310
  119.9 19.5 %collective-permute-start.5 = (bf16[272,1280]{1,0:T(8,128)(2,1)}, bf16[272,1280]{1,0:T(8,128)(2,1)S(1)}, u32[]{:S(2)}, u32[]{:S(2)}) collective-permute-start(bf16[272,1280]{1,0:T(8,128)(2,1)} %get-tuple-element.18), channel_id=1, source_target_pairs={{0,69},{32,104},{8,77},{40,112},{16,85},{48,120},{24,93},{56,96},{... | collective-permute-start | bytes 2088968 | tf_op jit(solution)/shard_map/ppermute | solution.py:310
  121.7 17.8 %collective-permute-start.6 = (bf16[272,1280]{1,0:T(8,128)(2,1)}, bf16[272,1280]{1,0:T(8,128)(2,1)S(1)}, u32[]{:S(2)}, u32[]{:S(2)}) collective-permute-start(bf16[272,1280]{1,0:T(8,128)(2,1)} %get-tuple-element.19), channel_id=1, source_target_pairs={{0,71},{32,120},{8,79},{40,96},{16,87},{48,104},{24,95},{56,112},{... | collective-permute-start | bytes 2088968 | tf_op jit(solution)/shard_map/ppermute | solution.py:310
  123.9 16.3 %collective-permute-start.7 = (bf16[272,1280]{1,0:T(8,128)(2,1)}, bf16[272,1280]{1,0:T(8,128)(2,1)S(1)}, u32[]{:S(2)}, u32[]{:S(2)}) collective-permute-start(bf16[272,1280]{1,0:T(8,128)(2,1)} %get-tuple-element.20), channel_id=1, source_target_pairs={{0,1},{32,40},{8,9},{40,48},{16,17},{48,56},{24,25},{56,32},{1,2},... | collective-permute-start | bytes 2088968 | tf_op jit(solution)/shard_map/ppermute | solution.py:310
  135.9 10.9 %collective-permute-start.8 = (bf16[272,1280]{1,0:T(8,128)(2,1)}, bf16[272,1280]{1,0:T(8,128)(2,1)S(1)}, u32[]{:S(2)}, u32[]{:S(2)}) collective-permute-start(bf16[272,1280]{1,0:T(8,128)(2,1)} %get-tuple-element.21), channel_id=1, source_target_pairs={{0,3},{32,56},{8,11},{40,32},{16,19},{48,40},{24,27},{56,48},{1,0}... | collective-permute-start | bytes 2088968 | tf_op jit(solution)/shard_map/ppermute | solution.py:310
  138.5 10.4 %collective-permute-start.9 = (bf16[272,1280]{1,0:T(8,128)(2,1)}, bf16[272,1280]{1,0:T(8,128)(2,1)S(1)}, u32[]{:S(2)}, u32[]{:S(2)}) collective-permute-start(bf16[272,1280]{1,0:T(8,128)(2,1)} %get-tuple-element.22), channel_id=1, source_target_pairs={{0,68},{32,96},{8,76},{40,104},{16,84},{48,112},{24,92},{56,120},{... | collective-permute-start | bytes 2088968 | tf_op jit(solution)/shard_map/ppermute | solution.py:310
  146.9 2.1 %copy-start = (f32[256,1280]{1,0:T(8,128)S(1)}, f32[256,1280]{1,0:T(8,128)}, u32[]{:S(2)}) copy-start(f32[256,1280]{1,0:T(8,128)} %get-tuple-element.23) | copy-start | bytes 3932164
  150.6 6.3 %collective-permute-start.10 = (f32[136,1280]{1,0:T(8,128)S(1)}, f32[136,1280]{1,0:T(8,128)S(1)}, u32[]{:S(2)}, u32[]{:S(2)}) collective-permute-start(f32[136,1280]{1,0:T(8,128)S(1)} %pad_maximum_fusion), channel_id=1, source_target_pairs={{0,32},{32,0},{8,40},{40,8},{16,48},{48,16},{24,56},{56,24},{1,33}... | collective-permute-start | bytes 2088968 | tf_op jit(solution)/shard_map/ppermute | solution.py:317
where the time goes:
time: 161 us; the launch traced here: 160 us
  Pallas kernels  52.1 us (32%)
  blocking collectives  38.7 us (24%)
  starting transfers between devices  26.6 us (17%)
  waiting for transfers between devices  23.8 us (15%)
  other arithmetic  7.23 us (4%)
  local copies, waits for them, and re-layouts  6.07 us (4%)
  between operations  5.85 us (4%)
    all_to_all x1, blocking collectives, spread(): lax.all_to_all(everywhere, AXES, 0, 0, axis_index_groups=members, tiled=T...  38.7 us
    pallas_call x3, Pallas kernels, grad_call(): pl.pallas_call(functools.partial(grad_kernel, pairs, count, has_own), gri...  33 us
    pallas_call x1, Pallas kernels, score_call(): pl.pallas_call(score_kernel, grid=(n // ROWS,), in_specs=[pl.BlockSpec(me...  19.1 us
    ppermute x7, starting transfers between devices, on_device(): received.append(lax.ppermute(grad, AXES, ring_perm(*target)))  11 us
    ppermute x7, waiting for transfers between devices, on_device(): received.append(lax.ppermute(grad, AXES, ring_perm(*target)))  8.97 us
    ppermute x1, waiting for transfers between devices, on_device(): other = swap(own)  6.74 us
    all_to_all x1, starting transfers between devices, spread(): lax.all_to_all(everywhere, AXES, 0, 0, axis_index_groups=members, tiled=T...  4.89 us
    all_to_all x1, waiting for transfers between devices, spread(): lax.all_to_all(everywhere, AXES, 0, 0, axis_index_groups=members, tiled=T...  4.8 us
  transfers between devices with their start and end apart: 12, of which 8 were waited for; matrix products, arithmetic and copies ran while one was open for 2% of the time, Pallas kernels for 15%

commit v1 on v0

v1 whole, which is shorter than its diff:
```python
import functools
import itertools

import jax
import jax.numpy as jnp
import numpy as np
from jax import lax
from jax.experimental import pallas as pl
from jax.experimental.pallas import tpu as pltpu
from jax.sharding import PartitionSpec as P

LOG2E = 1.4426950408889634
LN2 = 0.6931471805599453
AXES = ("row", "col")
ROWS = 256
VMEM = 63_400_000
EXTRA = 16
PAIR = 2


def linear(x, y, z, core):
    return (((x % 2) * 2 + core) * 4 + z) * 8 + (x // 2) * 4 + y


def devices():
    return itertools.product(range(4), range(4), range(4), range(2))


def partner_perm():
    return [(linear(x, y, z, c), linear(x, y, z, 1 - c)) for x, y, z, c in devices()]


PIECES = ((0, 0), (1, 0), (-1, 0), (0, 1), (2, 0), (-1, 1), (1, 1), (2, 1))


def moved(x, y, z, core, steps, pair):
    if core == 0:
        return (3 - x if pair else x, (y + steps) % 4, z, core)
    return (x ^ 1 if pair else x, y, (z + steps) % 4, core)


def ring_perm(steps, pair):
    return [(linear(*d), linear(*moved(*d, steps, pair))) for d in devices()]


def group_of(x, y, z, core):
    return sorted(linear(*moved(x, y, z, core, steps, pair)) for steps, pair in PIECES)


def groups():
    return sorted(set(tuple(group_of(*d)) for d in devices()))


def block_ids(x, y, z, core):
    out = []
    for steps, pair in PIECES:
        member = linear(*moved(x, y, z, core, steps, pair))
        row, col = member // 32, member % 32
        for c in (0, 1):
            at = (row // 2) * 2 + c
            out.append(at * 32 + col if core == 0 else col * 4 + at)
    return out


def tables():
    table = np.full((128, 32), -1, np.int32)
    for d in devices():
        x, y, z, c = d
        own, other = block_ids(x, y, z, c), block_ids(x, y, z, 1 - c)
        for k, block in enumerate(own):
            if block in other:
                table[linear(*d), k] = other.index(block)
        for side in (0, 1):
            e = (x, y, z, c ^ side)
            for k, (steps, pair) in enumerate(PIECES):
                table[linear(*d), 16 + 8 * side + k] = group_of(*e).index(linear(*moved(*e, steps, pair)))
    return table


def to_column(row):
    n = row.shape[1]
    eye = lax.broadcasted_iota(jnp.int32, (n, n), 0) == lax.broadcasted_iota(jnp.int32, (n, n), 1)
    return jnp.sum(jnp.where(eye, jnp.broadcast_to(row, (n, n)), 0.0), axis=1, keepdims=True)


def eye(n):
    return lax.broadcasted_iota(jnp.int32, (n, n), 0) == lax.broadcasted_iota(jnp.int32, (n, n), 1)


def fetch(parts, whole, sems):
    return [
        pltpu.make_async_copy(part, whole.at[pl.ds(k * ROWS, ROWS)], sems.at[k]) for k, part in enumerate(parts)
    ]


def table_place(table_ref, side, piece):
    return pl.multiple_of(table_ref[16 + 8 * side + piece] * ROWS, ROWS)


def tile_stats(scale, rows, other_at, width, scores_ref):
    chunk = 512 if width % 512 == 0 else 256
    peak = total = weighted = None
    for at in range(0, width, chunk):
        scores = scale * lax.dot_general(
            rows, other_at(at, chunk), (((1,), (1,)), ((), ())), preferred_element_type=jnp.float32
        )
        scores_ref[:, at : at + chunk] = scores
        parts = [scores[:, k : k + 128] for k in range(0, chunk, 128)]
        top = functools.reduce(jnp.maximum, parts)
        if peak is not None:
            top = jnp.maximum(top, peak)
        powers = [jnp.exp2(part - top) for part in parts]
        new_total = functools.reduce(jnp.add, powers)
        new_weighted = functools.reduce(jnp.add, [a * b for a, b in zip(powers, parts)])
        if peak is not None:
            shrink = jnp.exp2(peak - top)
            new_total = new_total + total * shrink
            new_weighted = new_weighted + weighted * shrink
        peak, total, weighted = top, new_total, new_weighted
    peak = peak.T
    top = jnp.max(peak, axis=0, keepdims=True)
    shrink = jnp.exp2(peak - top)
    return (
        top,
        jnp.sum(total.T * shrink, axis=0, keepdims=True),
        jnp.sum(weighted.T * shrink, axis=0, keepdims=True),
    )


def put_matched(table_ref, piece, begin, width, scores_ref, line):
    line[3:4, :] = jnp.zeros((1, ROWS), jnp.float32)
    for half in range(ROWS // 128):
        place = table_ref[piece * (ROWS // 128) + half] * 128 - begin

        @pl.when(jnp.logical_and(place >= 0, place < width))
        def _():
            span = slice(half * 128, half * 128 + 128)
            corner = scores_ref[span, pl.ds(pl.multiple_of(place, 128), 128)]
            line[3:4, span] = jnp.sum(jnp.where(eye(128), corner, 0.0), axis=0, keepdims=True)


def score_kernel(n, table_ref, scale_ref, *refs):
    own_refs, other_refs = refs[:n], refs[n : 2 * n]
    scores_ref, stats_ref, own, other, line, own_sems, other_sems = refs[2 * n :]
    step = pl.program_id(0)
    load_own, load_other = fetch(own_refs, own, own_sems), fetch(other_refs, other, other_sems)

    @pl.when(step == 0)
    def _():
        for copy in load_own[:1] + load_other + load_own[1:]:
            copy.start()
        for copy in load_own[:1] + load_other:
            copy.wait()

    @pl.when(step == 1)
    def _():
        for copy in load_own[1:]:
            copy.wait()

    rows = own[pl.ds(pl.multiple_of(step * ROWS, ROWS), ROWS), :]
    width = n * ROWS
    top, total, weighted = tile_stats(
        scale_ref[0], rows, lambda at, chunk: other[at : at + chunk, :], width, scores_ref
    )
    line[0:1, :] = top
    line[1:2, :] = total
    line[2:3, :] = weighted
    put_matched(table_ref, step, 0, width, scores_ref, line)
    stats_ref[...] = line[...]


def score_call(table, scale, own, other):
    n, width = len(own), own[0].shape[1]
    smem, anywhere = pl.BlockSpec(memory_space=pltpu.SMEM), pl.BlockSpec(memory_space=pl.ANY)
    return pl.pallas_call(
        functools.partial(score_kernel, n),
        grid=(n,),
        in_specs=[smem, smem] + [anywhere] * (2 * n),
        out_specs=[
            pl.BlockSpec((ROWS, n * ROWS), lambda i: (i, 0)),
            pl.BlockSpec((4, ROWS), lambda i: (0, i)),
        ],
        out_shape=[
            jax.ShapeDtypeStruct(((n + 1) * ROWS, (n + 1) * ROWS), jnp.float32),
            jax.ShapeDtypeStruct((4, n * ROWS), jnp.float32),
        ],
        scratch_shapes=[
            pltpu.VMEM((n * ROWS, width), jnp.bfloat16),
            pltpu.VMEM((n * ROWS, width), jnp.bfloat16),
            pltpu.VMEM((4, ROWS), jnp.float32),
            pltpu.SemaphoreType.DMA((n,)),
            pltpu.SemaphoreType.DMA((n,)),
        ],
        compiler_params=pltpu.CompilerParams(vmem_limit_bytes=VMEM),
        cost_estimate=pl.CostEstimate(
            flops=2 * n * n * ROWS * ROWS * width,
            bytes_accessed=4 * n * n * ROWS * ROWS,
            transcendentals=n * n * ROWS * ROWS,
        ),
        name="scores",
    )(table, scale, *own, *other)


def last_score_kernel(n, table_ref, scale_ref, before_ref, scores_in, *refs):
    own_refs, other_refs = refs[: n + 1], refs[n + 1 : 2 * n + 2]
    scores_out, stats_ref, own, other, row, column, line, own_sems, other_sems, out_sems = refs[2 * n + 2 :]
    load_own, load_other = fetch(own_refs, own, own_sems), fetch(other_refs, other, other_sems)
    for copy in load_own[n:] + load_other + load_own[:n]:
        copy.start()
    store_row = pltpu.make_async_copy(row, scores_out.at[pl.ds(n * ROWS, ROWS)], out_sems.at[n])
    store_column = [
        pltpu.make_async_copy(
            column.at[pl.ds(k * ROWS, ROWS)],
            scores_out.at[pl.ds(k * ROWS, ROWS), pl.ds(n * ROWS, ROWS)],
            out_sems.at[k],
        )
        for k in range(n)
    ]

    def put(piece):
        for member in range(8):
            stats_ref[member, :, pl.ds(table_place(table_ref, 0, piece), ROWS)] = line[...]

    def arrived(at, size):
        for k in range(at // ROWS, (at + size) // ROWS):
            load_other[k].wait()
        return other[at : at + size, :]

    load_own[n].wait()
    top, total, weighted = tile_stats(scale_ref[0], own[n * ROWS : (n + 1) * ROWS, :], arrived, (n + 1) * ROWS, row)
    line[0:1, :] = top
    line[1:2, :] = total
    line[2:3, :] = weighted
    put_matched(table_ref, n, 0, (n + 1) * ROWS, row, line)
    store_row.start()
    put(n)
    for copy in load_own[:n]:
        copy.wait()
    found = []
    for k in range(n):
        found.append(
            tile_stats(
                scale_ref[0],
                own[k * ROWS : (k + 1) * ROWS, :],
                lambda at, chunk: other[n * ROWS + at : n * ROWS + at + chunk, :],
                ROWS,
                column.at[pl.ds(k * ROWS, ROWS)],
            )
        )
    for k, (top, total, weighted) in enumerate(found):
        store_column[k].start()
        put_matched(table_ref, k, n * ROWS, ROWS, column.at[pl.ds(k * ROWS, ROWS)], line)
        old = before_ref[:, k * ROWS : (k + 1) * ROWS]
        new_top = jnp.maximum(old[0:1], top)
        old_shrink, new_shrink = jnp.exp2(old[0:1] - new_top), jnp.exp2(top - new_top)
        line[0:1, :] = new_top
        line[1:2, :] = old[1:2] * old_shrink + total * new_shrink
        line[2:3, :] = old[2:3] * old_shrink + weighted * new_shrink
        line[3:4, :] = old[3:4] + line[3:4, :]
        put(k)
    store_row.wait()
    for store in store_column:
        store.wait()


def last_score_call(table, scale, before, scores, own, other):
    n, width = len(own) - 1, own[0].shape[1]
    smem, vmem, anywhere = (pl.BlockSpec(memory_space=s) for s in (pltpu.SMEM, pltpu.VMEM, pl.ANY))
    rows = (n + 1) * ROWS
    return pl.pallas_call(
        functools.partial(last_score_kernel, n),
        in_specs=[smem, smem, vmem] + [anywhere] * (2 * n + 3),
        out_specs=[anywhere, vmem],
        out_shape=[
            jax.ShapeDtypeStruct(scores.shape, jnp.float32),
            jax.ShapeDtypeStruct((8, 4, rows), jnp.float32),
        ],
        scratch_shapes=[
            pltpu.VMEM((rows, width), jnp.bfloat16),
            pltpu.VMEM((rows, width), jnp.bfloat16),
            pltpu.VMEM((ROWS, rows), jnp.float32),
            pltpu.VMEM((n * ROWS, ROWS), jnp.float32),
            pltpu.VMEM((4, ROWS), jnp.float32),
            pltpu.SemaphoreType.DMA((n + 1,)),
            pltpu.SemaphoreType.DMA((n + 1,)),
            pltpu.SemaphoreType.DMA((n + 1,)),
        ],
        input_output_aliases={3: 0},
        compiler_params=pltpu.CompilerParams(vmem_limit_bytes=VMEM),
        cost_estimate=pl.CostEstimate(
            flops=2 * (2 * n + 1) * ROWS * ROWS * width,
            bytes_accessed=4 * (2 * n + 1) * ROWS * ROWS,
            transcendentals=(2 * n + 1) * ROWS * ROWS,
        ),
        name="last_scores",
    )(table, scale, before, scores, *own, *other)


def join_kernel(shift, stats_ref, out_ref):
    rows = out_ref.shape[1] - 256
    peak = functools.reduce(jnp.maximum, [stats_ref[k, 0:1, :] for k in range(8)])
    total = weighted = matched = 0.0
    for k in range(8):
        shrink = jnp.exp2(stats_ref[k, 0:1, :] - peak)
        total = total + stats_ref[k, 1:2, :] * shrink
        weighted = weighted + stats_ref[k, 2:3, :] * shrink
        matched = matched + stats_ref[k, 3:4, :]
    lse = peak + jnp.log2(total)
    out_ref[:, :rows] = lse + shift
    for k, value in enumerate((lse - matched, weighted / total - matched)):
        value = jnp.sum(value, axis=1, keepdims=True)
        out_ref[:, rows + 128 * k : rows + 128 * (k + 1)] = jnp.broadcast_to(value, (1, 128))


def join_call(shift, stats):
    return pl.pallas_call(
        functools.partial(join_kernel, shift),
        out_shape=jax.ShapeDtypeStruct((1, stats.shape[2] + 256), jnp.float32),
        name="join",
    )(stats)


def grad_kernel(pairs, pieces, table_ref, scale_ref, own_lse_ref, other_lse_ref, scores_ref, *refs):
    count = len(pieces)
    other_refs, outs = refs[:8], refs[8 : 8 + count]
    weights, (blocks, own, other, out_sems, other_sem) = refs[8 + count : 8 + count + PAIR], refs[8 + count + PAIR :]
    step = pl.program_id(0)
    m = scores_ref.shape[1]
    load_other = fetch(other_refs, other, other_sem)
    stores = [
        pltpu.make_async_copy(own if q == 0 else blocks.at[k], outs[k], out_sems.at[k])
        for k, q in enumerate(pieces)
    ]

    @pl.when(step == 0)
    def _():
        for copy in load_other:
            copy.start()

    extra = other_lse_ref[:, m : m + 256]
    high = extra.astype(jnp.bfloat16).astype(jnp.float32)
    middle = (extra - high).astype(jnp.bfloat16).astype(jnp.float32)
    row = lax.broadcasted_iota(jnp.int32, (EXTRA, 256), 0)
    rows = [jnp.broadcast_to(v, (EXTRA, 256)) for v in (high, middle, extra - high - middle)]
    tile = jnp.where(row == 0, rows[0], jnp.where(row == 1, rows[1], jnp.where(row == 2, rows[2], 0.0)))
    ones = eye(128).astype(jnp.float32)

    def weigh(k):
        piece = pieces[k] - PAIR * step
        own_lse = to_column(own_lse_ref[:, pl.ds(table_place(table_ref, 0, piece), ROWS)])
        at_row = (PAIR - 1 - k) * ROWS
        found = [table_ref[piece * (ROWS // 128) + half] for half in range(ROWS // 128)]
        for at in range(0, m, ROWS):
            part = scores_ref[at_row : at_row + ROWS, at : at + ROWS]
            other_lse = other_lse_ref[:, pl.ds(table_place(table_ref, 1, at // ROWS), ROWS)]
            weight = jnp.exp2(part - own_lse) + jnp.exp2(part - other_lse)
            for i in range(0, ROWS, 128):
                for j in range(0, ROWS, 128):
                    taken = jnp.where(found[i // 128] == (at + j) // 128, 1.0 / pairs, 0.0)
                    weights[k][i : i + 128, at + j : at + j + 128] = (
                        weight[i : i + 128, j : j + 128] - ones * taken
                    ).astype(jnp.bfloat16)

    def multiply(k):
        grad = scale_ref[0] * jnp.dot(weights[k][...], other[...], preferred_element_type=jnp.float32)
        slot = PAIR * step + k
        blocks[slot, 0:ROWS, :] = grad.astype(jnp.bfloat16)
        blocks[slot, ROWS:, :] = jnp.zeros((EXTRA, blocks.shape[2]), jnp.bfloat16)
        blocks[slot, ROWS:, 0:256] = tile.astype(jnp.bfloat16)
        if pieces[-1] == 0 and k == PAIR - 1:
            own[...] = grad

    weigh(0)

    @pl.when(step == 0)
    def _():
        for copy in load_other:
            copy.wait()

    multiply(0)
    for k in range(1, PAIR):
        weigh(k)
        multiply(k)
    for at in range(0, count, PAIR):

        @pl.when(step == at // PAIR)
        def _():
            for k in range(at, at + PAIR):
                stores[k].start()

    @pl.when(step == count // PAIR - 1)
    def _():
        for store in stores:
            store.wait()


def grad_call(name, pairs, pieces, table, scale, scores, own_lse, other_lse, other):
    width = other[0].shape[1]
    count = len(pieces)
    m = scores.shape[1]
    smem, vmem, anywhere = (pl.BlockSpec(memory_space=s) for s in (pltpu.SMEM, pltpu.VMEM, pl.ANY))
    sent = jax.ShapeDtypeStruct((ROWS + EXTRA, width), jnp.bfloat16)
    kept = jax.ShapeDtypeStruct((ROWS, width), jnp.float32)
    return pl.pallas_call(
        functools.partial(grad_kernel, pairs, pieces),
        grid=(count // PAIR,),
        in_specs=[
            smem,
            smem,
            vmem,
            vmem,
            pl.BlockSpec((PAIR * ROWS, m), lambda i: (pieces[0] // PAIR - i, 0)),
        ]
        + [anywhere] * 8,
        out_specs=[anywhere] * count,
        out_shape=[kept if q == 0 else sent for q in pieces],
        scratch_shapes=[pltpu.VMEM((ROWS, m), jnp.bfloat16)] * PAIR
        + [
            pltpu.VMEM((count, ROWS + EXTRA, width), jnp.bfloat16),
            pltpu.VMEM((ROWS, width), jnp.float32),
            pltpu.VMEM((m, width), jnp.bfloat16),
            pltpu.SemaphoreType.DMA((count,)),
            pltpu.SemaphoreType.DMA((8,)),
        ],
        compiler_params=pltpu.CompilerParams(vmem_limit_bytes=VMEM),
        cost_estimate=pl.CostEstimate(
            flops=2 * count * ROWS * m * width,
            bytes_accessed=4 * count * ROWS * m,
            transcendentals=2 * count * ROWS * m,
        ),
        name=name,
    )(table, scale, own_lse, other_lse, scores, *other)


def on_device(images, texts, logit_scale):
    shard, width = images.shape
    pairs = shard * 128
    me = lax.axis_index(AXES)
    first = lax.rem(lax.axis_index("row"), 2) == 0
    swap = functools.partial(lax.ppermute, axis_name=AXES, perm=partner_perm())
    members = [list(g) for g in groups()]
    table = lax.dynamic_slice(jnp.asarray(tables()), (me, 0), (1, 32)).reshape(-1)
    scale2 = (logit_scale * LOG2E).reshape(1)

    def send(value, steps, pair):
        return lax.ppermute(value, AXES, ring_perm(steps, pair))

    got = swap(jnp.where(first, texts, images))
    mine = jnp.where(first, images, texts)
    chip = jnp.concatenate([jnp.where(first, mine, got), jnp.where(first, got, mine)], axis=0)

    after, before, across = send(chip, -1, 0), send(chip, 1, 0), send(chip, 0, 1)
    near = [chip, after, before, across]
    middle = [send(after, -1, 0), send(across, 1, 0), send(after, 0, 1)]
    far = send(middle[2], -1, 0)
    own = near + middle
    other = [swap(v) for v in own]
    scores, stats = score_call(table, scale2, own, other)
    stats, far = lax.optimization_barrier((stats, far))
    other = other + [swap(far)]
    scores, stats = last_score_call(table, scale2, stats, scores, own + [far], other)

    spread = lax.all_to_all(stats, AXES, 0, 0, axis_index_groups=members, tiled=True)
    own_lse = join_call(float(np.log2(2.0 * pairs)), spread)
    other_lse = swap(own_lse)

    def grads(name, pieces):
        return grad_call(name, pairs, pieces, table, logit_scale.reshape(1), scores, own_lse, other_lse, other)

    received = [send(v, *PIECES[q]) for q, v in zip((7, 6, 5, 4), grads("grads_far", (7, 6, 5, 4)))]
    *near_grads, kept = grads("grads_near", (3, 2, 1, 0))
    received, near_grads = lax.optimization_barrier((received, near_grads))
    received += [send(v, *PIECES[q]) for q, v in zip((3, 2, 1), near_grads)]
    received = [v.astype(jnp.float32) for v in received]
    summed = functools.reduce(jnp.add, [v[:ROWS] for v in received]) + kept
    parts = functools.reduce(jnp.add, [jnp.sum(v[ROWS : ROWS + 3, 0:256], axis=0, keepdims=True) for v in received])
    parts = parts + other_lse[:, 16 * shard :]
    parts = jnp.pad(parts, ((0, 7), (0, width - 256)))
    keep = jnp.where(first, summed[:shard], summed[shard:])
    back = swap(jnp.concatenate([jnp.where(first, summed[shard:], summed[:shard]), parts], axis=0))
    parts = (parts[0] + back[shard]) * (LN2 / (2.0 * pairs))
    return (
        parts[0],
        jnp.where(first, keep, back[:shard]),
        jnp.where(first, back[:shard], keep),
        parts[128] / logit_scale,
    )


def solution(mesh):
    in_specs = (P(("row", "col"), None), P(("col", "row"), None), P())
    out_specs = (P(), P(("row", "col"), None), P(("col", "row"), None), P())
    return jax.shard_map(
        on_device, mesh=mesh, in_specs=in_specs, out_specs=out_specs, check_vma=False
    )
```

time: 161 us -> 154 us (0.957)
  blocking collectives: 38.7 us -> 10.2 us
  waiting for transfers between devices: 23.8 us -> 38 us
  starting transfers between devices: 26.6 us -> 36.7 us
  Pallas kernels: 52.1 us -> 55 us
  between operations: 5.85 us -> 3.35 us
  other arithmetic: 7.23 us -> 5.46 us
  local copies, waits for them, and re-layouts: 6.07 us -> 4.37 us
    all_to_all x1, blocking collectives: 38.7 us -> 10.2 us  [on_device(): lax.all_to_all(stats, AXES, 0, 0, axis_index_groups=members, tiled=True)]
    ppermute x9 -> x23, waiting for transfers between devices: 16 us -> 35 us  [the longest x14 31.6 us: send(): return lax.ppermute(value, AXES, ring_perm(steps, pair))]
    ppermute x9 -> x23, starting transfers between devices: 15.7 us -> 31.2 us  [the longest x14 19.9 us: send(): return lax.ppermute(value, AXES, ring_perm(steps, pair))]
    all_to_all x1 -> x0, starting transfers between devices: 4.89 us -> none  [spread(): lax.all_to_all(everywhere, AXES, 0, 0, axis_index_groups=members, tiled=T...]
    all_to_all x1 -> x0, waiting for transfers between devices: 4.8 us -> none  [spread(): lax.all_to_all(everywhere, AXES, 0, 0, axis_index_groups=members, tiled=T...]
    pallas_call x4 -> x5, Pallas kernels: 52.1 us -> 55 us  [the longest x2 26.9 us: grad_call(): pl.pallas_call(functools.partial(grad_kernel, pairs, pieces), grid=(count...]
    unnamed x6 -> x20, local copies, waits for them, and re-layouts: 0.6 us -> 2.64 us
    broadcast_in_dim x4 -> x0, local copies, waits for them, and re-layouts: 1.84 us -> none  [the longest x2 1.83 us: spread(): everywhere = jnp.broadcast_to(value[None], (8,) + value.shape)]
  transfers between devices with their start and end apart: 12 -> 25, of which waited for: 8 -> 12; matrix products, arithmetic and copies ran while one was open for 2% -> 1% of each run, Pallas kernels for 15% -> 20%
where the time goes in v1:
time: 154 us; the launch traced here: 153 us
  Pallas kernels  55 us (36%)
  waiting for transfers between devices  38 us (25%)
  starting transfers between devices  36.7 us (24%)
  blocking collectives  10.2 us (7%)
  other arithmetic  5.46 us (4%)
  local copies, waits for them, and re-layouts  4.37 us (3%)
  between operations  3.35 us (2%)
    ppermute x14, waiting for transfers between devices, send(): return lax.ppermute(value, AXES, ring_perm(steps, pair))  31.6 us
    pallas_call x2, Pallas kernels, grad_call(): pl.pallas_call(functools.partial(grad_kernel, pairs, pieces), grid=(count...  26.9 us
    ppermute x14, starting transfers between devices, send(): return lax.ppermute(value, AXES, ring_perm(steps, pair))  19.9 us
    pallas_call x1, Pallas kernels, score_call(): pl.pallas_call(functools.partial(score_kernel, n), grid=(n,), in_specs=[s...  17.3 us
    all_to_all x1, blocking collectives, on_device(): lax.all_to_all(stats, AXES, 0, 0, axis_index_groups=members, tiled=True)  10.2 us
    pallas_call x1, Pallas kernels, last_score_call(): pl.pallas_call(functools.partial(last_score_kernel, n), in_specs=[smem, s...  9.19 us
    ppermute x7, starting transfers between devices, on_device(): other = [swap(v) for v in own]  6.13 us
    ppermute x1, starting transfers between devices, on_device(): other_lse = swap(own_lse)  5.03 us
  transfers between devices with their start and end apart: 25, of which 12 were waited for; matrix products, arithmetic and copies ran while one was open for 1% of the time, Pallas kernels for 20%

profile of v1, /device:TPU:1, one launch (start us, length us, event | category | flops | bytes accessed | tf_op | source)
XLA Modules:
  0.0 153.1 jit_solution(10265373027367261928)
XLA Ops:
  1.7 1.5 collective-permute-start
  3.2 1.3 collective-permute-done
  5.5 1.4 collective-permute-start.3
  6.9 3.8 %collective-permute-start.1 = (bf16[256,1280]{1,0:T(8,128)(2,1)S(1)}, bf16[256,1280]{1,0:T(8,128)(2,1)}, u32[]{:S(2)}, u32[]{:S(2)}) collective-permute-start(bf16[256,1280]{1,0:T(8,128)(2,1)S(1)} %pad_maximum_fusion.1.refs_0_), channel_id=1, source_target_pairs={{0,3},{32,56},{8,11},{40,32},{16,19},{48,40},{24,27},{56,48},{1,0}... | collective-permute-start | bytes 1966088 | tf_op jit(solution)/shard_map/ppermute | solution.py:446
  10.7 1.2 collective-permute-start.7
  11.8 1.6 %collective-permute-start.2 = (bf16[256,1280]{1,0:T(8,128)(2,1)S(1)}, bf16[256,1280]{1,0:T(8,128)(2,1)}, u32[]{:S(2)}, u32[]{:S(2)}) collective-permute-start(bf16[256,1280]{1,0:T(8,128)(2,1)S(1)} %pad_maximum_fusion.1.refs_0_), channel_id=1, source_target_pairs={{0,1},{32,40},{8,9},{40,48},{16,17},{48,56},{24,25},{56,32},{1,2},... | collective-permute-start | bytes 1966088 | tf_op jit(solution)/shard_map/ppermute | solution.py:446
  13.5 2.0 %collective-permute-done.3.refs_3_ = bf16[256,1280]{1,0:T(8,128)(2,1)S(1)} collective-permute-done((bf16[256,1280]{1,0:T(8,128)(2,1)S(1)}, bf16[256,1280]{1,0:T(8,128)(2,1)S(1)}, u32[]{:S(2)}, u32[]{:S(2)}) %collective-permute-start.3) | collective-permute-done | bytes 655392 | tf_op jit(solution)/shard_map/ppermute | solution.py:446
  15.4 2.3 %collective-permute-start.10 = (bf16[256,1280]{1,0:T(8,128)(2,1)S(1)}, bf16[256,1280]{1,0:T(8,128)(2,1)S(1)}, u32[]{:S(2)}, u32[]{:S(2)}) collective-permute-start(bf16[256,1280]{1,0:T(8,128)(2,1)S(1)} %collective-permute-done.3.refs_3_), channel_id=1, source_target_pairs={{0,32},{32,0},{8,40},{40,8},{16,48},{48,16},{24,56},{56,24},{1,33}... | collective-permute-start | bytes 1966088 | tf_op jit(solution)/shard_map/ppermute | solution.py:457
  17.8 1.7 %collective-permute-start.5 = (bf16[256,1280]{1,0:T(8,128)(2,1)S(1)}, bf16[256,1280]{1,0:T(8,128)(2,1)}, u32[]{:S(2)}, u32[]{:S(2)}) collective-permute-start(bf16[256,1280]{1,0:T(8,128)(2,1)S(1)} %collective-permute-done.3.refs_3_), channel_id=1, source_target_pairs={{0,1},{32,40},{8,9},{40,48},{16,17},{48,56},{24,25},{56,32},{1,2},... | collective-permute-start | bytes 1966088 | tf_op jit(solution)/shard_map/ppermute | solution.py:446
  19.5 2.4 %collective-permute-start.4 = (bf16[256,1280]{1,0:T(8,128)(2,1)}, bf16[256,1280]{1,0:T(8,128)(2,1)}, u32[]{:S(2)}, u32[]{:S(2)}) collective-permute-start(bf16[256,1280]{1,0:T(8,128)(2,1)} %collective-permute-done.1.refs_1_), channel_id=1, source_target_pairs={{0,3},{32,56},{8,11},{40,32},{16,19},{48,40},{24,27},{56,48},{1,0}... | collective-permute-start | bytes 1966088 | tf_op jit(solution)/shard_map/ppermute | solution.py:446
  22.0 2.0 %collective-permute-done.2.refs_2_ = bf16[256,1280]{1,0:T(8,128)(2,1)} collective-permute-done((bf16[256,1280]{1,0:T(8,128)(2,1)S(1)}, bf16[256,1280]{1,0:T(8,128)(2,1)}, u32[]{:S(2)}, u32[]{:S(2)}) %collective-permute-start.2) | collective-permute-done | bytes 655392 | tf_op jit(solution)/shard_map/ppermute | solution.py:446
  24.5 6.5 %collective-permute-done.5.refs_5_ = bf16[256,1280]{1,0:T(8,128)(2,1)} collective-permute-done((bf16[256,1280]{1,0:T(8,128)(2,1)S(1)}, bf16[256,1280]{1,0:T(8,128)(2,1)}, u32[]{:S(2)}, u32[]{:S(2)}) %collective-permute-start.5) | collective-permute-done | bytes 655392 | tf_op jit(solution)/shard_map/ppermute | solution.py:446
  33.8 1.2 dynamic-slice_bitcast_fusion.table_ref
  35.0 3.8 %collective-permute-start.14 = (bf16[256,1280]{1,0:T(8,128)(2,1)}, bf16[256,1280]{1,0:T(8,128)(2,1)}, u32[]{:S(2)}, u32[]{:S(2)}) collective-permute-start(bf16[256,1280]{1,0:T(8,128)(2,1)} %collective-permute-done.6.refs_6_), channel_id=1, source_target_pairs={{0,3},{32,56},{8,11},{40,32},{16,19},{48,40},{24,27},{56,48},{1,0}... | collective-permute-start | bytes 1966088 | tf_op jit(solution)/shard_map/ppermute | solution.py:446
  39.8 17.3 %scores.1 = (f32[2048,2048]{1,0:T(8,128)}, f32[4,1792]{1,0:T(4,128)}) custom-call(s32[32]{0:T(128)} %dynamic-slice_bitcast_fusion.table_ref, f32[1]{0:T(128)} %bitcast.2.scale_ref, bf16[256,1280]{1,0:T(8,128)(2,1)} %copy-done.6, bf16[256,1280]{1,0:T(8,128)(2,1)} %collective-permute-done.1.refs_1_, bf16[256,1280]{1,0:T(8,128)(2,1)} %collective-permute-done.2.refs_2_, ...), custom_call_target="tpu_custom_call" | custom-call | flops 8220835840 | bytes 12845056 | tf_op jit(solution)/shard_map/scores/pallas_call | solution.py:175
  57.2 2.3 %collective-permute-done.15.refs_15_.refs_7_ = bf16[256,1280]{1,0:T(8,128)(2,1)S(1)} collective-permute-done((bf16[256,1280]{1,0:T(8,128)(2,1)}, bf16[256,1280]{1,0:T(8,128)(2,1)S(1)}, u32[]{:S(2)}, u32[]{:S(2)}) %collective-permute-start.15) | collective-permute-done | bytes 655392 | tf_op jit(solution)/shard_map/ppermute | solution.py:460
  60.3 9.2 %last_scores.1 = (f32[2048,2048]{1,0:T(8,128)}, f32[8,4,2048]{2,1,0:T(4,128)}) custom-call(s32[32]{0:T(128)} %dynamic-slice_bitcast_fusion.table_ref, f32[1]{0:T(128)} %bitcast.2.scale_ref, f32[4,1792]{1,0:T(4,128)} %get-tuple-element.26.before_ref, f32[2048,2048]{1,0:T(8,128)} %get-tuple-element.27.scores_in, ...), custom_call_target="tpu_custom_call", output_to_operand_aliasing={{0}: (3, {})} | custom-call | flops 2516582400 | bytes 3932160 | tf_op jit(solution)/shard_map/last_scores/pallas_call | solution.py:270
  69.5 10.2 %all_to_all.5.stats_ref = f32[8,4,2048]{2,1,0:T(4,128)} all-to-all(f32[8,4,2048]{2,1,0:T(4,128)} %get-tuple-element.29), channel_id=1, replica_groups={{0,1,2,3,68,69,70,71},{4,5,6,7,64,65,66,67},{8,9,10,11,76,77,78,79},{12..., dimensions={0} | all-to-all | bytes 524288 | tf_op jit(solution)/shard_map/all_to_all | solution.py:463
  79.7 1.7 %join.1.own_lse_ref = f32[1,2304]{1,0:T(1,128)} custom-call(f32[8,4,2048]{2,1,0:T(4,128)} %all_to_all.5.stats_ref), custom_call_target="tpu_custom_call" | custom-call | tf_op jit(solution)/shard_map/join/pallas_call | solution.py:316
  81.4 5.0 %collective-permute-start.16 = (f32[1,2304]{1,0:T(1,128)}, f32[1,2304]{1,0:T(1,128)S(1)}, u32[]{:S(2)}, u32[]{:S(2)}) collective-permute-start(f32[1,2304]{1,0:T(1,128)} %join.1.own_lse_ref), channel_id=1, source_target_pairs={{0,32},{32,0},{8,40},{40,8},{16,48},{48,16},{24,56},{56,24},{1,33}... | collective-permute-start | bytes 27656 | tf_op jit(solution)/shard_map/ppermute | solution.py:465
  88.0 13.4 %grads_far.1 = (bf16[272,1280]{1,0:T(8,128)(2,1)}, bf16[272,1280]{1,0:T(8,128)(2,1)}, bf16[272,1280]{1,0:T(8,128)(2,1)}, bf16[272,1280]{1,0:T(8,128)(2,1)}) custom-call(s32[32]{0:T(128)} %dynamic-slice_bitcast_fusion.table_ref, f32[1]{0:T(128)} %bitcast.7.scale_ref, f32[1,2304]{1,0:T(1,128)} %join.1.own_lse_ref, f32[1,2304]{1,0:T(1,128)} %copy-done.9, ...), custom_call_target="tpu_custom_call" | custom-call | flops 5368709120 | bytes 8388608 | tf_op jit(solution)/shard_map/grads_far/pallas_call | solution.py:404
  101.5 1.9 %collective-permute-start.18 = (bf16[272,1280]{1,0:T(8,128)(2,1)}, bf16[272,1280]{1,0:T(8,128)(2,1)S(1)}, u32[]{:S(2)}, u32[]{:S(2)}) collective-permute-start(bf16[272,1280]{1,0:T(8,128)(2,1)} %get-tuple-element.32), channel_id=1, source_target_pairs={{0,69},{32,104},{8,77},{40,112},{16,85},{48,120},{24,93},{56,96},{... | collective-permute-start | bytes 2088968 | tf_op jit(solution)/shard_map/ppermute | solution.py:446
  103.4 1.8 %collective-permute-start.19 = (bf16[272,1280]{1,0:T(8,128)(2,1)}, bf16[272,1280]{1,0:T(8,128)(2,1)S(1)}, u32[]{:S(2)}, u32[]{:S(2)}) collective-permute-start(bf16[272,1280]{1,0:T(8,128)(2,1)} %get-tuple-element.33), channel_id=1, source_target_pairs={{0,71},{32,120},{8,79},{40,96},{16,87},{48,104},{24,95},{56,112},{... | collective-permute-start | bytes 2088968 | tf_op jit(solution)/shard_map/ppermute | solution.py:446
  105.2 13.5 %grads_near.1 = (bf16[272,1280]{1,0:T(8,128)(2,1)}, bf16[272,1280]{1,0:T(8,128)(2,1)}, bf16[272,1280]{1,0:T(8,128)(2,1)}, f32[256,1280]{1,0:T(8,128)}) custom-call(s32[32]{0:T(128)} %dynamic-slice_bitcast_fusion.table_ref, f32[1]{0:T(128)} %bitcast.8.scale_ref, f32[1,2304]{1,0:T(1,128)} %join.1.own_lse_ref, f32[1,2304]{1,0:T(1,128)} %copy-done.9, ...), custom_call_target="tpu_custom_call" | custom-call | flops 5368709120 | bytes 8388608 | tf_op jit(solution)/shard_map/grads_near/pallas_call | solution.py:404
  118.7 3.1 %collective-permute-done.18 = bf16[272,1280]{1,0:T(8,128)(2,1)S(1)} collective-permute-done((bf16[272,1280]{1,0:T(8,128)(2,1)}, bf16[272,1280]{1,0:T(8,128)(2,1)S(1)}, u32[]{:S(2)}, u32[]{:S(2)}) %collective-permute-start.18) | collective-permute-done | bytes 696352 | tf_op jit(solution)/shard_map/ppermute | solution.py:446
  121.8 6.1 %collective-permute-done.19 = bf16[272,1280]{1,0:T(8,128)(2,1)S(1)} collective-permute-done((bf16[272,1280]{1,0:T(8,128)(2,1)}, bf16[272,1280]{1,0:T(8,128)(2,1)S(1)}, u32[]{:S(2)}, u32[]{:S(2)}) %collective-permute-start.19) | collective-permute-done | bytes 696352 | tf_op jit(solution)/shard_map/ppermute | solution.py:446
  127.8 2.6 %collective-permute-done.20 = bf16[272,1280]{1,0:T(8,128)(2,1)S(1)} collective-permute-done((bf16[272,1280]{1,0:T(8,128)(2,1)}, bf16[272,1280]{1,0:T(8,128)(2,1)S(1)}, u32[]{:S(2)}, u32[]{:S(2)}) %collective-permute-start.20) | collective-permute-done | bytes 696352 | tf_op jit(solution)/shard_map/ppermute | solution.py:446
  130.4 1.5 collective-permute-start.23
  132.3 8.5 %collective-permute-done.21 = bf16[272,1280]{1,0:T(8,128)(2,1)S(1)} collective-permute-done((bf16[272,1280]{1,0:T(8,128)(2,1)}, bf16[272,1280]{1,0:T(8,128)(2,1)S(1)}, u32[]{:S(2)}, u32[]{:S(2)}) %collective-permute-start.21) | collective-permute-done | bytes 696352 | tf_op jit(solution)/shard_map/ppermute | solution.py:446
  143.8 4.0 %collective-permute-start.24 = (f32[136,1280]{1,0:T(8,128)S(1)}, f32[136,1280]{1,0:T(8,128)S(1)}, u32[]{:S(2)}, u32[]{:S(2)}) collective-permute-start(f32[136,1280]{1,0:T(8,128)S(1)} %pad_maximum_fusion), channel_id=1, source_target_pairs={{0,32},{32,0},{8,40},{40,8},{16,48},{48,16},{24,56},{56,24},{1,33}... | collective-permute-start | bytes 2088968 | tf_op jit(solution)/shard_map/ppermute | solution.py:480
  147.8 1.8 %collective-permute-done.24 = f32[136,1280]{1,0:T(8,128)S(1)} collective-permute-done((f32[136,1280]{1,0:T(8,128)S(1)}, f32[136,1280]{1,0:T(8,128)S(1)}, u32[]{:S(2)}, u32[]{:S(2)}) %collective-permute-start.24) | collective-permute-done | bytes 696352 | tf_op jit(solution)/shard_map/ppermute | solution.py:480
  150.8 1.2 slice_select_fusion
  (69 shorter events, 12.3 us)
Async XLA Ops:
  1.7 2.8 %collective-permute-start = (bf16[128,1280]{1,0:T(8,128)(2,1)S(1)}, bf16[128,1280]{1,0:T(8,128)(2,1)S(1)}, u32[]{:S(2)}, u32[]{:S(2)}) collective-permute-start(bf16[128,1280]{1,0:T(8,128)(2,1)S(1)} %broadcast_select_fusion.2), channel_id=1, source_target_pairs={{0,32},{32,0},{8,40},{40,8},{16,48},{48,16},{24,56},{56,24},{1,33}... | collective-permute-start | bytes 983048 | tf_op jit(solution)/shard_map/ppermute | solution.py:448
  5.5 19.0 %copy-start.6 = (bf16[256,1280]{1,0:T(8,128)(2,1)}, bf16[256,1280]{1,0:T(8,128)(2,1)S(1)}, u32[]{:S(2)}) copy-start(bf16[256,1280]{1,0:T(8,128)(2,1)S(1)} %pad_maximum_fusion.1.refs_0_) | copy-start | bytes 1966084
  5.5 9.9 %collective-permute-start.3 = (bf16[256,1280]{1,0:T(8,128)(2,1)S(1)}, bf16[256,1280]{1,0:T(8,128)(2,1)S(1)}, u32[]{:S(2)}, u32[]{:S(2)}) collective-permute-start(bf16[256,1280]{1,0:T(8,128)(2,1)S(1)} %pad_maximum_fusion.1.refs_0_), channel_id=1, source_target_pairs={{0,68},{32,96},{8,76},{40,104},{16,84},{48,112},{24,92},{56,120},{... | collective-permute-start | bytes 1966088 | tf_op jit(solution)/shard_map/ppermute | solution.py:446
  6.9 12.6 %collective-permute-start.1 = (bf16[256,1280]{1,0:T(8,128)(2,1)S(1)}, bf16[256,1280]{1,0:T(8,128)(2,1)}, u32[]{:S(2)}, u32[]{:S(2)}) collective-permute-start(bf16[256,1280]{1,0:T(8,128)(2,1)S(1)} %pad_maximum_fusion.1.refs_0_), channel_id=1, source_target_pairs={{0,3},{32,56},{8,11},{40,32},{16,19},{48,40},{24,27},{56,48},{1,0}... | collective-permute-start | bytes 1966088 | tf_op jit(solution)/shard_map/ppermute | solution.py:446
  10.7 8.9 %collective-permute-start.7 = (bf16[256,1280]{1,0:T(8,128)(2,1)S(1)}, bf16[256,1280]{1,0:T(8,128)(2,1)S(1)}, u32[]{:S(2)}, u32[]{:S(2)}) collective-permute-start(bf16[256,1280]{1,0:T(8,128)(2,1)S(1)} %pad_maximum_fusion.1.refs_0_), channel_id=1, source_target_pairs={{0,32},{32,0},{8,40},{40,8},{16,48},{48,16},{24,56},{56,24},{1,33}... | collective-permute-start | bytes 1966088 | tf_op jit(solution)/shard_map/ppermute | solution.py:457
  11.8 12.1 %collective-permute-start.2 = (bf16[256,1280]{1,0:T(8,128)(2,1)S(1)}, bf16[256,1280]{1,0:T(8,128)(2,1)}, u32[]{:S(2)}, u32[]{:S(2)}) collective-permute-start(bf16[256,1280]{1,0:T(8,128)(2,1)S(1)} %pad_maximum_fusion.1.refs_0_), channel_id=1, source_target_pairs={{0,1},{32,40},{8,9},{40,48},{16,17},{48,56},{24,25},{56,32},{1,2},... | collective-permute-start | bytes 1966088 | tf_op jit(solution)/shard_map/ppermute | solution.py:446
  15.4 15.6 %copy-start.8 = (bf16[256,1280]{1,0:T(8,128)(2,1)}, bf16[256,1280]{1,0:T(8,128)(2,1)S(1)}, u32[]{:S(2)}) copy-start(bf16[256,1280]{1,0:T(8,128)(2,1)S(1)} %collective-permute-done.3.refs_3_) | copy-start | bytes 1966084
  15.4 8.8 %collective-permute-start.10 = (bf16[256,1280]{1,0:T(8,128)(2,1)S(1)}, bf16[256,1280]{1,0:T(8,128)(2,1)S(1)}, u32[]{:S(2)}, u32[]{:S(2)}) collective-permute-start(bf16[256,1280]{1,0:T(8,128)(2,1)S(1)} %collective-permute-done.3.refs_3_), channel_id=1, source_target_pairs={{0,32},{32,0},{8,40},{40,8},{16,48},{48,16},{24,56},{56,24},{1,33}... | collective-permute-start | bytes 1966088 | tf_op jit(solution)/shard_map/ppermute | solution.py:457
  17.8 13.2 %collective-permute-start.5 = (bf16[256,1280]{1,0:T(8,128)(2,1)S(1)}, bf16[256,1280]{1,0:T(8,128)(2,1)}, u32[]{:S(2)}, u32[]{:S(2)}) collective-permute-start(bf16[256,1280]{1,0:T(8,128)(2,1)S(1)} %collective-permute-done.3.refs_3_), channel_id=1, source_target_pairs={{0,1},{32,40},{8,9},{40,48},{16,17},{48,56},{24,25},{56,32},{1,2},... | collective-permute-start | bytes 1966088 | tf_op jit(solution)/shard_map/ppermute | solution.py:446
  19.5 11.5 %collective-permute-start.6 = (bf16[256,1280]{1,0:T(8,128)(2,1)}, bf16[256,1280]{1,0:T(8,128)(2,1)}, u32[]{:S(2)}, u32[]{:S(2)}) collective-permute-start(bf16[256,1280]{1,0:T(8,128)(2,1)} %collective-permute-done.1.refs_1_), channel_id=1, source_target_pairs={{0,68},{32,96},{8,76},{40,104},{16,84},{48,112},{24,92},{56,120},{... | collective-permute-start | bytes 1966088 | tf_op jit(solution)/shard_map/ppermute | solution.py:446
  19.5 19.3 %copy-start = (bf16[256,1280]{1,0:T(8,128)(2,1)}, bf16[256,1280]{1,0:T(8,128)(2,1)S(1)}, u32[]{:S(2)}) copy-start(bf16[256,1280]{1,0:T(8,128)(2,1)S(1)} %collective-permute-done.7.refs_7_.refs_8_.refs_0_) | copy-start | bytes 1966084
  19.5 12.5 %collective-permute-start.4 = (bf16[256,1280]{1,0:T(8,128)(2,1)}, bf16[256,1280]{1,0:T(8,128)(2,1)}, u32[]{:S(2)}, u32[]{:S(2)}) collective-permute-start(bf16[256,1280]{1,0:T(8,128)(2,1)} %collective-permute-done.1.refs_1_), channel_id=1, source_target_pairs={{0,3},{32,56},{8,11},{40,32},{16,19},{48,40},{24,27},{56,48},{1,0}... | collective-permute-start | bytes 1966088 | tf_op jit(solution)/shard_map/ppermute | solution.py:446
  24.0 14.8 %collective-permute-start.8 = (bf16[256,1280]{1,0:T(8,128)(2,1)}, bf16[256,1280]{1,0:T(8,128)(2,1)S(1)}, u32[]{:S(2)}, u32[]{:S(2)}) collective-permute-start(bf16[256,1280]{1,0:T(8,128)(2,1)} %collective-permute-done.1.refs_1_), channel_id=1, source_target_pairs={{0,32},{32,0},{8,40},{40,8},{16,48},{48,16},{24,56},{56,24},{1,33}... | collective-permute-start | bytes 1966088 | tf_op jit(solution)/shard_map/ppermute | solution.py:457
  24.2 14.6 %copy-start.1 = (bf16[256,1280]{1,0:T(8,128)(2,1)}, bf16[256,1280]{1,0:T(8,128)(2,1)S(1)}, u32[]{:S(2)}) copy-start(bf16[256,1280]{1,0:T(8,128)(2,1)S(1)} %collective-permute-done.10.refs_10_.refs_11_.refs_3_) | copy-start | bytes 1966084
  24.2 10.7 %collective-permute-start.9 = (bf16[256,1280]{1,0:T(8,128)(2,1)}, bf16[256,1280]{1,0:T(8,128)(2,1)S(1)}, u32[]{:S(2)}, u32[]{:S(2)}) collective-permute-start(bf16[256,1280]{1,0:T(8,128)(2,1)} %collective-permute-done.2.refs_2_), channel_id=1, source_target_pairs={{0,32},{32,0},{8,40},{40,8},{16,48},{48,16},{24,56},{56,24},{1,33}... | collective-permute-start | bytes 1966088 | tf_op jit(solution)/shard_map/ppermute | solution.py:457
  31.0 7.8 %collective-permute-start.12 = (bf16[256,1280]{1,0:T(8,128)(2,1)}, bf16[256,1280]{1,0:T(8,128)(2,1)S(1)}, u32[]{:S(2)}, u32[]{:S(2)}) collective-permute-start(bf16[256,1280]{1,0:T(8,128)(2,1)} %collective-permute-done.5.refs_5_), channel_id=1, source_target_pairs={{0,32},{32,0},{8,40},{40,8},{16,48},{48,16},{24,56},{56,24},{1,33}... | collective-permute-start | bytes 1966088 | tf_op jit(solution)/shard_map/ppermute | solution.py:457
  31.0 7.8 %collective-permute-start.13 = (bf16[256,1280]{1,0:T(8,128)(2,1)}, bf16[256,1280]{1,0:T(8,128)(2,1)}, u32[]{:S(2)}, u32[]{:S(2)}) collective-permute-start(bf16[256,1280]{1,0:T(8,128)(2,1)} %collective-permute-done.6.refs_6_), channel_id=1, source_target_pairs={{0,32},{32,0},{8,40},{40,8},{16,48},{48,16},{24,56},{56,24},{1,33}... | collective-permute-start | bytes 1966088 | tf_op jit(solution)/shard_map/ppermute | solution.py:457
  32.1 6.7 %collective-permute-start.11 = (bf16[256,1280]{1,0:T(8,128)(2,1)}, bf16[256,1280]{1,0:T(8,128)(2,1)}, u32[]{:S(2)}, u32[]{:S(2)}) collective-permute-start(bf16[256,1280]{1,0:T(8,128)(2,1)} %collective-permute-done.4.refs_4_), channel_id=1, source_target_pairs={{0,32},{32,0},{8,40},{40,8},{16,48},{48,16},{24,56},{56,24},{1,33}... | collective-permute-start | bytes 1966088 | tf_op jit(solution)/shard_map/ppermute | solution.py:457
  35.0 3.8 %copy-start.3 = (bf16[256,1280]{1,0:T(8,128)(2,1)}, bf16[256,1280]{1,0:T(8,128)(2,1)S(1)}, u32[]{:S(2)}) copy-start(bf16[256,1280]{1,0:T(8,128)(2,1)S(1)} %collective-permute-done.9.refs_9_.refs_10_.refs_2_) | copy-start | bytes 1966084
  35.0 22.1 %collective-permute-start.14 = (bf16[256,1280]{1,0:T(8,128)(2,1)}, bf16[256,1280]{1,0:T(8,128)(2,1)}, u32[]{:S(2)}, u32[]{:S(2)}) collective-permute-start(bf16[256,1280]{1,0:T(8,128)(2,1)} %collective-permute-done.6.refs_6_), channel_id=1, source_target_pairs={{0,3},{32,56},{8,11},{40,32},{16,19},{48,40},{24,27},{56,48},{1,0}... | collective-permute-start | bytes 1966088 | tf_op jit(solution)/shard_map/ppermute | solution.py:446
  38.7 1.1 copy-start.4
  57.1 2.4 %collective-permute-start.15 = (bf16[256,1280]{1,0:T(8,128)(2,1)}, bf16[256,1280]{1,0:T(8,128)(2,1)S(1)}, u32[]{:S(2)}, u32[]{:S(2)}) collective-permute-start(bf16[256,1280]{1,0:T(8,128)(2,1)} %collective-permute-done.14.refs_7_), channel_id=1, source_target_pairs={{0,32},{32,0},{8,40},{40,8},{16,48},{48,16},{24,56},{56,24},{1,33}... | collective-permute-start | bytes 1966088 | tf_op jit(solution)/shard_map/ppermute | solution.py:460
  81.4 6.1 %collective-permute-start.16 = (f32[1,2304]{1,0:T(1,128)}, f32[1,2304]{1,0:T(1,128)S(1)}, u32[]{:S(2)}, u32[]{:S(2)}) collective-permute-start(f32[1,2304]{1,0:T(1,128)} %join.1.own_lse_ref), channel_id=1, source_target_pairs={{0,32},{32,0},{8,40},{40,8},{16,48},{48,16},{24,56},{56,24},{1,33}... | collective-permute-start | bytes 27656 | tf_op jit(solution)/shard_map/ppermute | solution.py:465
  101.4 17.3 %collective-permute-start.17 = (bf16[272,1280]{1,0:T(8,128)(2,1)}, bf16[272,1280]{1,0:T(8,128)(2,1)S(1)}, u32[]{:S(2)}, u32[]{:S(2)}) collective-permute-start(bf16[272,1280]{1,0:T(8,128)(2,1)} %get-tuple-element.31), channel_id=1, source_target_pairs={{0,70},{32,112},{8,78},{40,120},{16,86},{48,96},{24,94},{56,104},{... | collective-permute-start | bytes 2088968 | tf_op jit(solution)/shard_map/ppermute | solution.py:446
  101.5 20.3 %collective-permute-start.18 = (bf16[272,1280]{1,0:T(8,128)(2,1)}, bf16[272,1280]{1,0:T(8,128)(2,1)S(1)}, u32[]{:S(2)}, u32[]{:S(2)}) collective-permute-start(bf16[272,1280]{1,0:T(8,128)(2,1)} %get-tuple-element.32), channel_id=1, source_target_pairs={{0,69},{32,104},{8,77},{40,112},{16,85},{48,120},{24,93},{56,96},{... | collective-permute-start | bytes 2088968 | tf_op jit(solution)/shard_map/ppermute | solution.py:446
  103.4 24.4 %collective-permute-start.19 = (bf16[272,1280]{1,0:T(8,128)(2,1)}, bf16[272,1280]{1,0:T(8,128)(2,1)S(1)}, u32[]{:S(2)}, u32[]{:S(2)}) collective-permute-start(bf16[272,1280]{1,0:T(8,128)(2,1)} %get-tuple-element.33), channel_id=1, source_target_pairs={{0,71},{32,120},{8,79},{40,96},{16,87},{48,104},{24,95},{56,112},{... | collective-permute-start | bytes 2088968 | tf_op jit(solution)/shard_map/ppermute | solution.py:446
  105.2 25.2 %collective-permute-start.20 = (bf16[272,1280]{1,0:T(8,128)(2,1)}, bf16[272,1280]{1,0:T(8,128)(2,1)S(1)}, u32[]{:S(2)}, u32[]{:S(2)}) collective-permute-start(bf16[272,1280]{1,0:T(8,128)(2,1)} %get-tuple-element.34), channel_id=1, source_target_pairs={{0,2},{32,48},{8,10},{40,56},{16,18},{48,32},{24,26},{56,40},{1,3}... | collective-permute-start | bytes 2088968 | tf_op jit(solution)/shard_map/ppermute | solution.py:446
  130.4 10.4 %collective-permute-start.21 = (bf16[272,1280]{1,0:T(8,128)(2,1)}, bf16[272,1280]{1,0:T(8,128)(2,1)S(1)}, u32[]{:S(2)}, u32[]{:S(2)}) collective-permute-start(bf16[272,1280]{1,0:T(8,128)(2,1)} %get-tuple-element.42), channel_id=1, source_target_pairs={{0,68},{32,96},{8,76},{40,104},{16,84},{48,112},{24,92},{56,120},{... | collective-permute-start | bytes 2088968 | tf_op jit(solution)/shard_map/ppermute | solution.py:446
  130.4 10.5 %collective-permute-start.22 = (bf16[272,1280]{1,0:T(8,128)(2,1)}, bf16[272,1280]{1,0:T(8,128)(2,1)S(1)}, u32[]{:S(2)}, u32[]{:S(2)}) collective-permute-start(bf16[272,1280]{1,0:T(8,128)(2,1)} %get-tuple-element.43), channel_id=1, source_target_pairs={{0,3},{32,56},{8,11},{40,32},{16,19},{48,40},{24,27},{56,48},{1,0}... | collective-permute-start | bytes 2088968 | tf_op jit(solution)/shard_map/ppermute | solution.py:446
  130.4 11.6 %collective-permute-start.23 = (bf16[272,1280]{1,0:T(8,128)(2,1)}, bf16[272,1280]{1,0:T(8,128)(2,1)S(1)}, u32[]{:S(2)}, u32[]{:S(2)}) collective-permute-start(bf16[272,1280]{1,0:T(8,128)(2,1)} %get-tuple-element.44), channel_id=1, source_target_pairs={{0,1},{32,40},{8,9},{40,48},{16,17},{48,56},{24,25},{56,32},{1,2},... | collective-permute-start | bytes 2088968 | tf_op jit(solution)/shard_map/ppermute | solution.py:446
  141.0 1.3 copy-start.7
  143.8 5.8 %collective-permute-start.24 = (f32[136,1280]{1,0:T(8,128)S(1)}, f32[136,1280]{1,0:T(8,128)S(1)}, u32[]{:S(2)}, u32[]{:S(2)}) collective-permute-start(f32[136,1280]{1,0:T(8,128)S(1)} %pad_maximum_fusion), channel_id=1, source_target_pairs={{0,32},{32,0},{8,40},{40,8},{16,48},{48,16},{24,56},{56,24},{1,33}... | collective-permute-start | bytes 2088968 | tf_op jit(solution)/shard_map/ppermute | solution.py:480
  (3 other events, 2.3 us)

commit v2 on v1

--- a/solution.py
+++ b/solution.py
@@ -13,7 +13,8 @@
 LN2 = 0.6931471805599453
 AXES = ("row", "col")
 ROWS = 256
-VMEM = 63_400_000
+VMEM = 24 * 1024 * 1024
+SPARE = 3328
 EXTRA = 16
 PAIR = 2
 
@@ -139,161 +140,128 @@
             line[3:4, span] = jnp.sum(jnp.where(eye(128), corner, 0.0), axis=0, keepdims=True)
 
 
-def score_kernel(n, table_ref, scale_ref, *refs):
-    own_refs, other_refs = refs[:n], refs[n : 2 * n]
-    scores_ref, stats_ref, own, other, line, own_sems, other_sems = refs[2 * n :]
-    step = pl.program_id(0)
+def score_kernel(old, new, last, table_ref, scale_ref, *refs):
+    total = old + new
+    if old:
+        before_ref, refs = refs[0], refs[2:]
+    own_refs, other_refs = refs[:total], refs[total : 2 * total]
+    scores_out, stats_ref, own, other, row, column, line, own_sems, other_sems, out_sems = refs[2 * total :]
     load_own, load_other = fetch(own_refs, own, own_sems), fetch(other_refs, other, other_sems)
-
-    @pl.when(step == 0)
-    def _():
-        for copy in load_own[:1] + load_other + load_own[1:]:
-            copy.start()
-        for copy in load_own[:1] + load_other:
-            copy.wait()
-
-    @pl.when(step == 1)
-    def _():
-        for copy in load_own[1:]:
-            copy.wait()
-
-    rows = own[pl.ds(pl.multiple_of(step * ROWS, ROWS), ROWS), :]
-    width = n * ROWS
-    top, total, weighted = tile_stats(
-        scale_ref[0], rows, lambda at, chunk: other[at : at + chunk, :], width, scores_ref
-    )
-    line[0:1, :] = top
-    line[1:2, :] = total
-    line[2:3, :] = weighted
-    put_matched(table_ref, step, 0, width, scores_ref, line)
-    stats_ref[...] = line[...]
-
-
-def score_call(table, scale, own, other):
-    n, width = len(own), own[0].shape[1]
-    smem, anywhere = pl.BlockSpec(memory_space=pltpu.SMEM), pl.BlockSpec(memory_space=pl.ANY)
+    for copy in load_own[old:] + load_other + load_own[:old]:
+        copy.start()
+
+    def piece_rows(k):
+        return pl.ds(k * ROWS if isinstance(k, int) else pl.multiple_of(k * ROWS, ROWS), ROWS)
+
+    def store_old(k):
+        return pltpu.make_async_copy(
+            column.at[piece_rows(k)],
+            scores_out.at[piece_rows(k), pl.ds(old * ROWS, new * ROWS)],
+            out_sems.at[k],
+        )
+
+    def store_new(k):
+        return pltpu.make_async_copy(
+            row.at[piece_rows(k)],
+            scores_out.at[piece_rows(k + old), pl.ds(0, total * ROWS)],
+            out_sems.at[k + old],
+        )
+
+    def put(piece, top, power, weighted):
+        line[0:1, :] = top
+        line[1:2, :] = power
+        line[2:3, :] = weighted
+        if last:
+            for member in range(8):
+                stats_ref[member, :, pl.ds(table_place(table_ref, 0, piece), ROWS)] = line[...]
+        else:
+            stats_ref[:, piece_rows(piece)] = line[...]
+
+    def part(at, size):
+        if new == 1:
+            for k in range(at // ROWS, (at + size) // ROWS):
+                load_other[k].wait()
+        return other[at : at + size, :]
+
+    def new_piece(k):
+        target = row.at[piece_rows(k)]
+        top, power, weighted = tile_stats(scale_ref[0], own[piece_rows(k + old), :], part, total * ROWS, target)
+        store_new(k).start()
+        put_matched(table_ref, k + old, 0, total * ROWS, target, line)
+        put(k + old, top, power, weighted)
+
+    def old_scores(k):
+        stats = tile_stats(
+            scale_ref[0],
+            own[piece_rows(k), :],
+            lambda at, size: other[old * ROWS + at : old * ROWS + at + size, :],
+            new * ROWS,
+            column.at[piece_rows(k)],
+        )
+        store_old(k).start()
+        return stats
+
+    def old_stats(k, top, power, weighted):
+        put_matched(table_ref, k, old * ROWS, new * ROWS, column.at[piece_rows(k)], line)
+        earlier = before_ref[:, piece_rows(k)]
+        new_top = jnp.maximum(earlier[0:1], top)
+        old_shrink, new_shrink = jnp.exp2(earlier[0:1] - new_top), jnp.exp2(top - new_top)
+        line[3:4, :] = earlier[3:4] + line[3:4, :]
+        put(k, new_top, earlier[1:2] * old_shrink + power * new_shrink, earlier[2:3] * old_shrink + weighted * new_shrink)
+
+    for copy in load_own[old:] + (load_other if new > 1 else []):
+        copy.wait()
+    if new == 1:
+        new_piece(0)
+    else:
+        pl.loop(0, new)(new_piece)
+    for copy in load_own[:old]:
+        copy.wait()
+    if new == 1:
+        found = [old_scores(k) for k in range(old)]
+        for k, stats in enumerate(found):
+            old_stats(k, *stats)
+    elif old:
+        pl.loop(0, old)(lambda k: old_stats(k, *old_scores(k)))
+    for k in range(old):
+        store_old(k).wait()
+    for k in range(new):
+        store_new(k).wait()
+
+
+def score_call(name, last, table, scale, before, own, other):
+    total, width = len(own), own[0].shape[1]
+    old = before[0].shape[1] // ROWS if before else 0
+    new = total - old
+    smem, vmem, anywhere = (pl.BlockSpec(memory_space=s) for s in (pltpu.SMEM, pltpu.VMEM, pl.ANY))
+    tiles = new * total + old * new
     return pl.pallas_call(
-        functools.partial(score_kernel, n),
-        grid=(n,),
-        in_specs=[smem, smem] + [anywhere] * (2 * n),
-        out_specs=[
-            pl.BlockSpec((ROWS, n * ROWS), lambda i: (i, 0)),
-            pl.BlockSpec((4, ROWS), lambda i: (0, i)),
-        ],
+        functools.partial(score_kernel, old, new, last),
+        in_specs=[smem, smem] + ([vmem, anywhere] if before else []) + [anywhere] * (2 * total),
+        out_specs=[anywhere, vmem],
         out_shape=[
-            jax.ShapeDtypeStruct(((n + 1) * ROWS, (n + 1) * ROWS), jnp.float32),
-            jax.ShapeDtypeStruct((4, n * ROWS), jnp.float32),
+            jax.ShapeDtypeStruct((8 * ROWS + SPARE, 8 * ROWS), jnp.float32),
+            jax.ShapeDtypeStruct((8, 4, total * ROWS) if last else (4, total * ROWS), jnp.float32),
         ],
         scratch_shapes=[
-            pltpu.VMEM((n * ROWS, width), jnp.bfloat16),
-            pltpu.VMEM((n * ROWS, width), jnp.bfloat16),
+            pltpu.VMEM((total * ROWS, width), jnp.bfloat16),
+            pltpu.VMEM((total * ROWS, width), jnp.bfloat16),
+            pltpu.VMEM((new * ROWS, total * ROWS), jnp.float32),
+            pltpu.VMEM((max(old, 1) * ROWS, new * ROWS), jnp.float32),
             pltpu.VMEM((4, ROWS), jnp.float32),
-            pltpu.SemaphoreType.DMA((n,)),
-            pltpu.SemaphoreType.DMA((n,)),
+            pltpu.SemaphoreType.DMA((total,)),
+            pltpu.SemaphoreType.DMA((total,)),
+            pltpu.SemaphoreType.DMA((total,)),
         ],
+        input_output_aliases={3: 0} if before else {},
         compiler_params=pltpu.CompilerParams(vmem_limit_bytes=VMEM),
         cost_estimate=pl.CostEstimate(
-            flops=2 * n * n * ROWS * ROWS * width,
-            bytes_accessed=4 * n * n * ROWS * ROWS,
-            transcendentals=n * n * ROWS * ROWS,
+            flops=2 * tiles * ROWS * ROWS * width,
+            bytes_accessed=4 * tiles * ROWS * ROWS,
+            transcendentals=tiles * ROWS * ROWS,
         ),
-        name="scores",
-    )(table, scale, *own, *other)
-
-
-def last_score_kernel(n, table_ref, scale_ref, before_ref, scores_in, *refs):
-    own_refs, other_refs = refs[: n + 1], refs[n + 1 : 2 * n + 2]
-    scores_out, stats_ref, own, other, row, column, line, own_sems, other_sems, out_sems = refs[2 * n + 2 :]
-    load_own, load_other = fetch(own_refs, own, own_sems), fetch(other_refs, other, other_sems)
-    for copy in load_own[n:] + load_other + load_own[:n]:
-        copy.start()
-    store_row = pltpu.make_async_copy(row, scores_out.at[pl.ds(n * ROWS, ROWS)], out_sems.at[n])
-    store_column = [
-        pltpu.make_async_copy(
-            column.at[pl.ds(k * ROWS, ROWS)],
-            scores_out.at[pl.ds(k * ROWS, ROWS), pl.ds(n * ROWS, ROWS)],
-            out_sems.at[k],
-        )
-        for k in range(n)
-    ]
-
-    def put(piece):
-        for member in range(8):
-            stats_ref[member, :, pl.ds(table_place(table_ref, 0, piece), ROWS)] = line[...]
-
-    def arrived(at, size):
-        for k in range(at // ROWS, (at + size) // ROWS):
-            load_other[k].wait()
-        return other[at : at + size, :]
-
-    load_own[n].wait()
-    top, total, weighted = tile_stats(scale_ref[0], own[n * ROWS : (n + 1) * ROWS, :], arrived, (n + 1) * ROWS, row)
-    line[0:1, :] = top
-    line[1:2, :] = total
-    line[2:3, :] = weighted
-    put_matched(table_ref, n, 0, (n + 1) * ROWS, row, line)
-    store_row.start()
-    put(n)
-    for copy in load_own[:n]:
-        copy.wait()
-    found = []
-    for k in range(n):
-        found.append(
-            tile_stats(
-                scale_ref[0],
-                own[k * ROWS : (k + 1) * ROWS, :],
-                lambda at, chunk: other[n * ROWS + at : n * ROWS + at + chunk, :],
-                ROWS,
-                column.at[pl.ds(k * ROWS, ROWS)],
-            )
-        )
-    for k, (top, total, weighted) in enumerate(found):
-        store_column[k].start()
-        put_matched(table_ref, k, n * ROWS, ROWS, column.at[pl.ds(k * ROWS, ROWS)], line)
-        old = before_ref[:, k * ROWS : (k + 1) * ROWS]
-        new_top = jnp.maximum(old[0:1], top)
-        old_shrink, new_shrink = jnp.exp2(old[0:1] - new_top), jnp.exp2(top - new_top)
-        line[0:1, :] = new_top
-        line[1:2, :] = old[1:2] * old_shrink + total * new_shrink
-        line[2:3, :] = old[2:3] * old_shrink + weighted * new_shrink
-        line[3:4, :] = old[3:4] + line[3:4, :]
-        put(k)
-    store_row.wait()
-    for store in store_column:
-        store.wait()
-
-
-def last_score_call(table, scale, before, scores, own, other):
-    n, width = len(own) - 1, own[0].shape[1]
-    smem, vmem, anywhere = (pl.BlockSpec(memory_space=s) for s in (pltpu.SMEM, pltpu.VMEM, pl.ANY))
-    rows = (n + 1) * ROWS
-    return pl.pallas_call(
-        functools.partial(last_score_kernel, n),
-        in_specs=[smem, smem, vmem] + [anywhere] * (2 * n + 3),
-        out_specs=[anywhere, vmem],
-        out_shape=[
-            jax.ShapeDtypeStruct(scores.shape, jnp.float32),
-            jax.ShapeDtypeStruct((8, 4, rows), jnp.float32),
-        ],
-        scratch_shapes=[
-            pltpu.VMEM((rows, width), jnp.bfloat16),
-            pltpu.VMEM((rows, width), jnp.bfloat16),
-            pltpu.VMEM((ROWS, rows), jnp.float32),
-            pltpu.VMEM((n * ROWS, ROWS), jnp.float32),
-            pltpu.VMEM((4, ROWS), jnp.float32),
-            pltpu.SemaphoreType.DMA((n + 1,)),
-            pltpu.SemaphoreType.DMA((n + 1,)),
-            pltpu.SemaphoreType.DMA((n + 1,)),
-        ],
-        input_output_aliases={3: 0},
-        compiler_params=pltpu.CompilerParams(vmem_limit_bytes=VMEM),
-        cost_estimate=pl.CostEstimate(
-            flops=2 * (2 * n + 1) * ROWS * ROWS * width,
-            bytes_accessed=4 * (2 * n + 1) * ROWS * ROWS,
-            transcendentals=(2 * n + 1) * ROWS * ROWS,
-        ),
-        name="last_scores",
-    )(table, scale, before, scores, *own, *other)
+        name=name,
+    )(table, scale, *before, *own, *other)
 
 
 def join_kernel(shift, stats_ref, out_ref):
@@ -450,15 +418,17 @@
     chip = jnp.concatenate([jnp.where(first, mine, got), jnp.where(first, got, mine)], axis=0)
 
     after, before, across = send(chip, -1, 0), send(chip, 1, 0), send(chip, 0, 1)
-    near = [chip, after, before, across]
+    own = [chip, after, before, across]
     middle = [send(after, -1, 0), send(across, 1, 0), send(after, 0, 1)]
+    other = [swap(v) for v in own]
+    scores, stats = score_call("scores_near", False, table, scale2, (), own, other)
+    stats, *middle = lax.optimization_barrier((stats, *middle))
     far = send(middle[2], -1, 0)
-    own = near + middle
-    other = [swap(v) for v in own]
-    scores, stats = score_call(table, scale2, own, other)
+    own, other = own + middle, other + [swap(v) for v in middle]
+    scores, stats = score_call("scores_middle", False, table, scale2, (stats, scores), own, other)
     stats, far = lax.optimization_barrier((stats, far))
-    other = other + [swap(far)]
-    scores, stats = last_score_call(table, scale2, stats, scores, own + [far], other)
+    own, other = own + [far], other + [swap(far)]
+    scores, stats = score_call("scores_far", True, table, scale2, (stats, scores), own, other)
 
     spread = lax.all_to_all(stats, AXES, 0, 0, axis_index_groups=members, tiled=True)
     own_lse = join_call(float(np.log2(2.0 * pairs)), spread)
@@ -469,7 +439,7 @@
 
     received = [send(v, *PIECES[q]) for q, v in zip((7, 6, 5, 4), grads("grads_far", (7, 6, 5, 4)))]
     *near_grads, kept = grads("grads_near", (3, 2, 1, 0))
-    received, near_grads = lax.optimization_barrier((received, near_grads))
+    received[0], near_grads = lax.optimization_barrier((received[0], near_grads))
     received += [send(v, *PIECES[q]) for q, v in zip((3, 2, 1), near_grads)]
     received = [v.astype(jnp.float32) for v in received]
     summed = functools.reduce(jnp.add, [v[:ROWS] for v in received]) + kept

time: 154 us -> 141 us (0.916)
  waiting for transfers between devices: 38 us -> 23.7 us
  local copies, waits for them, and re-layouts: 4.37 us -> 6.75 us
    ppermute x14, waiting for transfers between devices: 31.6 us -> 17.6 us  [send(): return lax.ppermute(value, AXES, ring_perm(steps, pair))]
    ppermute x1, starting transfers between devices: 4.05 us -> 0.96 us  [on_device(): swap(jnp.concatenate([jnp.where(first, summed[shard:], summed[:shard]), p...]
    unnamed x20 -> x18, local copies, waits for them, and re-layouts: 2.64 us -> 5.53 us
    ppermute x14, starting transfers between devices: 19.9 us -> 22.8 us  [send(): return lax.ppermute(value, AXES, ring_perm(steps, pair))]
    pallas_call x2 -> x3, Pallas kernels: 26.5 us -> 27.6 us  [score_call(): pl.pallas_call(functools.partial(score_kernel, old, new, last), in_specs=...]
    ppermute x7 -> x4, starting transfers between devices: 6.13 us -> 5.89 us  [on_device(): other = [swap(v) for v in own]]
  transfers between devices with their start and end apart: 25 -> 25, of which waited for: 12 -> 9; matrix products, arithmetic and copies ran while one was open for 1% -> 1% of each run, Pallas kernels for 20% -> 23%
where the time goes in v2:
time: 141 us
  Pallas kernels  55.1 us (39%)
  starting transfers between devices  36.5 us (26%)
  waiting for transfers between devices  23.7 us (17%)
  blocking collectives  10.3 us (7%)
  local copies, waits for them, and re-layouts  6.75 us (5%)
  other arithmetic  4.82 us (3%)
  between operations  3.37 us (2%)
    pallas_call x3, Pallas kernels, score_call(): pl.pallas_call(functools.partial(score_kernel, old, new, last), in_specs=...  27.6 us
    pallas_call x2, Pallas kernels, grad_call(): pl.pallas_call(functools.partial(grad_kernel, pairs, pieces), grid=(count...  25.8 us
    ppermute x14, starting transfers between devices, send(): return lax.ppermute(value, AXES, ring_perm(steps, pair))  22.8 us
    ppermute x14, waiting for transfers between devices, send(): return lax.ppermute(value, AXES, ring_perm(steps, pair))  17.6 us
    all_to_all x1, blocking collectives, on_device(): lax.all_to_all(stats, AXES, 0, 0, axis_index_groups=members, tiled=True)  10.3 us
    ppermute x4, starting transfers between devices, on_device(): other = [swap(v) for v in own]  5.89 us
    unnamed x18, local copies, waits for them, and re-layouts  5.53 us
    ppermute x1, starting transfers between devices, on_device(): other_lse = swap(own_lse)  3.9 us
  transfers between devices with their start and end apart: 25, of which 9 were waited for; matrix products, arithmetic and copies ran while one was open for 1% of the time, Pallas kernels for 23%

profile of v2, /device:TPU:1, one launch (start us, length us, event | category | flops | bytes accessed | tf_op | source)
XLA Modules:
  0.0 140.5 jit_solution(4935939592319634837)
XLA Ops:
  1.7 1.5 %collective-permute-start = (bf16[128,1280]{1,0:T(8,128)(2,1)S(1)}, bf16[128,1280]{1,0:T(8,128)(2,1)S(1)}, u32[]{:S(2)}, u32[]{:S(2)}) collective-permute-start(bf16[128,1280]{1,0:T(8,128)(2,1)S(1)} %broadcast_select_fusion.2), channel_id=1, source_target_pairs={{0,32},{32,0},{8,40},{40,8},{16,48},{48,16},{24,56},{56,24},{1,33}... | collective-permute-start | bytes 983048 | tf_op jit(solution)/shard_map/ppermute | solution.py:416
  3.2 1.3 collective-permute-done
  5.5 1.4 collective-permute-start.3
  6.9 1.6 %collective-permute-start.2 = (bf16[256,1280]{1,0:T(8,128)(2,1)S(1)}, bf16[256,1280]{1,0:T(8,128)(2,1)}, u32[]{:S(2)}, u32[]{:S(2)}) collective-permute-start(bf16[256,1280]{1,0:T(8,128)(2,1)S(1)} %pad_maximum_fusion.1.refs_0_.refs_2_), channel_id=1, source_target_pairs={{0,1},{32,40},{8,9},{40,48},{16,17},{48,56},{24,25},{56,32},{1,2},... | collective-permute-start | bytes 1966088 | tf_op jit(solution)/shard_map/ppermute | solution.py:414
  8.5 2.1 %collective-permute-start.1 = (bf16[256,1280]{1,0:T(8,128)(2,1)S(1)}, bf16[256,1280]{1,0:T(8,128)(2,1)}, u32[]{:S(2)}, u32[]{:S(2)}) collective-permute-start(bf16[256,1280]{1,0:T(8,128)(2,1)S(1)} %pad_maximum_fusion.1.refs_0_.refs_2_), channel_id=1, source_target_pairs={{0,3},{32,56},{8,11},{40,32},{16,19},{48,40},{24,27},{56,48},{1,0}... | collective-permute-start | bytes 1966088 | tf_op jit(solution)/shard_map/ppermute | solution.py:414
  10.7 1.4 collective-permute-start.4
  12.1 3.4 %collective-permute-done.3.refs_3_.refs_5_ = bf16[256,1280]{1,0:T(8,128)(2,1)} collective-permute-done((bf16[256,1280]{1,0:T(8,128)(2,1)S(1)}, bf16[256,1280]{1,0:T(8,128)(2,1)}, u32[]{:S(2)}, u32[]{:S(2)}) %collective-permute-start.3) | collective-permute-done | bytes 655392 | tf_op jit(solution)/shard_map/ppermute | solution.py:414
  15.4 2.4 %collective-permute-start.7 = (bf16[256,1280]{1,0:T(8,128)(2,1)}, bf16[256,1280]{1,0:T(8,128)(2,1)S(1)}, u32[]{:S(2)}, u32[]{:S(2)}) collective-permute-start(bf16[256,1280]{1,0:T(8,128)(2,1)} %collective-permute-done.3.refs_3_.refs_5_), channel_id=1, source_target_pairs={{0,32},{32,0},{8,40},{40,8},{16,48},{48,16},{24,56},{56,24},{1,33}... | collective-permute-start | bytes 1966088 | tf_op jit(solution)/shard_map/ppermute | solution.py:423
  17.9 1.1 collective-permute-done.2.refs_2_.refs_4_
  19.0 1.7 %collective-permute-start.6 = (bf16[256,1280]{1,0:T(8,128)(2,1)}, bf16[256,1280]{1,0:T(8,128)(2,1)S(1)}, u32[]{:S(2)}, u32[]{:S(2)}) collective-permute-start(bf16[256,1280]{1,0:T(8,128)(2,1)} %collective-permute-done.2.refs_2_.refs_4_), channel_id=1, source_target_pairs={{0,32},{32,0},{8,40},{40,8},{16,48},{48,16},{24,56},{56,24},{1,33}... | collective-permute-start | bytes 1966088 | tf_op jit(solution)/shard_map/ppermute | solution.py:423
  21.1 1.6 %collective-permute-start.9 = (bf16[256,1280]{1,0:T(8,128)(2,1)}, bf16[256,1280]{1,0:T(8,128)(2,1)}, u32[]{:S(2)}, u32[]{:S(2)}) collective-permute-start(bf16[256,1280]{1,0:T(8,128)(2,1)} %collective-permute-done.3.refs_3_.refs_5_), channel_id=1, source_target_pairs={{0,1},{32,40},{8,9},{40,48},{16,17},{48,56},{24,25},{56,32},{1,2},... | collective-permute-start | bytes 1966088 | tf_op jit(solution)/shard_map/ppermute | solution.py:414
  22.7 2.2 %collective-permute-start.8 = (bf16[256,1280]{1,0:T(8,128)(2,1)}, bf16[256,1280]{1,0:T(8,128)(2,1)}, u32[]{:S(2)}, u32[]{:S(2)}) collective-permute-start(bf16[256,1280]{1,0:T(8,128)(2,1)} %collective-permute-done.1.refs_1_.refs_3_), channel_id=1, source_target_pairs={{0,3},{32,56},{8,11},{40,32},{16,19},{48,40},{24,27},{56,48},{1,0}... | collective-permute-start | bytes 1966088 | tf_op jit(solution)/shard_map/ppermute | solution.py:414
  26.3 7.6 %scores_near.1 = (f32[5376,2048]{1,0:T(8,128)}, f32[4,1024]{1,0:T(4,128)S(1)}) custom-call(s32[32]{0:T(128)S(1)} %dynamic-slice_bitcast_fusion.table_ref, f32[1]{0:T(128)} %bitcast.2.scale_ref, bf16[256,1280]{1,0:T(8,128)(2,1)S(1)} %pad_maximum_fusion.1.refs_0_.refs_2_, bf16[256,1280]{1,0:T(8,128)(2,1)} %collective-permute-done.1.refs_1_.refs_3_, ...), custom_call_target="tpu_custom_call" | custom-call | flops 2684354560 | bytes 4194304 | tf_op jit(solution)/shard_map/scores_near/pallas_call | solution.py:238
  35.3 3.8 %collective-permute-start.14 = (bf16[256,1280]{1,0:T(8,128)(2,1)}, bf16[256,1280]{1,0:T(8,128)(2,1)S(1)}, u32[]{:S(2)}, u32[]{:S(2)}) collective-permute-start(bf16[256,1280]{1,0:T(8,128)(2,1)} %collective-permute-done.10.refs_8_), channel_id=1, source_target_pairs={{0,3},{32,56},{8,11},{40,32},{16,19},{48,40},{24,27},{56,48},{1,0}... | collective-permute-start | bytes 1966088 | tf_op jit(solution)/shard_map/ppermute | solution.py:414
  39.1 1.5 %copy-done.5 = bf16[256,1280]{1,0:T(8,128)(2,1)S(1)} copy-done((bf16[256,1280]{1,0:T(8,128)(2,1)S(1)}, bf16[256,1280]{1,0:T(8,128)(2,1)}, u32[]{:S(2)}) %copy-start.5) | copy-done | bytes 655384
  40.6 11.8 %scores_middle.1 = (f32[5376,2048]{1,0:T(8,128)}, f32[4,1792]{1,0:T(4,128)S(1)}) custom-call(s32[32]{0:T(128)S(1)} %dynamic-slice_bitcast_fusion.table_ref, f32[1]{0:T(128)} %bitcast.2.scale_ref, f32[4,1024]{1,0:T(4,128)S(1)} %get-tuple-element.29.refs_0_, f32[5376,2048]{1,0:T(8,128)} %get-tuple-element.30.refs_1_, ...), custom_call_target="tpu_custom_call", output_to_operand_aliasing={{0}: (3, {})} | custom-call | flops 5536481280 | bytes 8650752 | tf_op jit(solution)/shard_map/scores_middle/pallas_call | solution.py:238
  52.6 2.1 %collective-permute-done.15.refs_17_.refs_7_ = bf16[256,1280]{1,0:T(8,128)(2,1)S(1)} collective-permute-done((bf16[256,1280]{1,0:T(8,128)(2,1)S(1)}, bf16[256,1280]{1,0:T(8,128)(2,1)S(1)}, u32[]{:S(2)}, u32[]{:S(2)}) %collective-permute-start.15) | collective-permute-done | bytes 655392 | tf_op jit(solution)/shard_map/ppermute | solution.py:430
  54.7 8.2 %scores_far.1 = (f32[5376,2048]{1,0:T(8,128)}, f32[8,4,2048]{2,1,0:T(4,128)S(1)}) custom-call(s32[32]{0:T(128)S(1)} %dynamic-slice_bitcast_fusion.table_ref, f32[1]{0:T(128)} %bitcast.2.scale_ref, f32[4,1792]{1,0:T(4,128)S(1)} %get-tuple-element.35.refs_0_, f32[5376,2048]{1,0:T(8,128)} %get-tuple-element.36.refs_1_, ...), custom_call_target="tpu_custom_call", output_to_operand_aliasing={{0}: (3, {})} | custom-call | flops 2516582400 | bytes 3932160 | tf_op jit(solution)/shard_map/scores_far/pallas_call | solution.py:238
  62.9 10.3 %all_to_all.5.stats_ref = f32[8,4,2048]{2,1,0:T(4,128)} all-to-all(f32[8,4,2048]{2,1,0:T(4,128)S(1)} %get-tuple-element.38), channel_id=1, replica_groups={{0,1,2,3,68,69,70,71},{4,5,6,7,64,65,66,67},{8,9,10,11,76,77,78,79},{12..., dimensions={0} | all-to-all | bytes 524288 | tf_op jit(solution)/shard_map/all_to_all | solution.py:433
  73.2 1.7 %join.1.own_lse_ref = f32[1,2304]{1,0:T(1,128)} custom-call(f32[8,4,2048]{2,1,0:T(4,128)} %all_to_all.5.stats_ref), custom_call_target="tpu_custom_call" | custom-call | tf_op jit(solution)/shard_map/join/pallas_call | solution.py:284
  74.9 3.9 %collective-permute-start.16 = (f32[1,2304]{1,0:T(1,128)}, f32[1,2304]{1,0:T(1,128)S(1)}, u32[]{:S(2)}, u32[]{:S(2)}) collective-permute-start(f32[1,2304]{1,0:T(1,128)} %join.1.own_lse_ref), channel_id=1, source_target_pairs={{0,32},{32,0},{8,40},{40,8},{16,48},{48,16},{24,56},{56,24},{1,33}... | collective-permute-start | bytes 27656 | tf_op jit(solution)/shard_map/ppermute | solution.py:435
  79.8 1.1 copy-done.1
  83.8 13.0 %grads_far.1 = (bf16[272,1280]{1,0:T(8,128)(2,1)S(1)}, bf16[272,1280]{1,0:T(8,128)(2,1)S(1)}, bf16[272,1280]{1,0:T(8,128)(2,1)S(1)}, bf16[272,1280]{1,0:T(8,128)(2,1)S(1)}) custom-call(s32[32]{0:T(128)S(1)} %dynamic-slice_bitcast_fusion.table_ref, f32[1]{0:T(128)} %bitcast.7.scale_ref, f32[1,2304]{1,0:T(1,128)S(1)} %copy-done.8, ...), custom_call_target="tpu_custom_call" | custom-call | flops 5368709120 | bytes 8388608 | tf_op jit(solution)/shard_map/grads_far/pallas_call | solution.py:372
  96.9 4.8 %collective-permute-start.18 = (bf16[272,1280]{1,0:T(8,128)(2,1)S(1)}, bf16[272,1280]{1,0:T(8,128)(2,1)S(1)}, u32[]{:S(2)}, u32[]{:S(2)}) collective-permute-start(bf16[272,1280]{1,0:T(8,128)(2,1)S(1)} %get-tuple-element.45), channel_id=1, source_target_pairs={{0,69},{32,104},{8,77},{40,112},{16,85},{48,120},{24,93},{56,96},{... | collective-permute-start | bytes 2088968 | tf_op jit(solution)/shard_map/ppermute | solution.py:414
  101.7 1.8 %collective-permute-start.20 = (bf16[272,1280]{1,0:T(8,128)(2,1)S(1)}, bf16[272,1280]{1,0:T(8,128)(2,1)S(1)}, u32[]{:S(2)}, u32[]{:S(2)}) collective-permute-start(bf16[272,1280]{1,0:T(8,128)(2,1)S(1)} %get-tuple-element.47), channel_id=1, source_target_pairs={{0,2},{32,48},{8,10},{40,56},{16,18},{48,32},{24,26},{56,40},{1,3}... | collective-permute-start | bytes 2088968 | tf_op jit(solution)/shard_map/ppermute | solution.py:414
  103.5 12.8 %grads_near.1 = (bf16[272,1280]{1,0:T(8,128)(2,1)S(1)}, bf16[272,1280]{1,0:T(8,128)(2,1)S(1)}, bf16[272,1280]{1,0:T(8,128)(2,1)S(1)}, f32[256,1280]{1,0:T(8,128)S(1)}) custom-call(s32[32]{0:T(128)S(1)} %dynamic-slice_bitcast_fusion.table_ref, f32[1]{0:T(128)} %bitcast.8.scale_ref, f32[1,2304]{1,0:T(1,128)S(1)} %copy-done.8, ...), custom_call_target="tpu_custom_call" | custom-call | flops 5368709120 | bytes 8388608 | tf_op jit(solution)/shard_map/grads_near/pallas_call | solution.py:372
  116.3 1.4 collective-permute-start.21
  117.7 2.0 %collective-permute-start.22 = (bf16[272,1280]{1,0:T(8,128)(2,1)S(1)}, bf16[272,1280]{1,0:T(8,128)(2,1)S(1)}, u32[]{:S(2)}, u32[]{:S(2)}) collective-permute-start(bf16[272,1280]{1,0:T(8,128)(2,1)S(1)} %get-tuple-element.49), channel_id=1, source_target_pairs={{0,3},{32,56},{8,11},{40,32},{16,19},{48,40},{24,27},{56,48},{1,0}... | collective-permute-start | bytes 2088968 | tf_op jit(solution)/shard_map/ppermute | solution.py:414
  119.8 6.0 %collective-permute-done.19 = bf16[272,1280]{1,0:T(8,128)(2,1)S(1)} collective-permute-done((bf16[272,1280]{1,0:T(8,128)(2,1)S(1)}, bf16[272,1280]{1,0:T(8,128)(2,1)S(1)}, u32[]{:S(2)}, u32[]{:S(2)}) %collective-permute-start.19) | collective-permute-done | bytes 696352 | tf_op jit(solution)/shard_map/ppermute | solution.py:414
  126.1 6.8 %collective-permute-done.21 = bf16[272,1280]{1,0:T(8,128)(2,1)S(1)} collective-permute-done((bf16[272,1280]{1,0:T(8,128)(2,1)S(1)}, bf16[272,1280]{1,0:T(8,128)(2,1)S(1)}, u32[]{:S(2)}, u32[]{:S(2)}) %collective-permute-start.21) | collective-permute-done | bytes 696352 | tf_op jit(solution)/shard_map/ppermute | solution.py:414
  135.3 1.8 %collective-permute-done.24 = f32[136,1280]{1,0:T(8,128)S(1)} collective-permute-done((f32[136,1280]{1,0:T(8,128)S(1)}, f32[136,1280]{1,0:T(8,128)S(1)}, u32[]{:S(2)}, u32[]{:S(2)}) %collective-permute-start.24) | collective-permute-done | bytes 696352 | tf_op jit(solution)/shard_map/ppermute | solution.py:450
  138.2 1.2 slice_select_fusion
  (70 shorter events, 12.0 us)
Async XLA Ops:
  1.7 2.8 %collective-permute-start = (bf16[128,1280]{1,0:T(8,128)(2,1)S(1)}, bf16[128,1280]{1,0:T(8,128)(2,1)S(1)}, u32[]{:S(2)}, u32[]{:S(2)}) collective-permute-start(bf16[128,1280]{1,0:T(8,128)(2,1)S(1)} %broadcast_select_fusion.2), channel_id=1, source_target_pairs={{0,32},{32,0},{8,40},{40,8},{16,48},{48,16},{24,56},{56,24},{1,33}... | collective-permute-start | bytes 983048 | tf_op jit(solution)/shard_map/ppermute | solution.py:416
  5.5 28.4 %copy-start.4 = (bf16[256,1280]{1,0:T(8,128)(2,1)}, bf16[256,1280]{1,0:T(8,128)(2,1)S(1)}, u32[]{:S(2)}) copy-start(bf16[256,1280]{1,0:T(8,128)(2,1)S(1)} %pad_maximum_fusion.1.refs_0_.refs_2_) | copy-start | bytes 1966084
  5.5 9.9 %collective-permute-start.3 = (bf16[256,1280]{1,0:T(8,128)(2,1)S(1)}, bf16[256,1280]{1,0:T(8,128)(2,1)}, u32[]{:S(2)}, u32[]{:S(2)}) collective-permute-start(bf16[256,1280]{1,0:T(8,128)(2,1)S(1)} %pad_maximum_fusion.1.refs_0_.refs_2_), channel_id=1, source_target_pairs={{0,68},{32,96},{8,76},{40,104},{16,84},{48,112},{24,92},{56,120},{... | collective-permute-start | bytes 1966088 | tf_op jit(solution)/shard_map/ppermute | solution.py:414
  6.9 12.1 %collective-permute-start.2 = (bf16[256,1280]{1,0:T(8,128)(2,1)S(1)}, bf16[256,1280]{1,0:T(8,128)(2,1)}, u32[]{:S(2)}, u32[]{:S(2)}) collective-permute-start(bf16[256,1280]{1,0:T(8,128)(2,1)S(1)} %pad_maximum_fusion.1.refs_0_.refs_2_), channel_id=1, source_target_pairs={{0,1},{32,40},{8,9},{40,48},{16,17},{48,56},{24,25},{56,32},{1,2},... | collective-permute-start | bytes 1966088 | tf_op jit(solution)/shard_map/ppermute | solution.py:414
  8.5 12.2 %collective-permute-start.1 = (bf16[256,1280]{1,0:T(8,128)(2,1)S(1)}, bf16[256,1280]{1,0:T(8,128)(2,1)}, u32[]{:S(2)}, u32[]{:S(2)}) collective-permute-start(bf16[256,1280]{1,0:T(8,128)(2,1)S(1)} %pad_maximum_fusion.1.refs_0_.refs_2_), channel_id=1, source_target_pairs={{0,3},{32,56},{8,11},{40,32},{16,19},{48,40},{24,27},{56,48},{1,0}... | collective-permute-start | bytes 1966088 | tf_op jit(solution)/shard_map/ppermute | solution.py:414
  10.7 12.1 %collective-permute-start.4 = (bf16[256,1280]{1,0:T(8,128)(2,1)S(1)}, bf16[256,1280]{1,0:T(8,128)(2,1)S(1)}, u32[]{:S(2)}, u32[]{:S(2)}) collective-permute-start(bf16[256,1280]{1,0:T(8,128)(2,1)S(1)} %pad_maximum_fusion.1.refs_0_.refs_2_), channel_id=1, source_target_pairs={{0,32},{32,0},{8,40},{40,8},{16,48},{48,16},{24,56},{56,24},{1,33}... | collective-permute-start | bytes 1966088 | tf_op jit(solution)/shard_map/ppermute | solution.py:423
  15.4 7.3 %collective-permute-start.7 = (bf16[256,1280]{1,0:T(8,128)(2,1)}, bf16[256,1280]{1,0:T(8,128)(2,1)S(1)}, u32[]{:S(2)}, u32[]{:S(2)}) collective-permute-start(bf16[256,1280]{1,0:T(8,128)(2,1)} %collective-permute-done.3.refs_3_.refs_5_), channel_id=1, source_target_pairs={{0,32},{32,0},{8,40},{40,8},{16,48},{48,16},{24,56},{56,24},{1,33}... | collective-permute-start | bytes 1966088 | tf_op jit(solution)/shard_map/ppermute | solution.py:423
  19.0 7.3 %collective-permute-start.6 = (bf16[256,1280]{1,0:T(8,128)(2,1)}, bf16[256,1280]{1,0:T(8,128)(2,1)S(1)}, u32[]{:S(2)}, u32[]{:S(2)}) collective-permute-start(bf16[256,1280]{1,0:T(8,128)(2,1)} %collective-permute-done.2.refs_2_.refs_4_), channel_id=1, source_target_pairs={{0,32},{32,0},{8,40},{40,8},{16,48},{48,16},{24,56},{56,24},{1,33}... | collective-permute-start | bytes 1966088 | tf_op jit(solution)/shard_map/ppermute | solution.py:423
  20.7 5.6 %collective-permute-start.5 = (bf16[256,1280]{1,0:T(8,128)(2,1)}, bf16[256,1280]{1,0:T(8,128)(2,1)S(1)}, u32[]{:S(2)}, u32[]{:S(2)}) collective-permute-start(bf16[256,1280]{1,0:T(8,128)(2,1)} %collective-permute-done.1.refs_1_.refs_3_), channel_id=1, source_target_pairs={{0,32},{32,0},{8,40},{40,8},{16,48},{48,16},{24,56},{56,24},{1,33}... | collective-permute-start | bytes 1966088 | tf_op jit(solution)/shard_map/ppermute | solution.py:423
  21.1 12.8 %collective-permute-start.9 = (bf16[256,1280]{1,0:T(8,128)(2,1)}, bf16[256,1280]{1,0:T(8,128)(2,1)}, u32[]{:S(2)}, u32[]{:S(2)}) collective-permute-start(bf16[256,1280]{1,0:T(8,128)(2,1)} %collective-permute-done.3.refs_3_.refs_5_), channel_id=1, source_target_pairs={{0,1},{32,40},{8,9},{40,48},{16,17},{48,56},{24,25},{56,32},{1,2},... | collective-permute-start | bytes 1966088 | tf_op jit(solution)/shard_map/ppermute | solution.py:414
  22.7 11.2 %collective-permute-start.10 = (bf16[256,1280]{1,0:T(8,128)(2,1)}, bf16[256,1280]{1,0:T(8,128)(2,1)}, u32[]{:S(2)}, u32[]{:S(2)}) collective-permute-start(bf16[256,1280]{1,0:T(8,128)(2,1)} %collective-permute-done.1.refs_1_.refs_3_), channel_id=1, source_target_pairs={{0,68},{32,96},{8,76},{40,104},{16,84},{48,112},{24,92},{56,120},{... | collective-permute-start | bytes 1966088 | tf_op jit(solution)/shard_map/ppermute | solution.py:414
  22.7 11.2 %collective-permute-start.8 = (bf16[256,1280]{1,0:T(8,128)(2,1)}, bf16[256,1280]{1,0:T(8,128)(2,1)}, u32[]{:S(2)}, u32[]{:S(2)}) collective-permute-start(bf16[256,1280]{1,0:T(8,128)(2,1)} %collective-permute-done.1.refs_1_.refs_3_), channel_id=1, source_target_pairs={{0,3},{32,56},{8,11},{40,32},{16,19},{48,40},{24,27},{56,48},{1,0}... | collective-permute-start | bytes 1966088 | tf_op jit(solution)/shard_map/ppermute | solution.py:414
  33.9 5.1 %collective-permute-start.11 = (bf16[256,1280]{1,0:T(8,128)(2,1)}, bf16[256,1280]{1,0:T(8,128)(2,1)S(1)}, u32[]{:S(2)}, u32[]{:S(2)}) collective-permute-start(bf16[256,1280]{1,0:T(8,128)(2,1)} %collective-permute-done.8.refs_6_), channel_id=1, source_target_pairs={{0,32},{32,0},{8,40},{40,8},{16,48},{48,16},{24,56},{56,24},{1,33}... | collective-permute-start | bytes 1966088 | tf_op jit(solution)/shard_map/ppermute | solution.py:427
  34.8 4.3 %collective-permute-start.12 = (bf16[256,1280]{1,0:T(8,128)(2,1)}, bf16[256,1280]{1,0:T(8,128)(2,1)S(1)}, u32[]{:S(2)}, u32[]{:S(2)}) collective-permute-start(bf16[256,1280]{1,0:T(8,128)(2,1)} %collective-permute-done.9.refs_7_), channel_id=1, source_target_pairs={{0,32},{32,0},{8,40},{40,8},{16,48},{48,16},{24,56},{56,24},{1,33}... | collective-permute-start | bytes 1966088 | tf_op jit(solution)/shard_map/ppermute | solution.py:427
  34.8 4.3 %collective-permute-start.13 = (bf16[256,1280]{1,0:T(8,128)(2,1)}, bf16[256,1280]{1,0:T(8,128)(2,1)S(1)}, u32[]{:S(2)}, u32[]{:S(2)}) collective-permute-start(bf16[256,1280]{1,0:T(8,128)(2,1)} %collective-permute-done.10.refs_8_), channel_id=1, source_target_pairs={{0,32},{32,0},{8,40},{40,8},{16,48},{48,16},{24,56},{56,24},{1,33}... | collective-permute-start | bytes 1966088 | tf_op jit(solution)/shard_map/ppermute | solution.py:427
  35.3 17.2 %collective-permute-start.14 = (bf16[256,1280]{1,0:T(8,128)(2,1)}, bf16[256,1280]{1,0:T(8,128)(2,1)S(1)}, u32[]{:S(2)}, u32[]{:S(2)}) collective-permute-start(bf16[256,1280]{1,0:T(8,128)(2,1)} %collective-permute-done.10.refs_8_), channel_id=1, source_target_pairs={{0,3},{32,56},{8,11},{40,32},{16,19},{48,40},{24,27},{56,48},{1,0}... | collective-permute-start | bytes 1966088 | tf_op jit(solution)/shard_map/ppermute | solution.py:414
  39.1 15.6 %copy-start = (bf16[256,1280]{1,0:T(8,128)(2,1)}, bf16[256,1280]{1,0:T(8,128)(2,1)S(1)}, u32[]{:S(2)}) copy-start(bf16[256,1280]{1,0:T(8,128)(2,1)S(1)} %collective-permute-done.12.refs_14_.refs_15_.refs_5_) | copy-start | bytes 1966084
  39.1 15.6 %copy-start.2 = (bf16[256,1280]{1,0:T(8,128)(2,1)}, bf16[256,1280]{1,0:T(8,128)(2,1)S(1)}, u32[]{:S(2)}) copy-start(bf16[256,1280]{1,0:T(8,128)(2,1)S(1)} %collective-permute-done.13.refs_15_.refs_16_.refs_6_) | copy-start | bytes 1966084
  39.1 1.6 %copy-start.5 = (bf16[256,1280]{1,0:T(8,128)(2,1)S(1)}, bf16[256,1280]{1,0:T(8,128)(2,1)}, u32[]{:S(2)}) copy-start(bf16[256,1280]{1,0:T(8,128)(2,1)} %copy-done.4) | copy-start | bytes 1966084
  52.5 2.2 %collective-permute-start.15 = (bf16[256,1280]{1,0:T(8,128)(2,1)S(1)}, bf16[256,1280]{1,0:T(8,128)(2,1)S(1)}, u32[]{:S(2)}, u32[]{:S(2)}) collective-permute-start(bf16[256,1280]{1,0:T(8,128)(2,1)S(1)} %collective-permute-done.14.refs_9_), channel_id=1, source_target_pairs={{0,32},{32,0},{8,40},{40,8},{16,48},{48,16},{24,56},{56,24},{1,33}... | collective-permute-start | bytes 1966088 | tf_op jit(solution)/shard_map/ppermute | solution.py:430
  54.7 8.2 %copy-start.6 = (bf16[256,1280]{1,0:T(8,128)(2,1)}, bf16[256,1280]{1,0:T(8,128)(2,1)S(1)}, u32[]{:S(2)}) copy-start(bf16[256,1280]{1,0:T(8,128)(2,1)S(1)} %collective-permute-done.15.refs_17_.refs_7_) | copy-start | bytes 1966084
  74.9 4.9 %collective-permute-start.16 = (f32[1,2304]{1,0:T(1,128)}, f32[1,2304]{1,0:T(1,128)S(1)}, u32[]{:S(2)}, u32[]{:S(2)}) collective-permute-start(f32[1,2304]{1,0:T(1,128)} %join.1.own_lse_ref), channel_id=1, source_target_pairs={{0,32},{32,0},{8,40},{40,8},{16,48},{48,16},{24,56},{56,24},{1,33}... | collective-permute-start | bytes 27656 | tf_op jit(solution)/shard_map/ppermute | solution.py:435
  79.8 1.1 copy-start.1
  82.0 1.1 copy-start.7
  96.8 19.5 %collective-permute-start.17 = (bf16[272,1280]{1,0:T(8,128)(2,1)S(1)}, bf16[272,1280]{1,0:T(8,128)(2,1)S(1)}, u32[]{:S(2)}, u32[]{:S(2)}) collective-permute-start(bf16[272,1280]{1,0:T(8,128)(2,1)S(1)} %get-tuple-element.40), channel_id=1, source_target_pairs={{0,70},{32,112},{8,78},{40,120},{16,86},{48,96},{24,94},{56,104},{... | collective-permute-start | bytes 2088968 | tf_op jit(solution)/shard_map/ppermute | solution.py:414
  96.9 22.7 %collective-permute-start.18 = (bf16[272,1280]{1,0:T(8,128)(2,1)S(1)}, bf16[272,1280]{1,0:T(8,128)(2,1)S(1)}, u32[]{:S(2)}, u32[]{:S(2)}) collective-permute-start(bf16[272,1280]{1,0:T(8,128)(2,1)S(1)} %get-tuple-element.45), channel_id=1, source_target_pairs={{0,69},{32,104},{8,77},{40,112},{16,85},{48,120},{24,93},{56,96},{... | collective-permute-start | bytes 2088968 | tf_op jit(solution)/shard_map/ppermute | solution.py:414
  101.7 24.1 %collective-permute-start.19 = (bf16[272,1280]{1,0:T(8,128)(2,1)S(1)}, bf16[272,1280]{1,0:T(8,128)(2,1)S(1)}, u32[]{:S(2)}, u32[]{:S(2)}) collective-permute-start(bf16[272,1280]{1,0:T(8,128)(2,1)S(1)} %get-tuple-element.46), channel_id=1, source_target_pairs={{0,71},{32,120},{8,79},{40,96},{16,87},{48,104},{24,95},{56,112},{... | collective-permute-start | bytes 2088968 | tf_op jit(solution)/shard_map/ppermute | solution.py:414
  101.7 24.2 %collective-permute-start.20 = (bf16[272,1280]{1,0:T(8,128)(2,1)S(1)}, bf16[272,1280]{1,0:T(8,128)(2,1)S(1)}, u32[]{:S(2)}, u32[]{:S(2)}) collective-permute-start(bf16[272,1280]{1,0:T(8,128)(2,1)S(1)} %get-tuple-element.47), channel_id=1, source_target_pairs={{0,2},{32,48},{8,10},{40,56},{16,18},{48,32},{24,26},{56,40},{1,3}... | collective-permute-start | bytes 2088968 | tf_op jit(solution)/shard_map/ppermute | solution.py:414
  116.3 16.5 %collective-permute-start.21 = (bf16[272,1280]{1,0:T(8,128)(2,1)S(1)}, bf16[272,1280]{1,0:T(8,128)(2,1)S(1)}, u32[]{:S(2)}, u32[]{:S(2)}) collective-permute-start(bf16[272,1280]{1,0:T(8,128)(2,1)S(1)} %get-tuple-element.48), channel_id=1, source_target_pairs={{0,68},{32,96},{8,76},{40,104},{16,84},{48,112},{24,92},{56,120},{... | collective-permute-start | bytes 2088968 | tf_op jit(solution)/shard_map/ppermute | solution.py:414
  117.7 15.6 %collective-permute-start.22 = (bf16[272,1280]{1,0:T(8,128)(2,1)S(1)}, bf16[272,1280]{1,0:T(8,128)(2,1)S(1)}, u32[]{:S(2)}, u32[]{:S(2)}) collective-permute-start(bf16[272,1280]{1,0:T(8,128)(2,1)S(1)} %get-tuple-element.49), channel_id=1, source_target_pairs={{0,3},{32,56},{8,11},{40,32},{16,19},{48,40},{24,27},{56,48},{1,0}... | collective-permute-start | bytes 2088968 | tf_op jit(solution)/shard_map/ppermute | solution.py:414
  119.6 13.7 %collective-permute-start.23 = (bf16[272,1280]{1,0:T(8,128)(2,1)S(1)}, bf16[272,1280]{1,0:T(8,128)(2,1)S(1)}, u32[]{:S(2)}, u32[]{:S(2)}) collective-permute-start(bf16[272,1280]{1,0:T(8,128)(2,1)S(1)} %get-tuple-element.50), channel_id=1, source_target_pairs={{0,1},{32,40},{8,9},{40,48},{16,17},{48,56},{24,25},{56,32},{1,2},... | collective-permute-start | bytes 2088968 | tf_op jit(solution)/shard_map/ppermute | solution.py:414
  134.3 2.7 %collective-permute-start.24 = (f32[136,1280]{1,0:T(8,128)S(1)}, f32[136,1280]{1,0:T(8,128)S(1)}, u32[]{:S(2)}, u32[]{:S(2)}) collective-permute-start(f32[136,1280]{1,0:T(8,128)S(1)} %pad_maximum_fusion), channel_id=1, source_target_pairs={{0,32},{32,0},{8,40},{40,8},{16,48},{48,16},{24,56},{56,24},{1,33}... | collective-permute-start | bytes 2088968 | tf_op jit(solution)/shard_map/ppermute | solution.py:450
  (2 other events, 1.8 us)

commit v3 on v2

--- a/solution.py
+++ b/solution.py
@@ -14,6 +14,7 @@
 AXES = ("row", "col")
 ROWS = 256
 VMEM = 24 * 1024 * 1024
+GRAD_VMEM = 63_400_000
 SPARE = 3328
 EXTRA = 16
 PAIR = 2
@@ -390,7 +391,7 @@
             pltpu.SemaphoreType.DMA((count,)),
             pltpu.SemaphoreType.DMA((8,)),
         ],
-        compiler_params=pltpu.CompilerParams(vmem_limit_bytes=VMEM),
+        compiler_params=pltpu.CompilerParams(vmem_limit_bytes=GRAD_VMEM),
         cost_estimate=pl.CostEstimate(
             flops=2 * count * ROWS * m * width,
             bytes_accessed=4 * count * ROWS * m,

time: 141 us -> 139 us (0.986)
  local copies, waits for them, and re-layouts: 6.75 us -> 4.57 us
    unnamed x18 -> x26, local copies, waits for them, and re-layouts: 5.53 us -> 3.35 us
  transfers between devices with their start and end apart: 25 -> 25, of which waited for: 9 -> 9; matrix products, arithmetic and copies ran while one was open for 1% -> 1% of each run, Pallas kernels for 23% -> 24%
where the time goes in v3:
time: 139 us
  Pallas kernels  56.2 us (40%)
  starting transfers between devices  35.6 us (26%)
  waiting for transfers between devices  23.6 us (17%)
  blocking collectives  10.2 us (7%)
  other arithmetic  5.42 us (4%)
  local copies, waits for them, and re-layouts  4.57 us (3%)
  between operations  3.45 us (2%)
    pallas_call x3, Pallas kernels, score_call(): pl.pallas_call(functools.partial(score_kernel, old, new, last), in_specs=...  27.6 us
    pallas_call x2, Pallas kernels, grad_call(): pl.pallas_call(functools.partial(grad_kernel, pairs, pieces), grid=(count...  26.8 us
    ppermute x14, starting transfers between devices, send(): return lax.ppermute(value, AXES, ring_perm(steps, pair))  22.8 us
    ppermute x14, waiting for transfers between devices, send(): return lax.ppermute(value, AXES, ring_perm(steps, pair))  17 us
    all_to_all x1, blocking collectives, on_device(): lax.all_to_all(stats, AXES, 0, 0, axis_index_groups=members, tiled=True)  10.2 us
    ppermute x4, starting transfers between devices, on_device(): other = [swap(v) for v in own]  5.89 us
    ppermute x1, starting transfers between devices, on_device(): other_lse = swap(own_lse)  3.94 us
    unnamed x26, local copies, waits for them, and re-layouts  3.35 us
  transfers between devices with their start and end apart: 25, of which 9 were waited for; matrix products, arithmetic and copies ran while one was open for 1% of the time, Pallas kernels for 24%

profile of v3, /device:TPU:1, one launch (start us, length us, event | category | flops | bytes accessed | tf_op | source)
XLA Modules:
  0.0 139.0 jit_solution(7668548910307275612)
XLA Ops:
  1.7 1.5 %collective-permute-start = (bf16[128,1280]{1,0:T(8,128)(2,1)S(1)}, bf16[128,1280]{1,0:T(8,128)(2,1)S(1)}, u32[]{:S(2)}, u32[]{:S(2)}) collective-permute-start(bf16[128,1280]{1,0:T(8,128)(2,1)S(1)} %broadcast_select_fusion.2), channel_id=1, source_target_pairs={{0,32},{32,0},{8,40},{40,8},{16,48},{48,16},{24,56},{56,24},{1,33}... | collective-permute-start | bytes 983048 | tf_op jit(solution)/shard_map/ppermute | solution.py:417
  3.2 1.3 collective-permute-done
  5.5 1.4 collective-permute-start.3
  6.9 1.6 %collective-permute-start.2 = (bf16[256,1280]{1,0:T(8,128)(2,1)S(1)}, bf16[256,1280]{1,0:T(8,128)(2,1)}, u32[]{:S(2)}, u32[]{:S(2)}) collective-permute-start(bf16[256,1280]{1,0:T(8,128)(2,1)S(1)} %pad_maximum_fusion.1.refs_0_.refs_2_), channel_id=1, source_target_pairs={{0,1},{32,40},{8,9},{40,48},{16,17},{48,56},{24,25},{56,32},{1,2},... | collective-permute-start | bytes 1966088 | tf_op jit(solution)/shard_map/ppermute | solution.py:415
  8.5 2.1 %collective-permute-start.1 = (bf16[256,1280]{1,0:T(8,128)(2,1)S(1)}, bf16[256,1280]{1,0:T(8,128)(2,1)}, u32[]{:S(2)}, u32[]{:S(2)}) collective-permute-start(bf16[256,1280]{1,0:T(8,128)(2,1)S(1)} %pad_maximum_fusion.1.refs_0_.refs_2_), channel_id=1, source_target_pairs={{0,3},{32,56},{8,11},{40,32},{16,19},{48,40},{24,27},{56,48},{1,0}... | collective-permute-start | bytes 1966088 | tf_op jit(solution)/shard_map/ppermute | solution.py:415
  10.7 1.4 %collective-permute-start.4 = (bf16[256,1280]{1,0:T(8,128)(2,1)S(1)}, bf16[256,1280]{1,0:T(8,128)(2,1)S(1)}, u32[]{:S(2)}, u32[]{:S(2)}) collective-permute-start(bf16[256,1280]{1,0:T(8,128)(2,1)S(1)} %pad_maximum_fusion.1.refs_0_.refs_2_), channel_id=1, source_target_pairs={{0,32},{32,0},{8,40},{40,8},{16,48},{48,16},{24,56},{56,24},{1,33}... | collective-permute-start | bytes 1966088 | tf_op jit(solution)/shard_map/ppermute | solution.py:424
  12.1 3.4 %collective-permute-done.3.refs_3_.refs_5_ = bf16[256,1280]{1,0:T(8,128)(2,1)} collective-permute-done((bf16[256,1280]{1,0:T(8,128)(2,1)S(1)}, bf16[256,1280]{1,0:T(8,128)(2,1)}, u32[]{:S(2)}, u32[]{:S(2)}) %collective-permute-start.3) | collective-permute-done | bytes 655392 | tf_op jit(solution)/shard_map/ppermute | solution.py:415
  15.4 2.4 %collective-permute-start.7 = (bf16[256,1280]{1,0:T(8,128)(2,1)}, bf16[256,1280]{1,0:T(8,128)(2,1)S(1)}, u32[]{:S(2)}, u32[]{:S(2)}) collective-permute-start(bf16[256,1280]{1,0:T(8,128)(2,1)} %collective-permute-done.3.refs_3_.refs_5_), channel_id=1, source_target_pairs={{0,32},{32,0},{8,40},{40,8},{16,48},{48,16},{24,56},{56,24},{1,33}... | collective-permute-start | bytes 1966088 | tf_op jit(solution)/shard_map/ppermute | solution.py:424
  17.9 1.1 collective-permute-done.2.refs_2_.refs_4_
  19.0 1.7 %collective-permute-start.6 = (bf16[256,1280]{1,0:T(8,128)(2,1)}, bf16[256,1280]{1,0:T(8,128)(2,1)S(1)}, u32[]{:S(2)}, u32[]{:S(2)}) collective-permute-start(bf16[256,1280]{1,0:T(8,128)(2,1)} %collective-permute-done.2.refs_2_.refs_4_), channel_id=1, source_target_pairs={{0,32},{32,0},{8,40},{40,8},{16,48},{48,16},{24,56},{56,24},{1,33}... | collective-permute-start | bytes 1966088 | tf_op jit(solution)/shard_map/ppermute | solution.py:424
  21.1 1.6 %collective-permute-start.9 = (bf16[256,1280]{1,0:T(8,128)(2,1)}, bf16[256,1280]{1,0:T(8,128)(2,1)}, u32[]{:S(2)}, u32[]{:S(2)}) collective-permute-start(bf16[256,1280]{1,0:T(8,128)(2,1)} %collective-permute-done.3.refs_3_.refs_5_), channel_id=1, source_target_pairs={{0,1},{32,40},{8,9},{40,48},{16,17},{48,56},{24,25},{56,32},{1,2},... | collective-permute-start | bytes 1966088 | tf_op jit(solution)/shard_map/ppermute | solution.py:415
  22.8 2.3 %collective-permute-start.8 = (bf16[256,1280]{1,0:T(8,128)(2,1)}, bf16[256,1280]{1,0:T(8,128)(2,1)}, u32[]{:S(2)}, u32[]{:S(2)}) collective-permute-start(bf16[256,1280]{1,0:T(8,128)(2,1)} %collective-permute-done.1.refs_1_.refs_3_), channel_id=1, source_target_pairs={{0,3},{32,56},{8,11},{40,32},{16,19},{48,40},{24,27},{56,48},{1,0}... | collective-permute-start | bytes 1966088 | tf_op jit(solution)/shard_map/ppermute | solution.py:415
  26.4 7.6 %scores_near.1 = (f32[5376,2048]{1,0:T(8,128)}, f32[4,1024]{1,0:T(4,128)S(1)}) custom-call(s32[32]{0:T(128)S(1)} %dynamic-slice_bitcast_fusion.table_ref, f32[1]{0:T(128)} %bitcast.2.scale_ref, bf16[256,1280]{1,0:T(8,128)(2,1)S(1)} %pad_maximum_fusion.1.refs_0_.refs_2_, bf16[256,1280]{1,0:T(8,128)(2,1)} %collective-permute-done.1.refs_1_.refs_3_, ...), custom_call_target="tpu_custom_call" | custom-call | flops 2684354560 | bytes 4194304 | tf_op jit(solution)/shard_map/scores_near/pallas_call | solution.py:239
  35.3 3.8 %collective-permute-start.14 = (bf16[256,1280]{1,0:T(8,128)(2,1)}, bf16[256,1280]{1,0:T(8,128)(2,1)S(1)}, u32[]{:S(2)}, u32[]{:S(2)}) collective-permute-start(bf16[256,1280]{1,0:T(8,128)(2,1)} %collective-permute-done.10.refs_8_), channel_id=1, source_target_pairs={{0,3},{32,56},{8,11},{40,32},{16,19},{48,40},{24,27},{56,48},{1,0}... | collective-permute-start | bytes 1966088 | tf_op jit(solution)/shard_map/ppermute | solution.py:415
  39.1 1.6 %copy-done.8 = bf16[256,1280]{1,0:T(8,128)(2,1)S(1)} copy-done((bf16[256,1280]{1,0:T(8,128)(2,1)S(1)}, bf16[256,1280]{1,0:T(8,128)(2,1)}, u32[]{:S(2)}) %copy-start.8) | copy-done | bytes 655384
  40.7 11.9 %scores_middle.1 = (f32[5376,2048]{1,0:T(8,128)}, f32[4,1792]{1,0:T(4,128)S(1)}) custom-call(s32[32]{0:T(128)S(1)} %dynamic-slice_bitcast_fusion.table_ref, f32[1]{0:T(128)} %bitcast.2.scale_ref, f32[4,1024]{1,0:T(4,128)S(1)} %get-tuple-element.29.refs_0_, f32[5376,2048]{1,0:T(8,128)} %get-tuple-element.30.refs_1_, ...), custom_call_target="tpu_custom_call", output_to_operand_aliasing={{0}: (3, {})} | custom-call | flops 5536481280 | bytes 8650752 | tf_op jit(solution)/shard_map/scores_middle/pallas_call | solution.py:239
  52.6 2.1 %collective-permute-done.15.refs_17_.refs_7_ = bf16[256,1280]{1,0:T(8,128)(2,1)S(1)} collective-permute-done((bf16[256,1280]{1,0:T(8,128)(2,1)S(1)}, bf16[256,1280]{1,0:T(8,128)(2,1)S(1)}, u32[]{:S(2)}, u32[]{:S(2)}) %collective-permute-start.15) | collective-permute-done | bytes 655392 | tf_op jit(solution)/shard_map/ppermute | solution.py:431
  54.8 8.2 %scores_far.1 = (f32[5376,2048]{1,0:T(8,128)}, f32[8,4,2048]{2,1,0:T(4,128)S(1)}) custom-call(s32[32]{0:T(128)S(1)} %dynamic-slice_bitcast_fusion.table_ref, f32[1]{0:T(128)} %bitcast.2.scale_ref, f32[4,1792]{1,0:T(4,128)S(1)} %get-tuple-element.35.refs_0_, f32[5376,2048]{1,0:T(8,128)} %get-tuple-element.36.refs_1_, ...), custom_call_target="tpu_custom_call", output_to_operand_aliasing={{0}: (3, {})} | custom-call | flops 2516582400 | bytes 3932160 | tf_op jit(solution)/shard_map/scores_far/pallas_call | solution.py:239
  63.0 10.2 %all_to_all.5.stats_ref = f32[8,4,2048]{2,1,0:T(4,128)} all-to-all(f32[8,4,2048]{2,1,0:T(4,128)S(1)} %get-tuple-element.38), channel_id=1, replica_groups={{0,1,2,3,68,69,70,71},{4,5,6,7,64,65,66,67},{8,9,10,11,76,77,78,79},{12..., dimensions={0} | all-to-all | bytes 524288 | tf_op jit(solution)/shard_map/all_to_all | solution.py:434
  73.3 1.7 %join.1.own_lse_ref = f32[1,2304]{1,0:T(1,128)} custom-call(f32[8,4,2048]{2,1,0:T(4,128)} %all_to_all.5.stats_ref), custom_call_target="tpu_custom_call" | custom-call | tf_op jit(solution)/shard_map/join/pallas_call | solution.py:285
  74.9 3.9 %collective-permute-start.16 = (f32[1,2304]{1,0:T(1,128)}, f32[1,2304]{1,0:T(1,128)S(1)}, u32[]{:S(2)}, u32[]{:S(2)}) collective-permute-start(f32[1,2304]{1,0:T(1,128)} %join.1.own_lse_ref), channel_id=1, source_target_pairs={{0,32},{32,0},{8,40},{40,8},{16,48},{48,16},{24,56},{56,24},{1,33}... | collective-permute-start | bytes 27656 | tf_op jit(solution)/shard_map/ppermute | solution.py:436
  80.5 13.3 %grads_far.1 = (bf16[272,1280]{1,0:T(8,128)(2,1)}, bf16[272,1280]{1,0:T(8,128)(2,1)}, bf16[272,1280]{1,0:T(8,128)(2,1)}, bf16[272,1280]{1,0:T(8,128)(2,1)}) custom-call(s32[32]{0:T(128)} %copy-done.10, f32[1]{0:T(128)} %bitcast.7.scale_ref, f32[1,2304]{1,0:T(1,128)} %join.1.own_lse_ref, f32[1,2304]{1,0:T(1,128)} %copy-done.12, ...), custom_call_target="tpu_custom_call" | custom-call | flops 5368709120 | bytes 8388608 | tf_op jit(solution)/shard_map/grads_far/pallas_call | solution.py:373
  93.9 4.8 %collective-permute-start.18 = (bf16[272,1280]{1,0:T(8,128)(2,1)}, bf16[272,1280]{1,0:T(8,128)(2,1)S(1)}, u32[]{:S(2)}, u32[]{:S(2)}) collective-permute-start(bf16[272,1280]{1,0:T(8,128)(2,1)} %get-tuple-element.45), channel_id=1, source_target_pairs={{0,69},{32,104},{8,77},{40,112},{16,85},{48,120},{24,93},{56,96},{... | collective-permute-start | bytes 2088968 | tf_op jit(solution)/shard_map/ppermute | solution.py:415
  98.7 1.8 %collective-permute-start.20 = (bf16[272,1280]{1,0:T(8,128)(2,1)}, bf16[272,1280]{1,0:T(8,128)(2,1)S(1)}, u32[]{:S(2)}, u32[]{:S(2)}) collective-permute-start(bf16[272,1280]{1,0:T(8,128)(2,1)} %get-tuple-element.47), channel_id=1, source_target_pairs={{0,2},{32,48},{8,10},{40,56},{16,18},{48,32},{24,26},{56,40},{1,3}... | collective-permute-start | bytes 2088968 | tf_op jit(solution)/shard_map/ppermute | solution.py:415
  100.5 13.5 %grads_near.1 = (bf16[272,1280]{1,0:T(8,128)(2,1)}, bf16[272,1280]{1,0:T(8,128)(2,1)}, bf16[272,1280]{1,0:T(8,128)(2,1)}, f32[256,1280]{1,0:T(8,128)}) custom-call(s32[32]{0:T(128)} %copy-done.10, f32[1]{0:T(128)} %bitcast.8.scale_ref, f32[1,2304]{1,0:T(1,128)} %join.1.own_lse_ref, f32[1,2304]{1,0:T(1,128)} %copy-done.12, ...), custom_call_target="tpu_custom_call" | custom-call | flops 5368709120 | bytes 8388608 | tf_op jit(solution)/shard_map/grads_near/pallas_call | solution.py:373
  114.1 1.4 collective-permute-start.21
  115.4 2.0 %collective-permute-start.22 = (bf16[272,1280]{1,0:T(8,128)(2,1)}, bf16[272,1280]{1,0:T(8,128)(2,1)S(1)}, u32[]{:S(2)}, u32[]{:S(2)}) collective-permute-start(bf16[272,1280]{1,0:T(8,128)(2,1)} %get-tuple-element.49), channel_id=1, source_target_pairs={{0,3},{32,56},{8,11},{40,32},{16,19},{48,40},{24,27},{56,48},{1,0}... | collective-permute-start | bytes 2088968 | tf_op jit(solution)/shard_map/ppermute | solution.py:415
  117.6 5.4 %collective-permute-done.19 = bf16[272,1280]{1,0:T(8,128)(2,1)S(1)} collective-permute-done((bf16[272,1280]{1,0:T(8,128)(2,1)}, bf16[272,1280]{1,0:T(8,128)(2,1)S(1)}, u32[]{:S(2)}, u32[]{:S(2)}) %collective-permute-start.19) | collective-permute-done | bytes 696352 | tf_op jit(solution)/shard_map/ppermute | solution.py:415
  123.3 6.8 %collective-permute-done.21 = bf16[272,1280]{1,0:T(8,128)(2,1)S(1)} collective-permute-done((bf16[272,1280]{1,0:T(8,128)(2,1)}, bf16[272,1280]{1,0:T(8,128)(2,1)S(1)}, u32[]{:S(2)}, u32[]{:S(2)}) %collective-permute-start.21) | collective-permute-done | bytes 696352 | tf_op jit(solution)/shard_map/ppermute | solution.py:415
  130.7 1.1 copy-done.11
  133.4 2.1 %collective-permute-done.24 = f32[136,1280]{1,0:T(8,128)S(1)} collective-permute-done((f32[136,1280]{1,0:T(8,128)S(1)}, f32[136,1280]{1,0:T(8,128)S(1)}, u32[]{:S(2)}, u32[]{:S(2)}) %collective-permute-start.24) | collective-permute-done | bytes 696352 | tf_op jit(solution)/shard_map/ppermute | solution.py:451
  136.7 1.2 slice_select_fusion
  (78 shorter events, 9.4 us)
Async XLA Ops:
  1.7 2.8 %collective-permute-start = (bf16[128,1280]{1,0:T(8,128)(2,1)S(1)}, bf16[128,1280]{1,0:T(8,128)(2,1)S(1)}, u32[]{:S(2)}, u32[]{:S(2)}) collective-permute-start(bf16[128,1280]{1,0:T(8,128)(2,1)S(1)} %broadcast_select_fusion.2), channel_id=1, source_target_pairs={{0,32},{32,0},{8,40},{40,8},{16,48},{48,16},{24,56},{56,24},{1,33}... | collective-permute-start | bytes 983048 | tf_op jit(solution)/shard_map/ppermute | solution.py:417
  5.5 28.5 %copy-start.7 = (bf16[256,1280]{1,0:T(8,128)(2,1)}, bf16[256,1280]{1,0:T(8,128)(2,1)S(1)}, u32[]{:S(2)}) copy-start(bf16[256,1280]{1,0:T(8,128)(2,1)S(1)} %pad_maximum_fusion.1.refs_0_.refs_2_) | copy-start | bytes 1966084
  5.5 9.9 %collective-permute-start.3 = (bf16[256,1280]{1,0:T(8,128)(2,1)S(1)}, bf16[256,1280]{1,0:T(8,128)(2,1)}, u32[]{:S(2)}, u32[]{:S(2)}) collective-permute-start(bf16[256,1280]{1,0:T(8,128)(2,1)S(1)} %pad_maximum_fusion.1.refs_0_.refs_2_), channel_id=1, source_target_pairs={{0,68},{32,96},{8,76},{40,104},{16,84},{48,112},{24,92},{56,120},{... | collective-permute-start | bytes 1966088 | tf_op jit(solution)/shard_map/ppermute | solution.py:415
  6.9 12.1 %collective-permute-start.2 = (bf16[256,1280]{1,0:T(8,128)(2,1)S(1)}, bf16[256,1280]{1,0:T(8,128)(2,1)}, u32[]{:S(2)}, u32[]{:S(2)}) collective-permute-start(bf16[256,1280]{1,0:T(8,128)(2,1)S(1)} %pad_maximum_fusion.1.refs_0_.refs_2_), channel_id=1, source_target_pairs={{0,1},{32,40},{8,9},{40,48},{16,17},{48,56},{24,25},{56,32},{1,2},... | collective-permute-start | bytes 1966088 | tf_op jit(solution)/shard_map/ppermute | solution.py:415
  8.5 12.2 %collective-permute-start.1 = (bf16[256,1280]{1,0:T(8,128)(2,1)S(1)}, bf16[256,1280]{1,0:T(8,128)(2,1)}, u32[]{:S(2)}, u32[]{:S(2)}) collective-permute-start(bf16[256,1280]{1,0:T(8,128)(2,1)S(1)} %pad_maximum_fusion.1.refs_0_.refs_2_), channel_id=1, source_target_pairs={{0,3},{32,56},{8,11},{40,32},{16,19},{48,40},{24,27},{56,48},{1,0}... | collective-permute-start | bytes 1966088 | tf_op jit(solution)/shard_map/ppermute | solution.py:415
  10.7 12.1 %collective-permute-start.4 = (bf16[256,1280]{1,0:T(8,128)(2,1)S(1)}, bf16[256,1280]{1,0:T(8,128)(2,1)S(1)}, u32[]{:S(2)}, u32[]{:S(2)}) collective-permute-start(bf16[256,1280]{1,0:T(8,128)(2,1)S(1)} %pad_maximum_fusion.1.refs_0_.refs_2_), channel_id=1, source_target_pairs={{0,32},{32,0},{8,40},{40,8},{16,48},{48,16},{24,56},{56,24},{1,33}... | collective-permute-start | bytes 1966088 | tf_op jit(solution)/shard_map/ppermute | solution.py:424
  15.4 7.3 %collective-permute-start.7 = (bf16[256,1280]{1,0:T(8,128)(2,1)}, bf16[256,1280]{1,0:T(8,128)(2,1)S(1)}, u32[]{:S(2)}, u32[]{:S(2)}) collective-permute-start(bf16[256,1280]{1,0:T(8,128)(2,1)} %collective-permute-done.3.refs_3_.refs_5_), channel_id=1, source_target_pairs={{0,32},{32,0},{8,40},{40,8},{16,48},{48,16},{24,56},{56,24},{1,33}... | collective-permute-start | bytes 1966088 | tf_op jit(solution)/shard_map/ppermute | solution.py:424
  19.0 7.4 %collective-permute-start.6 = (bf16[256,1280]{1,0:T(8,128)(2,1)}, bf16[256,1280]{1,0:T(8,128)(2,1)S(1)}, u32[]{:S(2)}, u32[]{:S(2)}) collective-permute-start(bf16[256,1280]{1,0:T(8,128)(2,1)} %collective-permute-done.2.refs_2_.refs_4_), channel_id=1, source_target_pairs={{0,32},{32,0},{8,40},{40,8},{16,48},{48,16},{24,56},{56,24},{1,33}... | collective-permute-start | bytes 1966088 | tf_op jit(solution)/shard_map/ppermute | solution.py:424
  20.7 5.7 %collective-permute-start.5 = (bf16[256,1280]{1,0:T(8,128)(2,1)}, bf16[256,1280]{1,0:T(8,128)(2,1)S(1)}, u32[]{:S(2)}, u32[]{:S(2)}) collective-permute-start(bf16[256,1280]{1,0:T(8,128)(2,1)} %collective-permute-done.1.refs_1_.refs_3_), channel_id=1, source_target_pairs={{0,32},{32,0},{8,40},{40,8},{16,48},{48,16},{24,56},{56,24},{1,33}... | collective-permute-start | bytes 1966088 | tf_op jit(solution)/shard_map/ppermute | solution.py:424
  21.1 12.9 %collective-permute-start.9 = (bf16[256,1280]{1,0:T(8,128)(2,1)}, bf16[256,1280]{1,0:T(8,128)(2,1)}, u32[]{:S(2)}, u32[]{:S(2)}) collective-permute-start(bf16[256,1280]{1,0:T(8,128)(2,1)} %collective-permute-done.3.refs_3_.refs_5_), channel_id=1, source_target_pairs={{0,1},{32,40},{8,9},{40,48},{16,17},{48,56},{24,25},{56,32},{1,2},... | collective-permute-start | bytes 1966088 | tf_op jit(solution)/shard_map/ppermute | solution.py:415
  22.7 32.0 %copy-start = (bf16[256,1280]{1,0:T(8,128)(2,1)}, bf16[256,1280]{1,0:T(8,128)(2,1)S(1)}, u32[]{:S(2)}) copy-start(bf16[256,1280]{1,0:T(8,128)(2,1)S(1)} %collective-permute-done.4.refs_4_.refs_9_.refs_10_.refs_0_) | copy-start | bytes 1966084
  22.7 11.3 %collective-permute-start.10 = (bf16[256,1280]{1,0:T(8,128)(2,1)}, bf16[256,1280]{1,0:T(8,128)(2,1)}, u32[]{:S(2)}, u32[]{:S(2)}) collective-permute-start(bf16[256,1280]{1,0:T(8,128)(2,1)} %collective-permute-done.1.refs_1_.refs_3_), channel_id=1, source_target_pairs={{0,68},{32,96},{8,76},{40,104},{16,84},{48,112},{24,92},{56,120},{... | collective-permute-start | bytes 1966088 | tf_op jit(solution)/shard_map/ppermute | solution.py:415
  22.7 32.0 %copy-start.1 = (bf16[256,1280]{1,0:T(8,128)(2,1)}, bf16[256,1280]{1,0:T(8,128)(2,1)S(1)}, u32[]{:S(2)}) copy-start(bf16[256,1280]{1,0:T(8,128)(2,1)S(1)} %collective-permute-done.7.refs_7_.refs_12_.refs_13_.refs_3_) | copy-start | bytes 1966084
  22.8 11.3 %collective-permute-start.8 = (bf16[256,1280]{1,0:T(8,128)(2,1)}, bf16[256,1280]{1,0:T(8,128)(2,1)}, u32[]{:S(2)}, u32[]{:S(2)}) collective-permute-start(bf16[256,1280]{1,0:T(8,128)(2,1)} %collective-permute-done.1.refs_1_.refs_3_), channel_id=1, source_target_pairs={{0,3},{32,56},{8,11},{40,32},{16,19},{48,40},{24,27},{56,48},{1,0}... | collective-permute-start | bytes 1966088 | tf_op jit(solution)/shard_map/ppermute | solution.py:415
  26.4 28.3 %copy-start.10 = (s32[32]{0:T(128)}, s32[32]{0:T(128)S(1)}, u32[]{:S(2)}) copy-start(s32[32]{0:T(128)S(1)} %dynamic-slice_bitcast_fusion.table_ref) | copy-start | bytes 388
  26.4 28.3 %copy-start.2 = (bf16[256,1280]{1,0:T(8,128)(2,1)}, bf16[256,1280]{1,0:T(8,128)(2,1)S(1)}, u32[]{:S(2)}) copy-start(bf16[256,1280]{1,0:T(8,128)(2,1)S(1)} %collective-permute-done.6.refs_6_.refs_11_.refs_12_.refs_2_) | copy-start | bytes 1966084
  26.4 28.3 %copy-start.3 = (bf16[256,1280]{1,0:T(8,128)(2,1)}, bf16[256,1280]{1,0:T(8,128)(2,1)S(1)}, u32[]{:S(2)}) copy-start(bf16[256,1280]{1,0:T(8,128)(2,1)S(1)} %collective-permute-done.5.refs_5_.refs_10_.refs_11_.refs_1_) | copy-start | bytes 1966084
  34.0 5.0 %collective-permute-start.11 = (bf16[256,1280]{1,0:T(8,128)(2,1)}, bf16[256,1280]{1,0:T(8,128)(2,1)S(1)}, u32[]{:S(2)}, u32[]{:S(2)}) collective-permute-start(bf16[256,1280]{1,0:T(8,128)(2,1)} %collective-permute-done.8.refs_6_), channel_id=1, source_target_pairs={{0,32},{32,0},{8,40},{40,8},{16,48},{48,16},{24,56},{56,24},{1,33}... | collective-permute-start | bytes 1966088 | tf_op jit(solution)/shard_map/ppermute | solution.py:428
  34.8 4.3 %collective-permute-start.12 = (bf16[256,1280]{1,0:T(8,128)(2,1)}, bf16[256,1280]{1,0:T(8,128)(2,1)S(1)}, u32[]{:S(2)}, u32[]{:S(2)}) collective-permute-start(bf16[256,1280]{1,0:T(8,128)(2,1)} %collective-permute-done.9.refs_7_), channel_id=1, source_target_pairs={{0,32},{32,0},{8,40},{40,8},{16,48},{48,16},{24,56},{56,24},{1,33}... | collective-permute-start | bytes 1966088 | tf_op jit(solution)/shard_map/ppermute | solution.py:428
  34.8 4.3 %collective-permute-start.13 = (bf16[256,1280]{1,0:T(8,128)(2,1)}, bf16[256,1280]{1,0:T(8,128)(2,1)S(1)}, u32[]{:S(2)}, u32[]{:S(2)}) collective-permute-start(bf16[256,1280]{1,0:T(8,128)(2,1)} %collective-permute-done.10.refs_8_), channel_id=1, source_target_pairs={{0,32},{32,0},{8,40},{40,8},{16,48},{48,16},{24,56},{56,24},{1,33}... | collective-permute-start | bytes 1966088 | tf_op jit(solution)/shard_map/ppermute | solution.py:428
  35.3 17.2 %collective-permute-start.14 = (bf16[256,1280]{1,0:T(8,128)(2,1)}, bf16[256,1280]{1,0:T(8,128)(2,1)S(1)}, u32[]{:S(2)}, u32[]{:S(2)}) collective-permute-start(bf16[256,1280]{1,0:T(8,128)(2,1)} %collective-permute-done.10.refs_8_), channel_id=1, source_target_pairs={{0,3},{32,56},{8,11},{40,32},{16,19},{48,40},{24,27},{56,48},{1,0}... | collective-permute-start | bytes 1966088 | tf_op jit(solution)/shard_map/ppermute | solution.py:415
  39.1 15.7 %copy-start.5 = (bf16[256,1280]{1,0:T(8,128)(2,1)}, bf16[256,1280]{1,0:T(8,128)(2,1)S(1)}, u32[]{:S(2)}) copy-start(bf16[256,1280]{1,0:T(8,128)(2,1)S(1)} %collective-permute-done.12.refs_14_.refs_15_.refs_5_) | copy-start | bytes 1966084
  52.5 2.2 %collective-permute-start.15 = (bf16[256,1280]{1,0:T(8,128)(2,1)S(1)}, bf16[256,1280]{1,0:T(8,128)(2,1)S(1)}, u32[]{:S(2)}, u32[]{:S(2)}) collective-permute-start(bf16[256,1280]{1,0:T(8,128)(2,1)S(1)} %collective-permute-done.14.refs_9_), channel_id=1, source_target_pairs={{0,32},{32,0},{8,40},{40,8},{16,48},{48,16},{24,56},{56,24},{1,33}... | collective-permute-start | bytes 1966088 | tf_op jit(solution)/shard_map/ppermute | solution.py:431
  74.9 5.0 %collective-permute-start.16 = (f32[1,2304]{1,0:T(1,128)}, f32[1,2304]{1,0:T(1,128)S(1)}, u32[]{:S(2)}, u32[]{:S(2)}) collective-permute-start(f32[1,2304]{1,0:T(1,128)} %join.1.own_lse_ref), channel_id=1, source_target_pairs={{0,32},{32,0},{8,40},{40,8},{16,48},{48,16},{24,56},{56,24},{1,33}... | collective-permute-start | bytes 27656 | tf_op jit(solution)/shard_map/ppermute | solution.py:436
  93.8 20.2 %collective-permute-start.17 = (bf16[272,1280]{1,0:T(8,128)(2,1)}, bf16[272,1280]{1,0:T(8,128)(2,1)S(1)}, u32[]{:S(2)}, u32[]{:S(2)}) collective-permute-start(bf16[272,1280]{1,0:T(8,128)(2,1)} %get-tuple-element.40), channel_id=1, source_target_pairs={{0,70},{32,112},{8,78},{40,120},{16,86},{48,96},{24,94},{56,104},{... | collective-permute-start | bytes 2088968 | tf_op jit(solution)/shard_map/ppermute | solution.py:415
  93.9 23.5 %collective-permute-start.18 = (bf16[272,1280]{1,0:T(8,128)(2,1)}, bf16[272,1280]{1,0:T(8,128)(2,1)S(1)}, u32[]{:S(2)}, u32[]{:S(2)}) collective-permute-start(bf16[272,1280]{1,0:T(8,128)(2,1)} %get-tuple-element.45), channel_id=1, source_target_pairs={{0,69},{32,104},{8,77},{40,112},{16,85},{48,120},{24,93},{56,96},{... | collective-permute-start | bytes 2088968 | tf_op jit(solution)/shard_map/ppermute | solution.py:415
  98.7 24.3 %collective-permute-start.19 = (bf16[272,1280]{1,0:T(8,128)(2,1)}, bf16[272,1280]{1,0:T(8,128)(2,1)S(1)}, u32[]{:S(2)}, u32[]{:S(2)}) collective-permute-start(bf16[272,1280]{1,0:T(8,128)(2,1)} %get-tuple-element.46), channel_id=1, source_target_pairs={{0,71},{32,120},{8,79},{40,96},{16,87},{48,104},{24,95},{56,112},{... | collective-permute-start | bytes 2088968 | tf_op jit(solution)/shard_map/ppermute | solution.py:415
  98.7 24.4 %collective-permute-start.20 = (bf16[272,1280]{1,0:T(8,128)(2,1)}, bf16[272,1280]{1,0:T(8,128)(2,1)S(1)}, u32[]{:S(2)}, u32[]{:S(2)}) collective-permute-start(bf16[272,1280]{1,0:T(8,128)(2,1)} %get-tuple-element.47), channel_id=1, source_target_pairs={{0,2},{32,48},{8,10},{40,56},{16,18},{48,32},{24,26},{56,40},{1,3}... | collective-permute-start | bytes 2088968 | tf_op jit(solution)/shard_map/ppermute | solution.py:415
  114.1 16.0 %collective-permute-start.21 = (bf16[272,1280]{1,0:T(8,128)(2,1)}, bf16[272,1280]{1,0:T(8,128)(2,1)S(1)}, u32[]{:S(2)}, u32[]{:S(2)}) collective-permute-start(bf16[272,1280]{1,0:T(8,128)(2,1)} %get-tuple-element.48), channel_id=1, source_target_pairs={{0,68},{32,96},{8,76},{40,104},{16,84},{48,112},{24,92},{56,120},{... | collective-permute-start | bytes 2088968 | tf_op jit(solution)/shard_map/ppermute | solution.py:415
  115.4 15.0 %collective-permute-start.22 = (bf16[272,1280]{1,0:T(8,128)(2,1)}, bf16[272,1280]{1,0:T(8,128)(2,1)S(1)}, u32[]{:S(2)}, u32[]{:S(2)}) collective-permute-start(bf16[272,1280]{1,0:T(8,128)(2,1)} %get-tuple-element.49), channel_id=1, source_target_pairs={{0,3},{32,56},{8,11},{40,32},{16,19},{48,40},{24,27},{56,48},{1,0}... | collective-permute-start | bytes 2088968 | tf_op jit(solution)/shard_map/ppermute | solution.py:415
  117.4 13.2 %collective-permute-start.23 = (bf16[272,1280]{1,0:T(8,128)(2,1)}, bf16[272,1280]{1,0:T(8,128)(2,1)S(1)}, u32[]{:S(2)}, u32[]{:S(2)}) collective-permute-start(bf16[272,1280]{1,0:T(8,128)(2,1)} %get-tuple-element.50), channel_id=1, source_target_pairs={{0,1},{32,40},{8,9},{40,48},{16,17},{48,56},{24,25},{56,32},{1,2},... | collective-permute-start | bytes 2088968 | tf_op jit(solution)/shard_map/ppermute | solution.py:415
  133.3 2.2 %collective-permute-start.24 = (f32[136,1280]{1,0:T(8,128)S(1)}, f32[136,1280]{1,0:T(8,128)S(1)}, u32[]{:S(2)}, u32[]{:S(2)}) collective-permute-start(f32[136,1280]{1,0:T(8,128)S(1)} %pad_maximum_fusion), channel_id=1, source_target_pairs={{0,32},{32,0},{8,40},{40,8},{16,48},{48,16},{24,56},{56,24},{1,33}... | collective-permute-start | bytes 2088968 | tf_op jit(solution)/shard_map/ppermute | solution.py:451
  (6 other events, 43.1 us)

commit v4 on v3

--- a/solution.py
+++ b/solution.py
@@ -173,10 +173,14 @@
         line[1:2, :] = power
         line[2:3, :] = weighted
         if last:
+            columns = pl.ds(table_place(table_ref, 0, piece), ROWS)
+            lse, mean = top + jnp.log2(power), weighted / power
+            line[4:5, :] += line[3:4, :]
             for member in range(8):
-                stats_ref[member, :, pl.ds(table_place(table_ref, 0, piece), ROWS)] = line[...]
+                stats_ref[member, 0:1, columns] = lse
+                stats_ref[member, 1:2, columns] = mean
         else:
-            stats_ref[:, piece_rows(piece)] = line[...]
+            stats_ref[:, piece_rows(piece)] = line[0:4, :]
 
     def part(at, size):
         if new == 1:
@@ -210,6 +214,7 @@
         line[3:4, :] = earlier[3:4] + line[3:4, :]
         put(k, new_top, earlier[1:2] * old_shrink + power * new_shrink, earlier[2:3] * old_shrink + weighted * new_shrink)
 
+    line[4:5, :] = jnp.zeros((1, ROWS), jnp.float32)
     for copy in load_own[old:] + (load_other if new > 1 else []):
         copy.wait()
     if new == 1:
@@ -226,6 +231,10 @@
         pl.loop(0, old)(lambda k: old_stats(k, *old_scores(k)))
     for k in range(old):
         store_old(k).wait()
+    if last:
+        matched = jnp.broadcast_to(jnp.sum(line[4:5, :], axis=1, keepdims=True), (2, 128))
+        for member in range(8):
+            stats_ref[member, :, total * ROWS :] = matched
     for k in range(new):
         store_new(k).wait()
 
@@ -242,14 +251,14 @@
         out_specs=[anywhere, vmem],
         out_shape=[
             jax.ShapeDtypeStruct((8 * ROWS + SPARE, 8 * ROWS), jnp.float32),
-            jax.ShapeDtypeStruct((8, 4, total * ROWS) if last else (4, total * ROWS), jnp.float32),
+            jax.ShapeDtypeStruct((8, 2, total * ROWS + 128) if last else (4, total * ROWS), jnp.float32),
         ],
         scratch_shapes=[
             pltpu.VMEM((total * ROWS, width), jnp.bfloat16),
             pltpu.VMEM((total * ROWS, width), jnp.bfloat16),
             pltpu.VMEM((new * ROWS, total * ROWS), jnp.float32),
             pltpu.VMEM((max(old, 1) * ROWS, new * ROWS), jnp.float32),
-            pltpu.VMEM((4, ROWS), jnp.float32),
+            pltpu.VMEM((8, ROWS), jnp.float32),
             pltpu.SemaphoreType.DMA((total,)),
             pltpu.SemaphoreType.DMA((total,)),
             pltpu.SemaphoreType.DMA((total,)),
@@ -267,24 +276,24 @@
 
 def join_kernel(shift, stats_ref, out_ref):
     rows = out_ref.shape[1] - 256
-    peak = functools.reduce(jnp.maximum, [stats_ref[k, 0:1, :] for k in range(8)])
+    peak = functools.reduce(jnp.maximum, [stats_ref[k, 0:1, :rows] for k in range(8)])
     total = weighted = matched = 0.0
     for k in range(8):
-        shrink = jnp.exp2(stats_ref[k, 0:1, :] - peak)
-        total = total + stats_ref[k, 1:2, :] * shrink
-        weighted = weighted + stats_ref[k, 2:3, :] * shrink
-        matched = matched + stats_ref[k, 3:4, :]
+        power = jnp.exp2(stats_ref[k, 0:1, :rows] - peak)
+        total = total + power
+        weighted = weighted + stats_ref[k, 1:2, :rows] * power
+        matched = matched + stats_ref[k, 0:1, rows:]
     lse = peak + jnp.log2(total)
     out_ref[:, :rows] = lse + shift
-    for k, value in enumerate((lse - matched, weighted / total - matched)):
+    for k, value in enumerate((lse, weighted / total)):
         value = jnp.sum(value, axis=1, keepdims=True)
-        out_ref[:, rows + 128 * k : rows + 128 * (k + 1)] = jnp.broadcast_to(value, (1, 128))
+        out_ref[:, rows + 128 * k : rows + 128 * (k + 1)] = jnp.broadcast_to(value, (1, 128)) - matched
 
 
 def join_call(shift, stats):
     return pl.pallas_call(
         functools.partial(join_kernel, shift),
-        out_shape=jax.ShapeDtypeStruct((1, stats.shape[2] + 256), jnp.float32),
+        out_shape=jax.ShapeDtypeStruct((1, stats.shape[2] + 128), jnp.float32),
         name="join",
     )(stats)
 

time: 139 us -> 139 us (level)
  no operation moved by 1% of the time
where the time goes in v4:
time: 139 us; the launch traced here: 138 us
  Pallas kernels  56.2 us (40%)
  starting transfers between devices  35.6 us (26%)
  waiting for transfers between devices  23.6 us (17%)
  blocking collectives  9.63 us (7%)
  other arithmetic  5.42 us (4%)
  local copies, waits for them, and re-layouts  4.57 us (3%)
  between operations  3.44 us (2%)
    pallas_call x3, Pallas kernels, score_call(): pl.pallas_call(functools.partial(score_kernel, old, new, last), in_specs=...  27.7 us
    pallas_call x2, Pallas kernels, grad_call(): pl.pallas_call(functools.partial(grad_kernel, pairs, pieces), grid=(count...  26.8 us
    ppermute x14, starting transfers between devices, send(): return lax.ppermute(value, AXES, ring_perm(steps, pair))  22.8 us
    ppermute x14, waiting for transfers between devices, send(): return lax.ppermute(value, AXES, ring_perm(steps, pair))  17 us
    all_to_all x1, blocking collectives, on_device(): lax.all_to_all(stats, AXES, 0, 0, axis_index_groups=members, tiled=True)  9.63 us
    ppermute x4, starting transfers between devices, on_device(): other = [swap(v) for v in own]  5.89 us
    ppermute x1, starting transfers between devices, on_device(): other_lse = swap(own_lse)  3.95 us
    unnamed x26, local copies, waits for them, and re-layouts  3.35 us
  transfers between devices with their start and end apart: 25, of which 9 were waited for; matrix products, arithmetic and copies ran while one was open for 1% of the time, Pallas kernels for 24%

profile of v4, /device:TPU:1, one launch (start us, length us, event | category | flops | bytes accessed | tf_op | source)
XLA Modules:
  0.0 138.4 jit_solution(13198308652916511286)
XLA Ops:
  1.7 1.5 %collective-permute-start = (bf16[128,1280]{1,0:T(8,128)(2,1)S(1)}, bf16[128,1280]{1,0:T(8,128)(2,1)S(1)}, u32[]{:S(2)}, u32[]{:S(2)}) collective-permute-start(bf16[128,1280]{1,0:T(8,128)(2,1)S(1)} %broadcast_select_fusion.2), channel_id=1, source_target_pairs={{0,32},{32,0},{8,40},{40,8},{16,48},{48,16},{24,56},{56,24},{1,33}... | collective-permute-start | bytes 983048 | tf_op jit(solution)/shard_map/ppermute | solution.py:426
  3.2 1.3 collective-permute-done
  5.5 1.4 collective-permute-start.3
  6.9 1.6 %collective-permute-start.2 = (bf16[256,1280]{1,0:T(8,128)(2,1)S(1)}, bf16[256,1280]{1,0:T(8,128)(2,1)}, u32[]{:S(2)}, u32[]{:S(2)}) collective-permute-start(bf16[256,1280]{1,0:T(8,128)(2,1)S(1)} %pad_maximum_fusion.1.refs_0_.refs_2_), channel_id=1, source_target_pairs={{0,1},{32,40},{8,9},{40,48},{16,17},{48,56},{24,25},{56,32},{1,2},... | collective-permute-start | bytes 1966088 | tf_op jit(solution)/shard_map/ppermute | solution.py:424
  8.5 2.1 %collective-permute-start.1 = (bf16[256,1280]{1,0:T(8,128)(2,1)S(1)}, bf16[256,1280]{1,0:T(8,128)(2,1)}, u32[]{:S(2)}, u32[]{:S(2)}) collective-permute-start(bf16[256,1280]{1,0:T(8,128)(2,1)S(1)} %pad_maximum_fusion.1.refs_0_.refs_2_), channel_id=1, source_target_pairs={{0,3},{32,56},{8,11},{40,32},{16,19},{48,40},{24,27},{56,48},{1,0}... | collective-permute-start | bytes 1966088 | tf_op jit(solution)/shard_map/ppermute | solution.py:424
  10.7 1.4 %collective-permute-start.4 = (bf16[256,1280]{1,0:T(8,128)(2,1)S(1)}, bf16[256,1280]{1,0:T(8,128)(2,1)S(1)}, u32[]{:S(2)}, u32[]{:S(2)}) collective-permute-start(bf16[256,1280]{1,0:T(8,128)(2,1)S(1)} %pad_maximum_fusion.1.refs_0_.refs_2_), channel_id=1, source_target_pairs={{0,32},{32,0},{8,40},{40,8},{16,48},{48,16},{24,56},{56,24},{1,33}... | collective-permute-start | bytes 1966088 | tf_op jit(solution)/shard_map/ppermute | solution.py:433
  12.1 3.4 %collective-permute-done.3.refs_3_.refs_5_ = bf16[256,1280]{1,0:T(8,128)(2,1)} collective-permute-done((bf16[256,1280]{1,0:T(8,128)(2,1)S(1)}, bf16[256,1280]{1,0:T(8,128)(2,1)}, u32[]{:S(2)}, u32[]{:S(2)}) %collective-permute-start.3) | collective-permute-done | bytes 655392 | tf_op jit(solution)/shard_map/ppermute | solution.py:424
  15.4 2.4 %collective-permute-start.7 = (bf16[256,1280]{1,0:T(8,128)(2,1)}, bf16[256,1280]{1,0:T(8,128)(2,1)S(1)}, u32[]{:S(2)}, u32[]{:S(2)}) collective-permute-start(bf16[256,1280]{1,0:T(8,128)(2,1)} %collective-permute-done.3.refs_3_.refs_5_), channel_id=1, source_target_pairs={{0,32},{32,0},{8,40},{40,8},{16,48},{48,16},{24,56},{56,24},{1,33}... | collective-permute-start | bytes 1966088 | tf_op jit(solution)/shard_map/ppermute | solution.py:433
  17.9 1.1 collective-permute-done.2.refs_2_.refs_4_
  19.0 1.7 %collective-permute-start.6 = (bf16[256,1280]{1,0:T(8,128)(2,1)}, bf16[256,1280]{1,0:T(8,128)(2,1)S(1)}, u32[]{:S(2)}, u32[]{:S(2)}) collective-permute-start(bf16[256,1280]{1,0:T(8,128)(2,1)} %collective-permute-done.2.refs_2_.refs_4_), channel_id=1, source_target_pairs={{0,32},{32,0},{8,40},{40,8},{16,48},{48,16},{24,56},{56,24},{1,33}... | collective-permute-start | bytes 1966088 | tf_op jit(solution)/shard_map/ppermute | solution.py:433
  21.1 1.6 %collective-permute-start.9 = (bf16[256,1280]{1,0:T(8,128)(2,1)}, bf16[256,1280]{1,0:T(8,128)(2,1)}, u32[]{:S(2)}, u32[]{:S(2)}) collective-permute-start(bf16[256,1280]{1,0:T(8,128)(2,1)} %collective-permute-done.3.refs_3_.refs_5_), channel_id=1, source_target_pairs={{0,1},{32,40},{8,9},{40,48},{16,17},{48,56},{24,25},{56,32},{1,2},... | collective-permute-start | bytes 1966088 | tf_op jit(solution)/shard_map/ppermute | solution.py:424
  22.8 2.3 %collective-permute-start.8 = (bf16[256,1280]{1,0:T(8,128)(2,1)}, bf16[256,1280]{1,0:T(8,128)(2,1)}, u32[]{:S(2)}, u32[]{:S(2)}) collective-permute-start(bf16[256,1280]{1,0:T(8,128)(2,1)} %collective-permute-done.1.refs_1_.refs_3_), channel_id=1, source_target_pairs={{0,3},{32,56},{8,11},{40,32},{16,19},{48,40},{24,27},{56,48},{1,0}... | collective-permute-start | bytes 1966088 | tf_op jit(solution)/shard_map/ppermute | solution.py:424
  26.4 7.6 %scores_near.1 = (f32[5376,2048]{1,0:T(8,128)}, f32[4,1024]{1,0:T(4,128)S(1)}) custom-call(s32[32]{0:T(128)S(1)} %dynamic-slice_bitcast_fusion.table_ref, f32[1]{0:T(128)} %bitcast.2.scale_ref, bf16[256,1280]{1,0:T(8,128)(2,1)S(1)} %pad_maximum_fusion.1.refs_0_.refs_2_, bf16[256,1280]{1,0:T(8,128)(2,1)} %collective-permute-done.1.refs_1_.refs_3_, ...), custom_call_target="tpu_custom_call" | custom-call | flops 2684354560 | bytes 4194304 | tf_op jit(solution)/shard_map/scores_near/pallas_call | solution.py:248
  35.3 3.8 %collective-permute-start.14 = (bf16[256,1280]{1,0:T(8,128)(2,1)}, bf16[256,1280]{1,0:T(8,128)(2,1)S(1)}, u32[]{:S(2)}, u32[]{:S(2)}) collective-permute-start(bf16[256,1280]{1,0:T(8,128)(2,1)} %collective-permute-done.10.refs_8_), channel_id=1, source_target_pairs={{0,3},{32,56},{8,11},{40,32},{16,19},{48,40},{24,27},{56,48},{1,0}... | collective-permute-start | bytes 1966088 | tf_op jit(solution)/shard_map/ppermute | solution.py:424
  39.1 1.6 %copy-done.8 = bf16[256,1280]{1,0:T(8,128)(2,1)S(1)} copy-done((bf16[256,1280]{1,0:T(8,128)(2,1)S(1)}, bf16[256,1280]{1,0:T(8,128)(2,1)}, u32[]{:S(2)}) %copy-start.8) | copy-done | bytes 655384
  40.7 11.8 %scores_middle.1 = (f32[5376,2048]{1,0:T(8,128)}, f32[4,1792]{1,0:T(4,128)S(1)}) custom-call(s32[32]{0:T(128)S(1)} %dynamic-slice_bitcast_fusion.table_ref, f32[1]{0:T(128)} %bitcast.2.scale_ref, f32[4,1024]{1,0:T(4,128)S(1)} %get-tuple-element.29.refs_0_, f32[5376,2048]{1,0:T(8,128)} %get-tuple-element.30.refs_1_, ...), custom_call_target="tpu_custom_call", output_to_operand_aliasing={{0}: (3, {})} | custom-call | flops 5536481280 | bytes 8650752 | tf_op jit(solution)/shard_map/scores_middle/pallas_call | solution.py:248
  52.6 2.1 %collective-permute-done.15.refs_17_.refs_7_ = bf16[256,1280]{1,0:T(8,128)(2,1)S(1)} collective-permute-done((bf16[256,1280]{1,0:T(8,128)(2,1)S(1)}, bf16[256,1280]{1,0:T(8,128)(2,1)S(1)}, u32[]{:S(2)}, u32[]{:S(2)}) %collective-permute-start.15) | collective-permute-done | bytes 655392 | tf_op jit(solution)/shard_map/ppermute | solution.py:440
  54.8 8.3 %scores_far.1 = (f32[5376,2048]{1,0:T(8,128)}, f32[8,2,2176]{2,1,0:T(2,128)S(1)}) custom-call(s32[32]{0:T(128)S(1)} %dynamic-slice_bitcast_fusion.table_ref, f32[1]{0:T(128)} %bitcast.2.scale_ref, f32[4,1792]{1,0:T(4,128)S(1)} %get-tuple-element.35.refs_0_, f32[5376,2048]{1,0:T(8,128)} %get-tuple-element.36.refs_1_, ...), custom_call_target="tpu_custom_call", output_to_operand_aliasing={{0}: (3, {})} | custom-call | flops 2516582400 | bytes 3932160 | tf_op jit(solution)/shard_map/scores_far/pallas_call | solution.py:248
  63.1 9.6 %all_to_all.5.stats_ref = f32[8,2,2176]{2,1,0:T(2,128)} all-to-all(f32[8,2,2176]{2,1,0:T(2,128)S(1)} %get-tuple-element.38), channel_id=1, replica_groups={{0,1,2,3,68,69,70,71},{4,5,6,7,64,65,66,67},{8,9,10,11,76,77,78,79},{12..., dimensions={0} | all-to-all | bytes 278528 | tf_op jit(solution)/shard_map/all_to_all | solution.py:443
  72.7 1.6 %join.1.own_lse_ref = f32[1,2304]{1,0:T(1,128)} custom-call(f32[8,2,2176]{2,1,0:T(2,128)} %all_to_all.5.stats_ref), custom_call_target="tpu_custom_call" | custom-call | tf_op jit(solution)/shard_map/join/pallas_call | solution.py:294
  74.3 4.0 %collective-permute-start.16 = (f32[1,2304]{1,0:T(1,128)}, f32[1,2304]{1,0:T(1,128)S(1)}, u32[]{:S(2)}, u32[]{:S(2)}) collective-permute-start(f32[1,2304]{1,0:T(1,128)} %join.1.own_lse_ref), channel_id=1, source_target_pairs={{0,32},{32,0},{8,40},{40,8},{16,48},{48,16},{24,56},{56,24},{1,33}... | collective-permute-start | bytes 27656 | tf_op jit(solution)/shard_map/ppermute | solution.py:445
  79.9 13.3 %grads_far.1 = (bf16[272,1280]{1,0:T(8,128)(2,1)}, bf16[272,1280]{1,0:T(8,128)(2,1)}, bf16[272,1280]{1,0:T(8,128)(2,1)}, bf16[272,1280]{1,0:T(8,128)(2,1)}) custom-call(s32[32]{0:T(128)} %copy-done.10, f32[1]{0:T(128)} %bitcast.7.scale_ref, f32[1,2304]{1,0:T(1,128)} %join.1.own_lse_ref, f32[1,2304]{1,0:T(1,128)} %copy-done.12, ...), custom_call_target="tpu_custom_call" | custom-call | flops 5368709120 | bytes 8388608 | tf_op jit(solution)/shard_map/grads_far/pallas_call | solution.py:382
  93.3 4.8 %collective-permute-start.18 = (bf16[272,1280]{1,0:T(8,128)(2,1)}, bf16[272,1280]{1,0:T(8,128)(2,1)S(1)}, u32[]{:S(2)}, u32[]{:S(2)}) collective-permute-start(bf16[272,1280]{1,0:T(8,128)(2,1)} %get-tuple-element.45), channel_id=1, source_target_pairs={{0,69},{32,104},{8,77},{40,112},{16,85},{48,120},{24,93},{56,96},{... | collective-permute-start | bytes 2088968 | tf_op jit(solution)/shard_map/ppermute | solution.py:424
  98.1 1.8 %collective-permute-start.20 = (bf16[272,1280]{1,0:T(8,128)(2,1)}, bf16[272,1280]{1,0:T(8,128)(2,1)S(1)}, u32[]{:S(2)}, u32[]{:S(2)}) collective-permute-start(bf16[272,1280]{1,0:T(8,128)(2,1)} %get-tuple-element.47), channel_id=1, source_target_pairs={{0,2},{32,48},{8,10},{40,56},{16,18},{48,32},{24,26},{56,40},{1,3}... | collective-permute-start | bytes 2088968 | tf_op jit(solution)/shard_map/ppermute | solution.py:424
  99.9 13.5 %grads_near.1 = (bf16[272,1280]{1,0:T(8,128)(2,1)}, bf16[272,1280]{1,0:T(8,128)(2,1)}, bf16[272,1280]{1,0:T(8,128)(2,1)}, f32[256,1280]{1,0:T(8,128)}) custom-call(s32[32]{0:T(128)} %copy-done.10, f32[1]{0:T(128)} %bitcast.8.scale_ref, f32[1,2304]{1,0:T(1,128)} %join.1.own_lse_ref, f32[1,2304]{1,0:T(1,128)} %copy-done.12, ...), custom_call_target="tpu_custom_call" | custom-call | flops 5368709120 | bytes 8388608 | tf_op jit(solution)/shard_map/grads_near/pallas_call | solution.py:382
  113.5 1.4 collective-permute-start.21
  114.8 2.0 %collective-permute-start.22 = (bf16[272,1280]{1,0:T(8,128)(2,1)}, bf16[272,1280]{1,0:T(8,128)(2,1)S(1)}, u32[]{:S(2)}, u32[]{:S(2)}) collective-permute-start(bf16[272,1280]{1,0:T(8,128)(2,1)} %get-tuple-element.49), channel_id=1, source_target_pairs={{0,3},{32,56},{8,11},{40,32},{16,19},{48,40},{24,27},{56,48},{1,0}... | collective-permute-start | bytes 2088968 | tf_op jit(solution)/shard_map/ppermute | solution.py:424
  117.0 5.4 %collective-permute-done.19 = bf16[272,1280]{1,0:T(8,128)(2,1)S(1)} collective-permute-done((bf16[272,1280]{1,0:T(8,128)(2,1)}, bf16[272,1280]{1,0:T(8,128)(2,1)S(1)}, u32[]{:S(2)}, u32[]{:S(2)}) %collective-permute-start.19) | collective-permute-done | bytes 696352 | tf_op jit(solution)/shard_map/ppermute | solution.py:424
  122.7 6.8 %collective-permute-done.21 = bf16[272,1280]{1,0:T(8,128)(2,1)S(1)} collective-permute-done((bf16[272,1280]{1,0:T(8,128)(2,1)}, bf16[272,1280]{1,0:T(8,128)(2,1)S(1)}, u32[]{:S(2)}, u32[]{:S(2)}) %collective-permute-start.21) | collective-permute-done | bytes 696352 | tf_op jit(solution)/shard_map/ppermute | solution.py:424
  130.1 1.1 copy-done.11
  132.8 2.1 %collective-permute-done.24 = f32[136,1280]{1,0:T(8,128)S(1)} collective-permute-done((f32[136,1280]{1,0:T(8,128)S(1)}, f32[136,1280]{1,0:T(8,128)S(1)}, u32[]{:S(2)}, u32[]{:S(2)}) %collective-permute-start.24) | collective-permute-done | bytes 696352 | tf_op jit(solution)/shard_map/ppermute | solution.py:460
  136.1 1.2 slice_select_fusion
  (78 shorter events, 9.4 us)
Async XLA Ops:
  1.7 2.8 %collective-permute-start = (bf16[128,1280]{1,0:T(8,128)(2,1)S(1)}, bf16[128,1280]{1,0:T(8,128)(2,1)S(1)}, u32[]{:S(2)}, u32[]{:S(2)}) collective-permute-start(bf16[128,1280]{1,0:T(8,128)(2,1)S(1)} %broadcast_select_fusion.2), channel_id=1, source_target_pairs={{0,32},{32,0},{8,40},{40,8},{16,48},{48,16},{24,56},{56,24},{1,33}... | collective-permute-start | bytes 983048 | tf_op jit(solution)/shard_map/ppermute | solution.py:426
  5.5 28.5 %copy-start.7 = (bf16[256,1280]{1,0:T(8,128)(2,1)}, bf16[256,1280]{1,0:T(8,128)(2,1)S(1)}, u32[]{:S(2)}) copy-start(bf16[256,1280]{1,0:T(8,128)(2,1)S(1)} %pad_maximum_fusion.1.refs_0_.refs_2_) | copy-start | bytes 1966084
  5.5 9.9 %collective-permute-start.3 = (bf16[256,1280]{1,0:T(8,128)(2,1)S(1)}, bf16[256,1280]{1,0:T(8,128)(2,1)}, u32[]{:S(2)}, u32[]{:S(2)}) collective-permute-start(bf16[256,1280]{1,0:T(8,128)(2,1)S(1)} %pad_maximum_fusion.1.refs_0_.refs_2_), channel_id=1, source_target_pairs={{0,68},{32,96},{8,76},{40,104},{16,84},{48,112},{24,92},{56,120},{... | collective-permute-start | bytes 1966088 | tf_op jit(solution)/shard_map/ppermute | solution.py:424
  6.9 12.1 %collective-permute-start.2 = (bf16[256,1280]{1,0:T(8,128)(2,1)S(1)}, bf16[256,1280]{1,0:T(8,128)(2,1)}, u32[]{:S(2)}, u32[]{:S(2)}) collective-permute-start(bf16[256,1280]{1,0:T(8,128)(2,1)S(1)} %pad_maximum_fusion.1.refs_0_.refs_2_), channel_id=1, source_target_pairs={{0,1},{32,40},{8,9},{40,48},{16,17},{48,56},{24,25},{56,32},{1,2},... | collective-permute-start | bytes 1966088 | tf_op jit(solution)/shard_map/ppermute | solution.py:424
  8.5 12.2 %collective-permute-start.1 = (bf16[256,1280]{1,0:T(8,128)(2,1)S(1)}, bf16[256,1280]{1,0:T(8,128)(2,1)}, u32[]{:S(2)}, u32[]{:S(2)}) collective-permute-start(bf16[256,1280]{1,0:T(8,128)(2,1)S(1)} %pad_maximum_fusion.1.refs_0_.refs_2_), channel_id=1, source_target_pairs={{0,3},{32,56},{8,11},{40,32},{16,19},{48,40},{24,27},{56,48},{1,0}... | collective-permute-start | bytes 1966088 | tf_op jit(solution)/shard_map/ppermute | solution.py:424
  10.7 12.1 %collective-permute-start.4 = (bf16[256,1280]{1,0:T(8,128)(2,1)S(1)}, bf16[256,1280]{1,0:T(8,128)(2,1)S(1)}, u32[]{:S(2)}, u32[]{:S(2)}) collective-permute-start(bf16[256,1280]{1,0:T(8,128)(2,1)S(1)} %pad_maximum_fusion.1.refs_0_.refs_2_), channel_id=1, source_target_pairs={{0,32},{32,0},{8,40},{40,8},{16,48},{48,16},{24,56},{56,24},{1,33}... | collective-permute-start | bytes 1966088 | tf_op jit(solution)/shard_map/ppermute | solution.py:433
  15.4 7.3 %collective-permute-start.7 = (bf16[256,1280]{1,0:T(8,128)(2,1)}, bf16[256,1280]{1,0:T(8,128)(2,1)S(1)}, u32[]{:S(2)}, u32[]{:S(2)}) collective-permute-start(bf16[256,1280]{1,0:T(8,128)(2,1)} %collective-permute-done.3.refs_3_.refs_5_), channel_id=1, source_target_pairs={{0,32},{32,0},{8,40},{40,8},{16,48},{48,16},{24,56},{56,24},{1,33}... | collective-permute-start | bytes 1966088 | tf_op jit(solution)/shard_map/ppermute | solution.py:433
  19.0 7.4 %collective-permute-start.6 = (bf16[256,1280]{1,0:T(8,128)(2,1)}, bf16[256,1280]{1,0:T(8,128)(2,1)S(1)}, u32[]{:S(2)}, u32[]{:S(2)}) collective-permute-start(bf16[256,1280]{1,0:T(8,128)(2,1)} %collective-permute-done.2.refs_2_.refs_4_), channel_id=1, source_target_pairs={{0,32},{32,0},{8,40},{40,8},{16,48},{48,16},{24,56},{56,24},{1,33}... | collective-permute-start | bytes 1966088 | tf_op jit(solution)/shard_map/ppermute | solution.py:433
  20.7 5.7 %collective-permute-start.5 = (bf16[256,1280]{1,0:T(8,128)(2,1)}, bf16[256,1280]{1,0:T(8,128)(2,1)S(1)}, u32[]{:S(2)}, u32[]{:S(2)}) collective-permute-start(bf16[256,1280]{1,0:T(8,128)(2,1)} %collective-permute-done.1.refs_1_.refs_3_), channel_id=1, source_target_pairs={{0,32},{32,0},{8,40},{40,8},{16,48},{48,16},{24,56},{56,24},{1,33}... | collective-permute-start | bytes 1966088 | tf_op jit(solution)/shard_map/ppermute | solution.py:433
  21.1 12.9 %collective-permute-start.9 = (bf16[256,1280]{1,0:T(8,128)(2,1)}, bf16[256,1280]{1,0:T(8,128)(2,1)}, u32[]{:S(2)}, u32[]{:S(2)}) collective-permute-start(bf16[256,1280]{1,0:T(8,128)(2,1)} %collective-permute-done.3.refs_3_.refs_5_), channel_id=1, source_target_pairs={{0,1},{32,40},{8,9},{40,48},{16,17},{48,56},{24,25},{56,32},{1,2},... | collective-permute-start | bytes 1966088 | tf_op jit(solution)/shard_map/ppermute | solution.py:424
  22.7 32.0 %copy-start = (bf16[256,1280]{1,0:T(8,128)(2,1)}, bf16[256,1280]{1,0:T(8,128)(2,1)S(1)}, u32[]{:S(2)}) copy-start(bf16[256,1280]{1,0:T(8,128)(2,1)S(1)} %collective-permute-done.4.refs_4_.refs_9_.refs_10_.refs_0_) | copy-start | bytes 1966084
  22.7 11.3 %collective-permute-start.10 = (bf16[256,1280]{1,0:T(8,128)(2,1)}, bf16[256,1280]{1,0:T(8,128)(2,1)}, u32[]{:S(2)}, u32[]{:S(2)}) collective-permute-start(bf16[256,1280]{1,0:T(8,128)(2,1)} %collective-permute-done.1.refs_1_.refs_3_), channel_id=1, source_target_pairs={{0,68},{32,96},{8,76},{40,104},{16,84},{48,112},{24,92},{56,120},{... | collective-permute-start | bytes 1966088 | tf_op jit(solution)/shard_map/ppermute | solution.py:424
  22.7 32.0 %copy-start.1 = (bf16[256,1280]{1,0:T(8,128)(2,1)}, bf16[256,1280]{1,0:T(8,128)(2,1)S(1)}, u32[]{:S(2)}) copy-start(bf16[256,1280]{1,0:T(8,128)(2,1)S(1)} %collective-permute-done.7.refs_7_.refs_12_.refs_13_.refs_3_) | copy-start | bytes 1966084
  22.8 11.3 %collective-permute-start.8 = (bf16[256,1280]{1,0:T(8,128)(2,1)}, bf16[256,1280]{1,0:T(8,128)(2,1)}, u32[]{:S(2)}, u32[]{:S(2)}) collective-permute-start(bf16[256,1280]{1,0:T(8,128)(2,1)} %collective-permute-done.1.refs_1_.refs_3_), channel_id=1, source_target_pairs={{0,3},{32,56},{8,11},{40,32},{16,19},{48,40},{24,27},{56,48},{1,0}... | collective-permute-start | bytes 1966088 | tf_op jit(solution)/shard_map/ppermute | solution.py:424
  26.4 28.3 %copy-start.10 = (s32[32]{0:T(128)}, s32[32]{0:T(128)S(1)}, u32[]{:S(2)}) copy-start(s32[32]{0:T(128)S(1)} %dynamic-slice_bitcast_fusion.table_ref) | copy-start | bytes 388
  26.4 28.3 %copy-start.2 = (bf16[256,1280]{1,0:T(8,128)(2,1)}, bf16[256,1280]{1,0:T(8,128)(2,1)S(1)}, u32[]{:S(2)}) copy-start(bf16[256,1280]{1,0:T(8,128)(2,1)S(1)} %collective-permute-done.6.refs_6_.refs_11_.refs_12_.refs_2_) | copy-start | bytes 1966084
  26.4 28.3 %copy-start.3 = (bf16[256,1280]{1,0:T(8,128)(2,1)}, bf16[256,1280]{1,0:T(8,128)(2,1)S(1)}, u32[]{:S(2)}) copy-start(bf16[256,1280]{1,0:T(8,128)(2,1)S(1)} %collective-permute-done.5.refs_5_.refs_10_.refs_11_.refs_1_) | copy-start | bytes 1966084
  34.1 5.0 %collective-permute-start.11 = (bf16[256,1280]{1,0:T(8,128)(2,1)}, bf16[256,1280]{1,0:T(8,128)(2,1)S(1)}, u32[]{:S(2)}, u32[]{:S(2)}) collective-permute-start(bf16[256,1280]{1,0:T(8,128)(2,1)} %collective-permute-done.8.refs_6_), channel_id=1, source_target_pairs={{0,32},{32,0},{8,40},{40,8},{16,48},{48,16},{24,56},{56,24},{1,33}... | collective-permute-start | bytes 1966088 | tf_op jit(solution)/shard_map/ppermute | solution.py:437
  34.8 4.3 %collective-permute-start.12 = (bf16[256,1280]{1,0:T(8,128)(2,1)}, bf16[256,1280]{1,0:T(8,128)(2,1)S(1)}, u32[]{:S(2)}, u32[]{:S(2)}) collective-permute-start(bf16[256,1280]{1,0:T(8,128)(2,1)} %collective-permute-done.9.refs_7_), channel_id=1, source_target_pairs={{0,32},{32,0},{8,40},{40,8},{16,48},{48,16},{24,56},{56,24},{1,33}... | collective-permute-start | bytes 1966088 | tf_op jit(solution)/shard_map/ppermute | solution.py:437
  34.8 4.3 %collective-permute-start.13 = (bf16[256,1280]{1,0:T(8,128)(2,1)}, bf16[256,1280]{1,0:T(8,128)(2,1)S(1)}, u32[]{:S(2)}, u32[]{:S(2)}) collective-permute-start(bf16[256,1280]{1,0:T(8,128)(2,1)} %collective-permute-done.10.refs_8_), channel_id=1, source_target_pairs={{0,32},{32,0},{8,40},{40,8},{16,48},{48,16},{24,56},{56,24},{1,33}... | collective-permute-start | bytes 1966088 | tf_op jit(solution)/shard_map/ppermute | solution.py:437
  35.3 17.2 %collective-permute-start.14 = (bf16[256,1280]{1,0:T(8,128)(2,1)}, bf16[256,1280]{1,0:T(8,128)(2,1)S(1)}, u32[]{:S(2)}, u32[]{:S(2)}) collective-permute-start(bf16[256,1280]{1,0:T(8,128)(2,1)} %collective-permute-done.10.refs_8_), channel_id=1, source_target_pairs={{0,3},{32,56},{8,11},{40,32},{16,19},{48,40},{24,27},{56,48},{1,0}... | collective-permute-start | bytes 1966088 | tf_op jit(solution)/shard_map/ppermute | solution.py:424
  39.1 15.7 %copy-start.5 = (bf16[256,1280]{1,0:T(8,128)(2,1)}, bf16[256,1280]{1,0:T(8,128)(2,1)S(1)}, u32[]{:S(2)}) copy-start(bf16[256,1280]{1,0:T(8,128)(2,1)S(1)} %collective-permute-done.12.refs_14_.refs_15_.refs_5_) | copy-start | bytes 1966084
  52.5 2.2 %collective-permute-start.15 = (bf16[256,1280]{1,0:T(8,128)(2,1)S(1)}, bf16[256,1280]{1,0:T(8,128)(2,1)S(1)}, u32[]{:S(2)}, u32[]{:S(2)}) collective-permute-start(bf16[256,1280]{1,0:T(8,128)(2,1)S(1)} %collective-permute-done.14.refs_9_), channel_id=1, source_target_pairs={{0,32},{32,0},{8,40},{40,8},{16,48},{48,16},{24,56},{56,24},{1,33}... | collective-permute-start | bytes 1966088 | tf_op jit(solution)/shard_map/ppermute | solution.py:440
  74.3 5.0 %collective-permute-start.16 = (f32[1,2304]{1,0:T(1,128)}, f32[1,2304]{1,0:T(1,128)S(1)}, u32[]{:S(2)}, u32[]{:S(2)}) collective-permute-start(f32[1,2304]{1,0:T(1,128)} %join.1.own_lse_ref), channel_id=1, source_target_pairs={{0,32},{32,0},{8,40},{40,8},{16,48},{48,16},{24,56},{56,24},{1,33}... | collective-permute-start | bytes 27656 | tf_op jit(solution)/shard_map/ppermute | solution.py:445
  93.3 20.2 %collective-permute-start.17 = (bf16[272,1280]{1,0:T(8,128)(2,1)}, bf16[272,1280]{1,0:T(8,128)(2,1)S(1)}, u32[]{:S(2)}, u32[]{:S(2)}) collective-permute-start(bf16[272,1280]{1,0:T(8,128)(2,1)} %get-tuple-element.40), channel_id=1, source_target_pairs={{0,70},{32,112},{8,78},{40,120},{16,86},{48,96},{24,94},{56,104},{... | collective-permute-start | bytes 2088968 | tf_op jit(solution)/shard_map/ppermute | solution.py:424
  93.3 23.5 %collective-permute-start.18 = (bf16[272,1280]{1,0:T(8,128)(2,1)}, bf16[272,1280]{1,0:T(8,128)(2,1)S(1)}, u32[]{:S(2)}, u32[]{:S(2)}) collective-permute-start(bf16[272,1280]{1,0:T(8,128)(2,1)} %get-tuple-element.45), channel_id=1, source_target_pairs={{0,69},{32,104},{8,77},{40,112},{16,85},{48,120},{24,93},{56,96},{... | collective-permute-start | bytes 2088968 | tf_op jit(solution)/shard_map/ppermute | solution.py:424
  98.1 24.3 %collective-permute-start.19 = (bf16[272,1280]{1,0:T(8,128)(2,1)}, bf16[272,1280]{1,0:T(8,128)(2,1)S(1)}, u32[]{:S(2)}, u32[]{:S(2)}) collective-permute-start(bf16[272,1280]{1,0:T(8,128)(2,1)} %get-tuple-element.46), channel_id=1, source_target_pairs={{0,71},{32,120},{8,79},{40,96},{16,87},{48,104},{24,95},{56,112},{... | collective-permute-start | bytes 2088968 | tf_op jit(solution)/shard_map/ppermute | solution.py:424
  98.1 24.4 %collective-permute-start.20 = (bf16[272,1280]{1,0:T(8,128)(2,1)}, bf16[272,1280]{1,0:T(8,128)(2,1)S(1)}, u32[]{:S(2)}, u32[]{:S(2)}) collective-permute-start(bf16[272,1280]{1,0:T(8,128)(2,1)} %get-tuple-element.47), channel_id=1, source_target_pairs={{0,2},{32,48},{8,10},{40,56},{16,18},{48,32},{24,26},{56,40},{1,3}... | collective-permute-start | bytes 2088968 | tf_op jit(solution)/shard_map/ppermute | solution.py:424
  113.5 16.0 %collective-permute-start.21 = (bf16[272,1280]{1,0:T(8,128)(2,1)}, bf16[272,1280]{1,0:T(8,128)(2,1)S(1)}, u32[]{:S(2)}, u32[]{:S(2)}) collective-permute-start(bf16[272,1280]{1,0:T(8,128)(2,1)} %get-tuple-element.48), channel_id=1, source_target_pairs={{0,68},{32,96},{8,76},{40,104},{16,84},{48,112},{24,92},{56,120},{... | collective-permute-start | bytes 2088968 | tf_op jit(solution)/shard_map/ppermute | solution.py:424
  114.8 15.0 %collective-permute-start.22 = (bf16[272,1280]{1,0:T(8,128)(2,1)}, bf16[272,1280]{1,0:T(8,128)(2,1)S(1)}, u32[]{:S(2)}, u32[]{:S(2)}) collective-permute-start(bf16[272,1280]{1,0:T(8,128)(2,1)} %get-tuple-element.49), channel_id=1, source_target_pairs={{0,3},{32,56},{8,11},{40,32},{16,19},{48,40},{24,27},{56,48},{1,0}... | collective-permute-start | bytes 2088968 | tf_op jit(solution)/shard_map/ppermute | solution.py:424
  116.8 13.2 %collective-permute-start.23 = (bf16[272,1280]{1,0:T(8,128)(2,1)}, bf16[272,1280]{1,0:T(8,128)(2,1)S(1)}, u32[]{:S(2)}, u32[]{:S(2)}) collective-permute-start(bf16[272,1280]{1,0:T(8,128)(2,1)} %get-tuple-element.50), channel_id=1, source_target_pairs={{0,1},{32,40},{8,9},{40,48},{16,17},{48,56},{24,25},{56,32},{1,2},... | collective-permute-start | bytes 2088968 | tf_op jit(solution)/shard_map/ppermute | solution.py:424
  132.7 2.2 %collective-permute-start.24 = (f32[136,1280]{1,0:T(8,128)S(1)}, f32[136,1280]{1,0:T(8,128)S(1)}, u32[]{:S(2)}, u32[]{:S(2)}) collective-permute-start(f32[136,1280]{1,0:T(8,128)S(1)} %pad_maximum_fusion), channel_id=1, source_target_pairs={{0,32},{32,0},{8,40},{40,8},{16,48},{48,16},{24,56},{56,24},{1,33}... | collective-permute-start | bytes 2088968 | tf_op jit(solution)/shard_map/ppermute | solution.py:460
  (6 other events, 43.2 us)

commit v5 on v4

--- a/solution.py
+++ b/solution.py
@@ -449,7 +449,7 @@
 
     received = [send(v, *PIECES[q]) for q, v in zip((7, 6, 5, 4), grads("grads_far", (7, 6, 5, 4)))]
     *near_grads, kept = grads("grads_near", (3, 2, 1, 0))
-    received[0], near_grads = lax.optimization_barrier((received[0], near_grads))
+    received[:2], near_grads = lax.optimization_barrier((received[:2], near_grads))
     received += [send(v, *PIECES[q]) for q, v in zip((3, 2, 1), near_grads)]
     received = [v.astype(jnp.float32) for v in received]
     summed = functools.reduce(jnp.add, [v[:ROWS] for v in received]) + kept

time: 139 us -> 139 us (level)
  transfers between devices with their start and end apart: 25 -> 25, of which waited for: 9 -> 10; matrix products, arithmetic and copies ran while one was open for 1% -> 1% of each run, Pallas kernels for 24% -> 24%
where the time goes in v5:
time: 139 us; the launch traced here: 138 us
  Pallas kernels  56.2 us (40%)
  starting transfers between devices  34.6 us (25%)
  waiting for transfers between devices  24.5 us (18%)
  blocking collectives  9.65 us (7%)
  other arithmetic  5.41 us (4%)
  local copies, waits for them, and re-layouts  4.57 us (3%)
  between operations  3.44 us (2%)
    pallas_call x3, Pallas kernels, score_call(): pl.pallas_call(functools.partial(score_kernel, old, new, last), in_specs=...  27.7 us
    pallas_call x2, Pallas kernels, grad_call(): pl.pallas_call(functools.partial(grad_kernel, pairs, pieces), grid=(count...  26.8 us
    ppermute x14, starting transfers between devices, send(): return lax.ppermute(value, AXES, ring_perm(steps, pair))  21.9 us
    ppermute x14, waiting for transfers between devices, send(): return lax.ppermute(value, AXES, ring_perm(steps, pair))  18 us
    all_to_all x1, blocking collectives, on_device(): lax.all_to_all(stats, AXES, 0, 0, axis_index_groups=members, tiled=True)  9.65 us
    ppermute x4, starting transfers between devices, on_device(): other = [swap(v) for v in own]  5.89 us
    ppermute x1, starting transfers between devices, on_device(): other_lse = swap(own_lse)  3.95 us
    unnamed x26, local copies, waits for them, and re-layouts  3.34 us
  transfers between devices with their start and end apart: 25, of which 10 were waited for; matrix products, arithmetic and copies ran while one was open for 1% of the time, Pallas kernels for 24%

profile of v5, /device:TPU:1, one launch (start us, length us, event | category | flops | bytes accessed | tf_op | source)
XLA Modules:
  0.0 138.4 jit_solution(14777601518921542110)
XLA Ops:
  1.7 1.5 %collective-permute-start = (bf16[128,1280]{1,0:T(8,128)(2,1)S(1)}, bf16[128,1280]{1,0:T(8,128)(2,1)S(1)}, u32[]{:S(2)}, u32[]{:S(2)}) collective-permute-start(bf16[128,1280]{1,0:T(8,128)(2,1)S(1)} %broadcast_select_fusion.2), channel_id=1, source_target_pairs={{0,32},{32,0},{8,40},{40,8},{16,48},{48,16},{24,56},{56,24},{1,33}... | collective-permute-start | bytes 983048 | tf_op jit(solution)/shard_map/ppermute | solution.py:426
  3.2 1.3 collective-permute-done
  5.5 1.4 collective-permute-start.3
  6.9 1.6 %collective-permute-start.2 = (bf16[256,1280]{1,0:T(8,128)(2,1)S(1)}, bf16[256,1280]{1,0:T(8,128)(2,1)}, u32[]{:S(2)}, u32[]{:S(2)}) collective-permute-start(bf16[256,1280]{1,0:T(8,128)(2,1)S(1)} %pad_maximum_fusion.1.refs_0_.refs_2_), channel_id=1, source_target_pairs={{0,1},{32,40},{8,9},{40,48},{16,17},{48,56},{24,25},{56,32},{1,2},... | collective-permute-start | bytes 1966088 | tf_op jit(solution)/shard_map/ppermute | solution.py:424
  8.5 2.1 %collective-permute-start.1 = (bf16[256,1280]{1,0:T(8,128)(2,1)S(1)}, bf16[256,1280]{1,0:T(8,128)(2,1)}, u32[]{:S(2)}, u32[]{:S(2)}) collective-permute-start(bf16[256,1280]{1,0:T(8,128)(2,1)S(1)} %pad_maximum_fusion.1.refs_0_.refs_2_), channel_id=1, source_target_pairs={{0,3},{32,56},{8,11},{40,32},{16,19},{48,40},{24,27},{56,48},{1,0}... | collective-permute-start | bytes 1966088 | tf_op jit(solution)/shard_map/ppermute | solution.py:424
  10.7 1.4 %collective-permute-start.4 = (bf16[256,1280]{1,0:T(8,128)(2,1)S(1)}, bf16[256,1280]{1,0:T(8,128)(2,1)S(1)}, u32[]{:S(2)}, u32[]{:S(2)}) collective-permute-start(bf16[256,1280]{1,0:T(8,128)(2,1)S(1)} %pad_maximum_fusion.1.refs_0_.refs_2_), channel_id=1, source_target_pairs={{0,32},{32,0},{8,40},{40,8},{16,48},{48,16},{24,56},{56,24},{1,33}... | collective-permute-start | bytes 1966088 | tf_op jit(solution)/shard_map/ppermute | solution.py:433
  12.1 3.4 %collective-permute-done.3.refs_3_.refs_5_ = bf16[256,1280]{1,0:T(8,128)(2,1)} collective-permute-done((bf16[256,1280]{1,0:T(8,128)(2,1)S(1)}, bf16[256,1280]{1,0:T(8,128)(2,1)}, u32[]{:S(2)}, u32[]{:S(2)}) %collective-permute-start.3) | collective-permute-done | bytes 655392 | tf_op jit(solution)/shard_map/ppermute | solution.py:424
  15.4 2.4 %collective-permute-start.7 = (bf16[256,1280]{1,0:T(8,128)(2,1)}, bf16[256,1280]{1,0:T(8,128)(2,1)S(1)}, u32[]{:S(2)}, u32[]{:S(2)}) collective-permute-start(bf16[256,1280]{1,0:T(8,128)(2,1)} %collective-permute-done.3.refs_3_.refs_5_), channel_id=1, source_target_pairs={{0,32},{32,0},{8,40},{40,8},{16,48},{48,16},{24,56},{56,24},{1,33}... | collective-permute-start | bytes 1966088 | tf_op jit(solution)/shard_map/ppermute | solution.py:433
  17.9 1.1 collective-permute-done.2.refs_2_.refs_4_
  19.0 1.7 %collective-permute-start.6 = (bf16[256,1280]{1,0:T(8,128)(2,1)}, bf16[256,1280]{1,0:T(8,128)(2,1)S(1)}, u32[]{:S(2)}, u32[]{:S(2)}) collective-permute-start(bf16[256,1280]{1,0:T(8,128)(2,1)} %collective-permute-done.2.refs_2_.refs_4_), channel_id=1, source_target_pairs={{0,32},{32,0},{8,40},{40,8},{16,48},{48,16},{24,56},{56,24},{1,33}... | collective-permute-start | bytes 1966088 | tf_op jit(solution)/shard_map/ppermute | solution.py:433
  21.1 1.6 %collective-permute-start.9 = (bf16[256,1280]{1,0:T(8,128)(2,1)}, bf16[256,1280]{1,0:T(8,128)(2,1)}, u32[]{:S(2)}, u32[]{:S(2)}) collective-permute-start(bf16[256,1280]{1,0:T(8,128)(2,1)} %collective-permute-done.3.refs_3_.refs_5_), channel_id=1, source_target_pairs={{0,1},{32,40},{8,9},{40,48},{16,17},{48,56},{24,25},{56,32},{1,2},... | collective-permute-start | bytes 1966088 | tf_op jit(solution)/shard_map/ppermute | solution.py:424
  22.8 2.3 %collective-permute-start.8 = (bf16[256,1280]{1,0:T(8,128)(2,1)}, bf16[256,1280]{1,0:T(8,128)(2,1)}, u32[]{:S(2)}, u32[]{:S(2)}) collective-permute-start(bf16[256,1280]{1,0:T(8,128)(2,1)} %collective-permute-done.1.refs_1_.refs_3_), channel_id=1, source_target_pairs={{0,3},{32,56},{8,11},{40,32},{16,19},{48,40},{24,27},{56,48},{1,0}... | collective-permute-start | bytes 1966088 | tf_op jit(solution)/shard_map/ppermute | solution.py:424
  26.4 7.6 %scores_near.1 = (f32[5376,2048]{1,0:T(8,128)}, f32[4,1024]{1,0:T(4,128)S(1)}) custom-call(s32[32]{0:T(128)S(1)} %dynamic-slice_bitcast_fusion.table_ref, f32[1]{0:T(128)} %bitcast.2.scale_ref, bf16[256,1280]{1,0:T(8,128)(2,1)S(1)} %pad_maximum_fusion.1.refs_0_.refs_2_, bf16[256,1280]{1,0:T(8,128)(2,1)} %collective-permute-done.1.refs_1_.refs_3_, ...), custom_call_target="tpu_custom_call" | custom-call | flops 2684354560 | bytes 4194304 | tf_op jit(solution)/shard_map/scores_near/pallas_call | solution.py:248
  35.3 3.8 %collective-permute-start.14 = (bf16[256,1280]{1,0:T(8,128)(2,1)}, bf16[256,1280]{1,0:T(8,128)(2,1)S(1)}, u32[]{:S(2)}, u32[]{:S(2)}) collective-permute-start(bf16[256,1280]{1,0:T(8,128)(2,1)} %collective-permute-done.10.refs_8_), channel_id=1, source_target_pairs={{0,3},{32,56},{8,11},{40,32},{16,19},{48,40},{24,27},{56,48},{1,0}... | collective-permute-start | bytes 1966088 | tf_op jit(solution)/shard_map/ppermute | solution.py:424
  39.1 1.6 %copy-done.8 = bf16[256,1280]{1,0:T(8,128)(2,1)S(1)} copy-done((bf16[256,1280]{1,0:T(8,128)(2,1)S(1)}, bf16[256,1280]{1,0:T(8,128)(2,1)}, u32[]{:S(2)}) %copy-start.8) | copy-done | bytes 655384
  40.7 11.9 %scores_middle.1 = (f32[5376,2048]{1,0:T(8,128)}, f32[4,1792]{1,0:T(4,128)S(1)}) custom-call(s32[32]{0:T(128)S(1)} %dynamic-slice_bitcast_fusion.table_ref, f32[1]{0:T(128)} %bitcast.2.scale_ref, f32[4,1024]{1,0:T(4,128)S(1)} %get-tuple-element.30.refs_0_, f32[5376,2048]{1,0:T(8,128)} %get-tuple-element.31.refs_1_, ...), custom_call_target="tpu_custom_call", output_to_operand_aliasing={{0}: (3, {})} | custom-call | flops 5536481280 | bytes 8650752 | tf_op jit(solution)/shard_map/scores_middle/pallas_call | solution.py:248
  52.6 2.1 %collective-permute-done.15.refs_17_.refs_7_ = bf16[256,1280]{1,0:T(8,128)(2,1)S(1)} collective-permute-done((bf16[256,1280]{1,0:T(8,128)(2,1)S(1)}, bf16[256,1280]{1,0:T(8,128)(2,1)S(1)}, u32[]{:S(2)}, u32[]{:S(2)}) %collective-permute-start.15) | collective-permute-done | bytes 655392 | tf_op jit(solution)/shard_map/ppermute | solution.py:440
  54.8 8.3 %scores_far.1 = (f32[5376,2048]{1,0:T(8,128)}, f32[8,2,2176]{2,1,0:T(2,128)S(1)}) custom-call(s32[32]{0:T(128)S(1)} %dynamic-slice_bitcast_fusion.table_ref, f32[1]{0:T(128)} %bitcast.2.scale_ref, f32[4,1792]{1,0:T(4,128)S(1)} %get-tuple-element.36.refs_0_, f32[5376,2048]{1,0:T(8,128)} %get-tuple-element.37.refs_1_, ...), custom_call_target="tpu_custom_call", output_to_operand_aliasing={{0}: (3, {})} | custom-call | flops 2516582400 | bytes 3932160 | tf_op jit(solution)/shard_map/scores_far/pallas_call | solution.py:248
  63.1 9.7 %all_to_all.5.stats_ref = f32[8,2,2176]{2,1,0:T(2,128)} all-to-all(f32[8,2,2176]{2,1,0:T(2,128)S(1)} %get-tuple-element.39), channel_id=1, replica_groups={{0,1,2,3,68,69,70,71},{4,5,6,7,64,65,66,67},{8,9,10,11,76,77,78,79},{12..., dimensions={0} | all-to-all | bytes 278528 | tf_op jit(solution)/shard_map/all_to_all | solution.py:443
  72.7 1.6 %join.1.own_lse_ref = f32[1,2304]{1,0:T(1,128)} custom-call(f32[8,2,2176]{2,1,0:T(2,128)} %all_to_all.5.stats_ref), custom_call_target="tpu_custom_call" | custom-call | tf_op jit(solution)/shard_map/join/pallas_call | solution.py:294
  74.3 3.9 %collective-permute-start.16 = (f32[1,2304]{1,0:T(1,128)}, f32[1,2304]{1,0:T(1,128)S(1)}, u32[]{:S(2)}, u32[]{:S(2)}) collective-permute-start(f32[1,2304]{1,0:T(1,128)} %join.1.own_lse_ref), channel_id=1, source_target_pairs={{0,32},{32,0},{8,40},{40,8},{16,48},{48,16},{24,56},{56,24},{1,33}... | collective-permute-start | bytes 27656 | tf_op jit(solution)/shard_map/ppermute | solution.py:445
  78.3 1.0 collective-permute-done.16.other_lse_ref
  79.9 13.3 %grads_far.1 = (bf16[272,1280]{1,0:T(8,128)(2,1)}, bf16[272,1280]{1,0:T(8,128)(2,1)}, bf16[272,1280]{1,0:T(8,128)(2,1)}, bf16[272,1280]{1,0:T(8,128)(2,1)}) custom-call(s32[32]{0:T(128)} %copy-done.10, f32[1]{0:T(128)} %bitcast.7.scale_ref, f32[1,2304]{1,0:T(1,128)} %join.1.own_lse_ref, f32[1,2304]{1,0:T(1,128)} %copy-done.12, ...), custom_call_target="tpu_custom_call" | custom-call | flops 5368709120 | bytes 8388608 | tf_op jit(solution)/shard_map/grads_far/pallas_call | solution.py:382
  93.4 4.8 %collective-permute-start.18 = (bf16[272,1280]{1,0:T(8,128)(2,1)}, bf16[272,1280]{1,0:T(8,128)(2,1)S(1)}, u32[]{:S(2)}, u32[]{:S(2)}) collective-permute-start(bf16[272,1280]{1,0:T(8,128)(2,1)} %get-tuple-element.42), channel_id=1, source_target_pairs={{0,69},{32,104},{8,77},{40,112},{16,85},{48,120},{24,93},{56,96},{... | collective-permute-start | bytes 2088968 | tf_op jit(solution)/shard_map/ppermute | solution.py:424
  98.2 1.8 %collective-permute-start.20 = (bf16[272,1280]{1,0:T(8,128)(2,1)}, bf16[272,1280]{1,0:T(8,128)(2,1)S(1)}, u32[]{:S(2)}, u32[]{:S(2)}) collective-permute-start(bf16[272,1280]{1,0:T(8,128)(2,1)} %get-tuple-element.49), channel_id=1, source_target_pairs={{0,2},{32,48},{8,10},{40,56},{16,18},{48,32},{24,26},{56,40},{1,3}... | collective-permute-start | bytes 2088968 | tf_op jit(solution)/shard_map/ppermute | solution.py:424
  99.9 13.5 %grads_near.1 = (bf16[272,1280]{1,0:T(8,128)(2,1)}, bf16[272,1280]{1,0:T(8,128)(2,1)}, bf16[272,1280]{1,0:T(8,128)(2,1)}, f32[256,1280]{1,0:T(8,128)}) custom-call(s32[32]{0:T(128)} %copy-done.10, f32[1]{0:T(128)} %bitcast.8.scale_ref, f32[1,2304]{1,0:T(1,128)} %join.1.own_lse_ref, f32[1,2304]{1,0:T(1,128)} %copy-done.12, ...), custom_call_target="tpu_custom_call" | custom-call | flops 5368709120 | bytes 8388608 | tf_op jit(solution)/shard_map/grads_near/pallas_call | solution.py:382
  114.8 2.0 %collective-permute-start.22 = (bf16[272,1280]{1,0:T(8,128)(2,1)}, bf16[272,1280]{1,0:T(8,128)(2,1)S(1)}, u32[]{:S(2)}, u32[]{:S(2)}) collective-permute-start(bf16[272,1280]{1,0:T(8,128)(2,1)} %get-tuple-element.51), channel_id=1, source_target_pairs={{0,3},{32,56},{8,11},{40,32},{16,19},{48,40},{24,27},{56,48},{1,0}... | collective-permute-start | bytes 2088968 | tf_op jit(solution)/shard_map/ppermute | solution.py:424
  117.0 5.4 %collective-permute-done.19 = bf16[272,1280]{1,0:T(8,128)(2,1)S(1)} collective-permute-done((bf16[272,1280]{1,0:T(8,128)(2,1)}, bf16[272,1280]{1,0:T(8,128)(2,1)S(1)}, u32[]{:S(2)}, u32[]{:S(2)}) %collective-permute-start.19) | collective-permute-done | bytes 696352 | tf_op jit(solution)/shard_map/ppermute | solution.py:424
  122.7 6.8 %collective-permute-done.21 = bf16[272,1280]{1,0:T(8,128)(2,1)S(1)} collective-permute-done((bf16[272,1280]{1,0:T(8,128)(2,1)}, bf16[272,1280]{1,0:T(8,128)(2,1)S(1)}, u32[]{:S(2)}, u32[]{:S(2)}) %collective-permute-start.21) | collective-permute-done | bytes 696352 | tf_op jit(solution)/shard_map/ppermute | solution.py:424
  130.1 1.1 copy-done.11
  132.8 2.1 %collective-permute-done.24 = f32[136,1280]{1,0:T(8,128)S(1)} collective-permute-done((f32[136,1280]{1,0:T(8,128)S(1)}, f32[136,1280]{1,0:T(8,128)S(1)}, u32[]{:S(2)}, u32[]{:S(2)}) %collective-permute-start.24) | collective-permute-done | bytes 696352 | tf_op jit(solution)/shard_map/ppermute | solution.py:460
  136.1 1.2 slice_select_fusion
  (77 shorter events, 9.6 us)
Async XLA Ops:
  1.7 2.8 %collective-permute-start = (bf16[128,1280]{1,0:T(8,128)(2,1)S(1)}, bf16[128,1280]{1,0:T(8,128)(2,1)S(1)}, u32[]{:S(2)}, u32[]{:S(2)}) collective-permute-start(bf16[128,1280]{1,0:T(8,128)(2,1)S(1)} %broadcast_select_fusion.2), channel_id=1, source_target_pairs={{0,32},{32,0},{8,40},{40,8},{16,48},{48,16},{24,56},{56,24},{1,33}... | collective-permute-start | bytes 983048 | tf_op jit(solution)/shard_map/ppermute | solution.py:426
  5.5 28.5 %copy-start.7 = (bf16[256,1280]{1,0:T(8,128)(2,1)}, bf16[256,1280]{1,0:T(8,128)(2,1)S(1)}, u32[]{:S(2)}) copy-start(bf16[256,1280]{1,0:T(8,128)(2,1)S(1)} %pad_maximum_fusion.1.refs_0_.refs_2_) | copy-start | bytes 1966084
  5.5 9.9 %collective-permute-start.3 = (bf16[256,1280]{1,0:T(8,128)(2,1)S(1)}, bf16[256,1280]{1,0:T(8,128)(2,1)}, u32[]{:S(2)}, u32[]{:S(2)}) collective-permute-start(bf16[256,1280]{1,0:T(8,128)(2,1)S(1)} %pad_maximum_fusion.1.refs_0_.refs_2_), channel_id=1, source_target_pairs={{0,68},{32,96},{8,76},{40,104},{16,84},{48,112},{24,92},{56,120},{... | collective-permute-start | bytes 1966088 | tf_op jit(solution)/shard_map/ppermute | solution.py:424
  6.9 12.1 %collective-permute-start.2 = (bf16[256,1280]{1,0:T(8,128)(2,1)S(1)}, bf16[256,1280]{1,0:T(8,128)(2,1)}, u32[]{:S(2)}, u32[]{:S(2)}) collective-permute-start(bf16[256,1280]{1,0:T(8,128)(2,1)S(1)} %pad_maximum_fusion.1.refs_0_.refs_2_), channel_id=1, source_target_pairs={{0,1},{32,40},{8,9},{40,48},{16,17},{48,56},{24,25},{56,32},{1,2},... | collective-permute-start | bytes 1966088 | tf_op jit(solution)/shard_map/ppermute | solution.py:424
  8.5 12.2 %collective-permute-start.1 = (bf16[256,1280]{1,0:T(8,128)(2,1)S(1)}, bf16[256,1280]{1,0:T(8,128)(2,1)}, u32[]{:S(2)}, u32[]{:S(2)}) collective-permute-start(bf16[256,1280]{1,0:T(8,128)(2,1)S(1)} %pad_maximum_fusion.1.refs_0_.refs_2_), channel_id=1, source_target_pairs={{0,3},{32,56},{8,11},{40,32},{16,19},{48,40},{24,27},{56,48},{1,0}... | collective-permute-start | bytes 1966088 | tf_op jit(solution)/shard_map/ppermute | solution.py:424
  10.7 12.1 %collective-permute-start.4 = (bf16[256,1280]{1,0:T(8,128)(2,1)S(1)}, bf16[256,1280]{1,0:T(8,128)(2,1)S(1)}, u32[]{:S(2)}, u32[]{:S(2)}) collective-permute-start(bf16[256,1280]{1,0:T(8,128)(2,1)S(1)} %pad_maximum_fusion.1.refs_0_.refs_2_), channel_id=1, source_target_pairs={{0,32},{32,0},{8,40},{40,8},{16,48},{48,16},{24,56},{56,24},{1,33}... | collective-permute-start | bytes 1966088 | tf_op jit(solution)/shard_map/ppermute | solution.py:433
  15.4 7.3 %collective-permute-start.7 = (bf16[256,1280]{1,0:T(8,128)(2,1)}, bf16[256,1280]{1,0:T(8,128)(2,1)S(1)}, u32[]{:S(2)}, u32[]{:S(2)}) collective-permute-start(bf16[256,1280]{1,0:T(8,128)(2,1)} %collective-permute-done.3.refs_3_.refs_5_), channel_id=1, source_target_pairs={{0,32},{32,0},{8,40},{40,8},{16,48},{48,16},{24,56},{56,24},{1,33}... | collective-permute-start | bytes 1966088 | tf_op jit(solution)/shard_map/ppermute | solution.py:433
  19.0 7.4 %collective-permute-start.6 = (bf16[256,1280]{1,0:T(8,128)(2,1)}, bf16[256,1280]{1,0:T(8,128)(2,1)S(1)}, u32[]{:S(2)}, u32[]{:S(2)}) collective-permute-start(bf16[256,1280]{1,0:T(8,128)(2,1)} %collective-permute-done.2.refs_2_.refs_4_), channel_id=1, source_target_pairs={{0,32},{32,0},{8,40},{40,8},{16,48},{48,16},{24,56},{56,24},{1,33}... | collective-permute-start | bytes 1966088 | tf_op jit(solution)/shard_map/ppermute | solution.py:433
  20.7 5.7 %collective-permute-start.5 = (bf16[256,1280]{1,0:T(8,128)(2,1)}, bf16[256,1280]{1,0:T(8,128)(2,1)S(1)}, u32[]{:S(2)}, u32[]{:S(2)}) collective-permute-start(bf16[256,1280]{1,0:T(8,128)(2,1)} %collective-permute-done.1.refs_1_.refs_3_), channel_id=1, source_target_pairs={{0,32},{32,0},{8,40},{40,8},{16,48},{48,16},{24,56},{56,24},{1,33}... | collective-permute-start | bytes 1966088 | tf_op jit(solution)/shard_map/ppermute | solution.py:433
  21.1 13.0 %collective-permute-start.9 = (bf16[256,1280]{1,0:T(8,128)(2,1)}, bf16[256,1280]{1,0:T(8,128)(2,1)}, u32[]{:S(2)}, u32[]{:S(2)}) collective-permute-start(bf16[256,1280]{1,0:T(8,128)(2,1)} %collective-permute-done.3.refs_3_.refs_5_), channel_id=1, source_target_pairs={{0,1},{32,40},{8,9},{40,48},{16,17},{48,56},{24,25},{56,32},{1,2},... | collective-permute-start | bytes 1966088 | tf_op jit(solution)/shard_map/ppermute | solution.py:424
  22.7 32.0 %copy-start = (bf16[256,1280]{1,0:T(8,128)(2,1)}, bf16[256,1280]{1,0:T(8,128)(2,1)S(1)}, u32[]{:S(2)}) copy-start(bf16[256,1280]{1,0:T(8,128)(2,1)S(1)} %collective-permute-done.4.refs_4_.refs_9_.refs_10_.refs_0_) | copy-start | bytes 1966084
  22.7 11.3 %collective-permute-start.10 = (bf16[256,1280]{1,0:T(8,128)(2,1)}, bf16[256,1280]{1,0:T(8,128)(2,1)}, u32[]{:S(2)}, u32[]{:S(2)}) collective-permute-start(bf16[256,1280]{1,0:T(8,128)(2,1)} %collective-permute-done.1.refs_1_.refs_3_), channel_id=1, source_target_pairs={{0,68},{32,96},{8,76},{40,104},{16,84},{48,112},{24,92},{56,120},{... | collective-permute-start | bytes 1966088 | tf_op jit(solution)/shard_map/ppermute | solution.py:424
  22.7 32.0 %copy-start.1 = (bf16[256,1280]{1,0:T(8,128)(2,1)}, bf16[256,1280]{1,0:T(8,128)(2,1)S(1)}, u32[]{:S(2)}) copy-start(bf16[256,1280]{1,0:T(8,128)(2,1)S(1)} %collective-permute-done.7.refs_7_.refs_12_.refs_13_.refs_3_) | copy-start | bytes 1966084
  22.8 11.3 %collective-permute-start.8 = (bf16[256,1280]{1,0:T(8,128)(2,1)}, bf16[256,1280]{1,0:T(8,128)(2,1)}, u32[]{:S(2)}, u32[]{:S(2)}) collective-permute-start(bf16[256,1280]{1,0:T(8,128)(2,1)} %collective-permute-done.1.refs_1_.refs_3_), channel_id=1, source_target_pairs={{0,3},{32,56},{8,11},{40,32},{16,19},{48,40},{24,27},{56,48},{1,0}... | collective-permute-start | bytes 1966088 | tf_op jit(solution)/shard_map/ppermute | solution.py:424
  26.4 28.3 %copy-start.10 = (s32[32]{0:T(128)}, s32[32]{0:T(128)S(1)}, u32[]{:S(2)}) copy-start(s32[32]{0:T(128)S(1)} %dynamic-slice_bitcast_fusion.table_ref) | copy-start | bytes 388
  26.4 28.3 %copy-start.2 = (bf16[256,1280]{1,0:T(8,128)(2,1)}, bf16[256,1280]{1,0:T(8,128)(2,1)S(1)}, u32[]{:S(2)}) copy-start(bf16[256,1280]{1,0:T(8,128)(2,1)S(1)} %collective-permute-done.6.refs_6_.refs_11_.refs_12_.refs_2_) | copy-start | bytes 1966084
  26.4 28.3 %copy-start.3 = (bf16[256,1280]{1,0:T(8,128)(2,1)}, bf16[256,1280]{1,0:T(8,128)(2,1)S(1)}, u32[]{:S(2)}) copy-start(bf16[256,1280]{1,0:T(8,128)(2,1)S(1)} %collective-permute-done.5.refs_5_.refs_10_.refs_11_.refs_1_) | copy-start | bytes 1966084
  34.1 5.0 %collective-permute-start.11 = (bf16[256,1280]{1,0:T(8,128)(2,1)}, bf16[256,1280]{1,0:T(8,128)(2,1)S(1)}, u32[]{:S(2)}, u32[]{:S(2)}) collective-permute-start(bf16[256,1280]{1,0:T(8,128)(2,1)} %collective-permute-done.8.refs_6_), channel_id=1, source_target_pairs={{0,32},{32,0},{8,40},{40,8},{16,48},{48,16},{24,56},{56,24},{1,33}... | collective-permute-start | bytes 1966088 | tf_op jit(solution)/shard_map/ppermute | solution.py:437
  34.8 4.3 %collective-permute-start.12 = (bf16[256,1280]{1,0:T(8,128)(2,1)}, bf16[256,1280]{1,0:T(8,128)(2,1)S(1)}, u32[]{:S(2)}, u32[]{:S(2)}) collective-permute-start(bf16[256,1280]{1,0:T(8,128)(2,1)} %collective-permute-done.9.refs_7_), channel_id=1, source_target_pairs={{0,32},{32,0},{8,40},{40,8},{16,48},{48,16},{24,56},{56,24},{1,33}... | collective-permute-start | bytes 1966088 | tf_op jit(solution)/shard_map/ppermute | solution.py:437
  34.8 4.3 %collective-permute-start.13 = (bf16[256,1280]{1,0:T(8,128)(2,1)}, bf16[256,1280]{1,0:T(8,128)(2,1)S(1)}, u32[]{:S(2)}, u32[]{:S(2)}) collective-permute-start(bf16[256,1280]{1,0:T(8,128)(2,1)} %collective-permute-done.10.refs_8_), channel_id=1, source_target_pairs={{0,32},{32,0},{8,40},{40,8},{16,48},{48,16},{24,56},{56,24},{1,33}... | collective-permute-start | bytes 1966088 | tf_op jit(solution)/shard_map/ppermute | solution.py:437
  35.3 17.2 %collective-permute-start.14 = (bf16[256,1280]{1,0:T(8,128)(2,1)}, bf16[256,1280]{1,0:T(8,128)(2,1)S(1)}, u32[]{:S(2)}, u32[]{:S(2)}) collective-permute-start(bf16[256,1280]{1,0:T(8,128)(2,1)} %collective-permute-done.10.refs_8_), channel_id=1, source_target_pairs={{0,3},{32,56},{8,11},{40,32},{16,19},{48,40},{24,27},{56,48},{1,0}... | collective-permute-start | bytes 1966088 | tf_op jit(solution)/shard_map/ppermute | solution.py:424
  39.1 15.7 %copy-start.5 = (bf16[256,1280]{1,0:T(8,128)(2,1)}, bf16[256,1280]{1,0:T(8,128)(2,1)S(1)}, u32[]{:S(2)}) copy-start(bf16[256,1280]{1,0:T(8,128)(2,1)S(1)} %collective-permute-done.12.refs_14_.refs_15_.refs_5_) | copy-start | bytes 1966084
  52.6 2.2 %collective-permute-start.15 = (bf16[256,1280]{1,0:T(8,128)(2,1)S(1)}, bf16[256,1280]{1,0:T(8,128)(2,1)S(1)}, u32[]{:S(2)}, u32[]{:S(2)}) collective-permute-start(bf16[256,1280]{1,0:T(8,128)(2,1)S(1)} %collective-permute-done.14.refs_9_), channel_id=1, source_target_pairs={{0,32},{32,0},{8,40},{40,8},{16,48},{48,16},{24,56},{56,24},{1,33}... | collective-permute-start | bytes 1966088 | tf_op jit(solution)/shard_map/ppermute | solution.py:440
  74.3 5.0 %collective-permute-start.16 = (f32[1,2304]{1,0:T(1,128)}, f32[1,2304]{1,0:T(1,128)S(1)}, u32[]{:S(2)}, u32[]{:S(2)}) collective-permute-start(f32[1,2304]{1,0:T(1,128)} %join.1.own_lse_ref), channel_id=1, source_target_pairs={{0,32},{32,0},{8,40},{40,8},{16,48},{48,16},{24,56},{56,24},{1,33}... | collective-permute-start | bytes 27656 | tf_op jit(solution)/shard_map/ppermute | solution.py:445
  93.3 20.2 %collective-permute-start.17 = (bf16[272,1280]{1,0:T(8,128)(2,1)}, bf16[272,1280]{1,0:T(8,128)(2,1)S(1)}, u32[]{:S(2)}, u32[]{:S(2)}) collective-permute-start(bf16[272,1280]{1,0:T(8,128)(2,1)} %get-tuple-element.41), channel_id=1, source_target_pairs={{0,70},{32,112},{8,78},{40,120},{16,86},{48,96},{24,94},{56,104},{... | collective-permute-start | bytes 2088968 | tf_op jit(solution)/shard_map/ppermute | solution.py:424
  93.4 21.1 %collective-permute-start.18 = (bf16[272,1280]{1,0:T(8,128)(2,1)}, bf16[272,1280]{1,0:T(8,128)(2,1)S(1)}, u32[]{:S(2)}, u32[]{:S(2)}) collective-permute-start(bf16[272,1280]{1,0:T(8,128)(2,1)} %get-tuple-element.42), channel_id=1, source_target_pairs={{0,69},{32,104},{8,77},{40,112},{16,85},{48,120},{24,93},{56,96},{... | collective-permute-start | bytes 2088968 | tf_op jit(solution)/shard_map/ppermute | solution.py:424
  98.1 24.3 %collective-permute-start.19 = (bf16[272,1280]{1,0:T(8,128)(2,1)}, bf16[272,1280]{1,0:T(8,128)(2,1)S(1)}, u32[]{:S(2)}, u32[]{:S(2)}) collective-permute-start(bf16[272,1280]{1,0:T(8,128)(2,1)} %get-tuple-element.48), channel_id=1, source_target_pairs={{0,71},{32,120},{8,79},{40,96},{16,87},{48,104},{24,95},{56,112},{... | collective-permute-start | bytes 2088968 | tf_op jit(solution)/shard_map/ppermute | solution.py:424
  98.2 24.4 %collective-permute-start.20 = (bf16[272,1280]{1,0:T(8,128)(2,1)}, bf16[272,1280]{1,0:T(8,128)(2,1)S(1)}, u32[]{:S(2)}, u32[]{:S(2)}) collective-permute-start(bf16[272,1280]{1,0:T(8,128)(2,1)} %get-tuple-element.49), channel_id=1, source_target_pairs={{0,2},{32,48},{8,10},{40,56},{16,18},{48,32},{24,26},{56,40},{1,3}... | collective-permute-start | bytes 2088968 | tf_op jit(solution)/shard_map/ppermute | solution.py:424
  114.4 15.1 %collective-permute-start.21 = (bf16[272,1280]{1,0:T(8,128)(2,1)}, bf16[272,1280]{1,0:T(8,128)(2,1)S(1)}, u32[]{:S(2)}, u32[]{:S(2)}) collective-permute-start(bf16[272,1280]{1,0:T(8,128)(2,1)} %get-tuple-element.50), channel_id=1, source_target_pairs={{0,68},{32,96},{8,76},{40,104},{16,84},{48,112},{24,92},{56,120},{... | collective-permute-start | bytes 2088968 | tf_op jit(solution)/shard_map/ppermute | solution.py:424
  114.8 15.0 %collective-permute-start.22 = (bf16[272,1280]{1,0:T(8,128)(2,1)}, bf16[272,1280]{1,0:T(8,128)(2,1)S(1)}, u32[]{:S(2)}, u32[]{:S(2)}) collective-permute-start(bf16[272,1280]{1,0:T(8,128)(2,1)} %get-tuple-element.51), channel_id=1, source_target_pairs={{0,3},{32,56},{8,11},{40,32},{16,19},{48,40},{24,27},{56,48},{1,0}... | collective-permute-start | bytes 2088968 | tf_op jit(solution)/shard_map/ppermute | solution.py:424
  116.8 13.2 %collective-permute-start.23 = (bf16[272,1280]{1,0:T(8,128)(2,1)}, bf16[272,1280]{1,0:T(8,128)(2,1)S(1)}, u32[]{:S(2)}, u32[]{:S(2)}) collective-permute-start(bf16[272,1280]{1,0:T(8,128)(2,1)} %get-tuple-element.52), channel_id=1, source_target_pairs={{0,1},{32,40},{8,9},{40,48},{16,17},{48,56},{24,25},{56,32},{1,2},... | collective-permute-start | bytes 2088968 | tf_op jit(solution)/shard_map/ppermute | solution.py:424
  132.7 2.2 %collective-permute-start.24 = (f32[136,1280]{1,0:T(8,128)S(1)}, f32[136,1280]{1,0:T(8,128)S(1)}, u32[]{:S(2)}, u32[]{:S(2)}) collective-permute-start(f32[136,1280]{1,0:T(8,128)S(1)} %pad_maximum_fusion), channel_id=1, source_target_pairs={{0,32},{32,0},{8,40},{40,8},{16,48},{48,16},{24,56},{56,24},{1,33}... | collective-permute-start | bytes 2088968 | tf_op jit(solution)/shard_map/ppermute | solution.py:460
  (6 other events, 43.2 us)
